TPU v7x, 32 devices: a whole 2x2x4 slice. The times are simulated.
32 devices in a mesh: rowa: 4 (over y, x), rowb: 8 (over z, core).
Axes of the slice: x: 2, y: 2, z: 4, core: 2. Of those that a mesh axis runs over, the one named last changes fastest.
Arguments:
- right_side: float32 [12288, 8], P(('rowa', 'rowb')), may hold values from -6 to 6
- leaves: float32 [12288, 384], P(('rowa', 'rowb')), as said below
- bases: float32 [5, 12288, 128], P(None, ('rowa', 'rowb')), may hold values from -0.3125 to 0.3125
- ranks: int32 [31], replicated, may hold values from 64 to 128
Outputs:
- solution: float32 [12288, 8], P(('rowa', 'rowb'))
Inputs may be any that keep to these rules, and one draw needn't show every extreme that they name: `ranks`: entry 2^(5 - m) + k - 1 is the rank of node k of level m (levels counted from the leaves, the root at level 5). `leaves`: each leaf block is symmetric positive definite.
All inputs are finite; a program needn't handle non-finite values.
Results may differ from a plain program's by a relative error of at most 0.0001.
Values sent between devices are 32-bit elements; how exact they have to be, the bound alone decides.
No kernel may reach another device: no remote copies, remote signals or barrier semaphores. Data moves between devices by JAX's collectives and lax.ppermute only.
A program may use at most 64 MiB of HBM per device.

v0:
```python
import functools

import jax
import jax.numpy as jnp
from jax import lax
from jax.experimental import pallas as pl
from jax.experimental.pallas import tpu as pltpu
from jax.sharding import PartitionSpec as P

HIGHEST = lax.Precision.HIGHEST
F32 = jnp.float32
BF16 = jnp.bfloat16
STEP = 16
VMEM_LIMIT = 48 * 1024 * 1024


def dot(left, right):
    return jnp.dot(left, right, precision=HIGHEST, preferred_element_type=F32)


def dot_nt(left, right):
    return lax.dot_general(
        left, right, (((1,), (1,)), ((), ())), precision=HIGHEST, preferred_element_type=F32
    )


def split3(value):
    high = value.astype(BF16).astype(F32)
    rest = value - high
    middle = rest.astype(BF16).astype(F32)
    return high, middle, rest - middle


def reciprocal(value):
    guess = pltpu.reciprocal(value, approx=True)
    return guess * (2.0 - value * guess)


def inverse(matrix):
    size = matrix.shape[0]
    lane = lax.broadcasted_iota(jnp.int32, (STEP, size), 1)
    sub = lax.broadcasted_iota(jnp.int32, (STEP, size), 0)
    lane_all = lax.broadcasted_iota(jnp.int32, (size, size), 1)
    sub_all = lax.broadcasted_iota(jnp.int32, (size, size), 0)
    for start in range(0, size, STEP):
        stop = start + STEP
        rows = matrix[start:stop, :]
        pivots = [
            jnp.broadcast_to(rows[:, start + index : start + index + 1], (STEP, size))
            for index in range(STEP)
        ]
        inside = (lane >= start) & (lane < stop)
        panel = jnp.where(inside, jnp.where(lane - start == sub, 1.0, 0.0), rows)
        for index in range(STEP):
            scale = reciprocal(pivots[index][index : index + 1, :])
            factor = jnp.where(sub == index, -1.0, pivots[index])
            panel = jnp.where(sub == index, 0.0, panel) - factor * (panel[index : index + 1] * scale)
            for later in range(index + 1, STEP):
                row = pivots[later][index : index + 1] * scale
                pivots[later] = jnp.where(sub == index, 0.0, pivots[later]) - factor * row
        row_inside = (sub_all >= start) & (sub_all < stop)
        lane_inside = (lane_all >= start) & (lane_all < stop)
        column = jnp.where(row_inside, 0.0, matrix)[:, start:stop]
        base = jnp.where(row_inside | lane_inside, 0.0, matrix)
        c_high, c_mid, c_low = split3(column)
        p_high, p_mid, p_low = split3(panel)
        left = jnp.concatenate([c_high, c_high, c_mid, c_high, c_mid, c_low], axis=1).astype(BF16)
        right = jnp.concatenate([p_high, p_mid, p_high, p_low, p_mid, p_high], axis=0).astype(BF16)
        matrix = base - jnp.dot(left, right, preferred_element_type=F32)
        pieces = [matrix[:start]] if start else []
        pieces.append(panel)
        if stop < size:
            pieces.append(matrix[stop:])
        matrix = jnp.concatenate(pieces, axis=0)
    return matrix


def leaf_kernel(levels, width, blocks, ranks_ref, place_ref, rhs_ref, leaf_ref, bases_ref, *refs):
    head_ref, tail_ref, scaled_ref, lower_ref, v_ref = refs
    nrhs = rhs_ref.shape[1]
    place = place_ref[0]
    sub = lax.broadcasted_iota(jnp.int32, (width, width), 0)
    rows = levels * width
    for block in range(blocks):
        span = slice(block * width, (block + 1) * width)
        for level in range(1, levels + 1):
            rank = ranks_ref[2 ** (levels - level) + lax.shift_right_logical(place, level) - 1]
            piece = bases_ref[level - 1, span, :].T
            v_ref[block, (level - 1) * width : level * width, :] = jnp.where(sub < rank, piece, 0.0)
        v_ref[block, rows : rows + nrhs, :] = rhs_ref[span, :].T
    schur = {}
    for first in range(blocks):
        for second in range(first, blocks):
            schur[first, second] = leaf_ref[
                first * width : (first + 1) * width, second * width : (second + 1) * width
            ]
    for block in range(blocks):
        inv = inverse(schur[block, block])
        values = v_ref[block]
        scaled = dot(values, inv)
        scaled_ref[block] = scaled
        upper = {}
        for later in range(block + 1, blocks):
            upper[later] = dot(inv, schur[block, later])
            lower_ref[block, later - 1] = upper[later]
            v_ref[later] = v_ref[later] - dot(scaled, schur[block, later])
        for first in range(block + 1, blocks):
            for second in range(first, blocks):
                product = lax.dot_general(
                    schur[block, first],
                    upper[second],
                    (((0,), (0,)), ((), ())),
                    precision=HIGHEST,
                    preferred_element_type=F32,
                )
                schur[first, second] = schur[first, second] - product
        offset = 0
        for level in range(1, levels + 1):
            low = (level - 1) * width
            product = dot_nt(values[low:], scaled[low : low + width])
            if level == 1:
                target, span = head_ref, slice(0, product.shape[0])
            else:
                target, span = tail_ref, slice(offset, offset + product.shape[0])
                offset += product.shape[0]
            if block == 0:
                target[span, :] = product
            else:
                target[span, :] = target[span, :] + product


def pivot_kernel(width, own_ref, other_ref, rest_ref, coef_ref):
    total = own_ref[...] + other_ref[...]
    row = lax.broadcasted_iota(jnp.int32, (width, width), 0)
    column = lax.broadcasted_iota(jnp.int32, (width, width), 1)
    inv = inverse(total[:width] + jnp.where(row == column, 1.0, 0.0))
    rest = total[width:]
    rest_ref[...] = rest
    coef_ref[...] = dot(rest, inv)


def update_kernel(width, left, own_ref, other_ref, rest_ref, coef_ref, head_ref, *refs):
    offset = 0
    for level in range(left):
        low = level * width
        count = coef_ref.shape[0] - low
        span = slice(offset, offset + count)
        product = dot_nt(coef_ref[low:, :], rest_ref[low : low + width, :])
        value = own_ref[span, :] + other_ref[span, :] - product
        if level == 0:
            head_ref[...] = value
        else:
            refs[0][offset - head_ref.shape[0] : offset - head_ref.shape[0] + count, :] = value
        offset += count


def back_kernel(levels, width, blocks, scaled_ref, lower_ref, out_ref):
    values = [None] * blocks
    for block in reversed(range(blocks)):
        value = scaled_ref[block]
        for later in range(block + 1, blocks):
            value = value - dot_nt(values[later], lower_ref[block, later - 1])
        values[block] = value
        out_ref[:, block * width : (block + 1) * width] = value


def final_kernel(levels, width, weights_ref, *refs):
    coef_refs, out_ref = refs[:-1], refs[-1]
    known = []
    for level in reversed(range(levels)):
        coef = coef_refs[level]
        count = (levels - 1 - level) * width
        value = coef[count:, :]
        for index, later in enumerate(known):
            low = (len(known) - 1 - index) * width
            value = value - dot(later, coef[low : low + width, :])
        known.append(value)
    rows = levels * width
    result = weights_ref[rows:, :]
    for level in range(levels):
        result = result - dot(
            known[levels - 1 - level], weights_ref[level * width : (level + 1) * width, :]
        )
    out_ref[...] = result.T


def call(kernel, shapes, *operands, flops=0, smem=0, scratch=()):
    space = [pl.BlockSpec(memory_space=pltpu.SMEM)] * smem
    space += [pl.BlockSpec(memory_space=pltpu.VMEM)] * (len(operands) - smem)
    outs = [jax.ShapeDtypeStruct(shape, F32) for shape in shapes]
    return pl.pallas_call(
        kernel,
        out_shape=outs,
        in_specs=space,
        out_specs=[pl.BlockSpec(memory_space=pltpu.VMEM)] * len(outs),
        scratch_shapes=list(scratch),
        compiler_params=pltpu.CompilerParams(vmem_limit_bytes=VMEM_LIMIT),
        cost_estimate=pl.CostEstimate(flops=flops, bytes_accessed=0, transcendentals=0),
    )(*operands)


def partner(value, tree_level, inner_bits):
    bit = tree_level - 1
    axis, stride = ("rowb", bit) if bit < inner_bits else ("rowa", bit - inner_bits)
    mask = 2**stride
    pairs = [(source, source ^ mask) for source in range(lax.axis_size(axis))]
    return lax.ppermute(value, axis, pairs)


def body(right_side, leaves, bases, ranks):
    levels = bases.shape[0]
    leaf_rows = leaves.shape[0]
    width = bases.shape[2]
    nrhs = right_side.shape[1]
    blocks = leaf_rows // width
    inner_bits = lax.axis_size("rowb").bit_length() - 1
    place = lax.axis_index("rowa") * lax.axis_size("rowb") + lax.axis_index("rowb")
    place = place.astype(jnp.int32).reshape(1)
    rows = levels * width + nrhs
    counts = [rows - level * width for level in range(levels)]
    head, tail, scaled, lower = call(
        functools.partial(leaf_kernel, levels, width, blocks),
        [
            (counts[0], width),
            (sum(counts[1:]), width),
            (blocks, rows, width),
            (blocks, max(blocks - 1, 1), width, width),
        ],
        ranks,
        place,
        right_side,
        leaves,
        bases,
        smem=2,
        scratch=[pltpu.VMEM((blocks, rows, width), F32)],
    )
    coefs = []
    for level in range(levels):
        other_head = partner(head, level + 1, inner_bits)
        if level < levels - 1:
            other_tail = partner(tail, level + 1, inner_bits)
        if level == 0:
            (weights,) = call(
                functools.partial(back_kernel, levels, width, blocks),
                [(rows, leaf_rows)],
                scaled,
                lower,
            )
        count = counts[level] - width
        rest, coef = call(
            functools.partial(pivot_kernel, width),
            [(count, width), (count, width)],
            head,
            other_head,
        )
        coefs.append(coef)
        if level < levels - 1:
            shapes = [(counts[level + 1], width)]
            if level < levels - 2:
                shapes.append((sum(counts[level + 2 :]), width))
            result = call(
                functools.partial(update_kernel, width, levels - 1 - level),
                shapes,
                tail,
                other_tail,
                rest,
                coef,
            )
            head = result[0]
            tail = result[1] if level < levels - 2 else None
    (solution_rows,) = call(
        functools.partial(final_kernel, levels, width), [(leaf_rows, nrhs)], weights, *coefs
    )
    return solution_rows


def solution(mesh):
    placed = (
        P(("rowa", "rowb"), None),
        P(("rowa", "rowb"), None),
        P(None, ("rowa", "rowb"), None),
        P(),
    )
    return jax.shard_map(
        body, mesh=mesh, in_specs=placed, out_specs=P(("rowa", "rowb"), None), check_vma=False
    )
```

profile of v0, /device:TPU:0, one launch (start us, length us, event | category | flops | bytes accessed | tf_op | source)
XLA Modules:
  0.0 103.0 jit_solution(17674881400603811142)
XLA Ops:
  0.0 0.8 copy.5.rhs_ref
  0.8 0.0 copy-start.2
  0.9 0.6 copy-done.2
  1.5 0.0 copy-start
  1.5 1.2 %copy-done = f32[5,384,128]{2,1,0:T(8,128)S(1)} copy-done((f32[5,384,128]{2,1,0:T(8,128)S(1)}, f32[5,384,128]{2,1,0:T(8,128)}, u32[]{:S(2)}) %copy-start) | copy-done | bytes 983064
  2.7 0.0 copy-start.1
  2.7 1.1 %copy-done.1 = f32[384,384]{1,0:T(8,128)S(1)} copy-done((f32[384,384]{1,0:T(8,128)S(1)}, f32[384,384]{1,0:T(8,128)}, u32[]{:S(2)}) %copy-start.1) | copy-done | bytes 589848
  3.8 21.8 %shard_map.46 = (f32[648,128]{1,0:T(8,128)S(1)}, f32[1312,128]{1,0:T(8,128)S(1)}, f32[3,648,128]{2,1,0:T(8,128)S(1)}, f32[3,2,128,128]{3,2,1,0:T(8,128)S(1)}) custom-call(s32[31]{0:T(128)S(1)} %copy-done.2, s32[1]{0:T(128)} %bitcast.place_ref, f32[384,8]{1,0:T(8,128)S(1)} %copy.5.rhs_ref, f32[384,384]{1,0:T(8,128)S(1)} %copy-done.1, f32[5,384,128]{2,1,0:T(8,128)S(1)} %copy-done), custom_call_target="tpu_custom_call" | custom-call | tf_op jit(solution)/shard_map/pallas_call | solution.py:191
  25.6 0.5 collective-permute-start.1
  26.1 0.1 collective-permute-start
  26.2 2.1 %collective-permute-done.other_ref = f32[648,128]{1,0:T(8,128)S(1)} collective-permute-done((f32[648,128]{1,0:T(8,128)S(1)}, f32[648,128]{1,0:T(8,128)S(1)}, u32[]{:S(2)}, u32[]{:S(2)}) %collective-permute-start) | collective-permute-done | bytes 331808 | tf_op jit(solution)/shard_map/ppermute | solution.py:207
  28.3 4.2 %shard_map.48 = (f32[520,128]{1,0:T(8,128)S(1)}, f32[520,128]{1,0:T(8,128)S(1)}) custom-call(f32[648,128]{1,0:T(8,128)S(1)} %get-tuple-element.26.own_ref, f32[648,128]{1,0:T(8,128)S(1)} %collective-permute-done.other_ref), custom_call_target="tpu_custom_call" | custom-call | tf_op jit(solution)/shard_map/pallas_call | solution.py:191
  32.6 0.0 collective-permute-done.1.other_ref
  32.6 1.2 %shard_map.49 = (f32[520,128]{1,0:T(8,128)S(1)}, f32[792,128]{1,0:T(8,128)S(1)}) custom-call(f32[1312,128]{1,0:T(8,128)S(1)} %get-tuple-element.28.own_ref, f32[1312,128]{1,0:T(8,128)S(1)} %collective-permute-done.1.other_ref, f32[520,128]{1,0:T(8,128)S(1)} %get-tuple-element.29.rest_ref, f32[520,128]{1,0:T(8,128)S(1)} %get-tuple-element.27.coef_ref.refs_0_), custom_call_target="tpu_custom_call" | custom-call | tf_op jit(solution)/shard_map/pallas_call | solution.py:191
  33.8 3.0 %collective-permute-start.3 = (f32[792,128]{1,0:T(8,128)S(1)}, f32[792,128]{1,0:T(8,128)S(1)}, u32[]{:S(2)}, u32[]{:S(2)}) collective-permute-start(f32[792,128]{1,0:T(8,128)S(1)} %get-tuple-element.32.own_ref), channel_id=1, source_target_pairs={{0,2},{1,3},{2,0},{3,1},{4,6},{5,7},{6,4},{7,5},{8,10},{9,11},{10,... | collective-permute-start | bytes 1216520 | tf_op jit(solution)/shard_map/ppermute | solution.py:207
  36.8 0.1 collective-permute-start.2
  36.9 15.3 %collective-permute-done.2.other_ref = f32[520,128]{1,0:T(8,128)S(1)} collective-permute-done((f32[520,128]{1,0:T(8,128)S(1)}, f32[520,128]{1,0:T(8,128)S(1)}, u32[]{:S(2)}, u32[]{:S(2)}) %collective-permute-start.2) | collective-permute-done | bytes 266272 | tf_op jit(solution)/shard_map/ppermute | solution.py:207
  52.2 4.1 %shard_map.50 = (f32[392,128]{1,0:T(8,128)S(1)}, f32[392,128]{1,0:T(8,128)S(1)}) custom-call(f32[520,128]{1,0:T(8,128)S(1)} %get-tuple-element.30.own_ref, f32[520,128]{1,0:T(8,128)S(1)} %collective-permute-done.2.other_ref), custom_call_target="tpu_custom_call" | custom-call | tf_op jit(solution)/shard_map/pallas_call | solution.py:191
  56.3 0.0 collective-permute-done.3.other_ref
  56.4 0.8 shard_map.51
  57.2 2.8 %collective-permute-start.5 = (f32[400,128]{1,0:T(8,128)S(1)}, f32[400,128]{1,0:T(8,128)S(1)}, u32[]{:S(2)}, u32[]{:S(2)}) collective-permute-start(f32[400,128]{1,0:T(8,128)S(1)} %get-tuple-element.36.own_ref), channel_id=1, source_target_pairs={{0,4},{1,5},{2,6},{3,7},{4,0},{5,1},{6,2},{7,3},{8,12},{9,13},{10,... | collective-permute-start | bytes 614408 | tf_op jit(solution)/shard_map/ppermute | solution.py:207
  60.0 0.2 collective-permute-start.4
  60.2 17.6 %collective-permute-done.4.other_ref = f32[392,128]{1,0:T(8,128)S(1)} collective-permute-done((f32[392,128]{1,0:T(8,128)S(1)}, f32[392,128]{1,0:T(8,128)S(1)}, u32[]{:S(2)}, u32[]{:S(2)}) %collective-permute-start.4) | collective-permute-done | bytes 200736 | tf_op jit(solution)/shard_map/ppermute | solution.py:207
  77.7 4.3 %shard_map.52 = (f32[264,128]{1,0:T(8,128)S(1)}, f32[264,128]{1,0:T(8,128)S(1)}) custom-call(f32[392,128]{1,0:T(8,128)S(1)} %get-tuple-element.34.own_ref, f32[392,128]{1,0:T(8,128)S(1)} %collective-permute-done.4.other_ref), custom_call_target="tpu_custom_call" | custom-call | tf_op jit(solution)/shard_map/pallas_call | solution.py:191
  82.0 0.0 collective-permute-done.5.other_ref
  82.0 0.5 shard_map.53
  82.5 1.4 %collective-permute-start.6 = (f32[264,128]{1,0:T(8,128)S(1)}, f32[264,128]{1,0:T(8,128)S(1)}, u32[]{:S(2)}, u32[]{:S(2)}) collective-permute-start(f32[264,128]{1,0:T(8,128)S(1)} %get-tuple-element.38.own_ref), channel_id=1, source_target_pairs={{0,8},{8,0},{16,24},{24,16},{1,9},{9,1},{17,25},{25,17},{2,10},{10... | collective-permute-start | bytes 405512 | tf_op jit(solution)/shard_map/ppermute | solution.py:207
  83.9 0.7 collective-permute-start.7
  84.6 3.3 %collective-permute-done.6.other_ref = f32[264,128]{1,0:T(8,128)S(1)} collective-permute-done((f32[264,128]{1,0:T(8,128)S(1)}, f32[264,128]{1,0:T(8,128)S(1)}, u32[]{:S(2)}, u32[]{:S(2)}) %collective-permute-start.6) | collective-permute-done | bytes 135200 | tf_op jit(solution)/shard_map/ppermute | solution.py:207
  87.9 3.9 %shard_map.54 = (f32[136,128]{1,0:T(8,128)S(1)}, f32[136,128]{1,0:T(8,128)S(1)}) custom-call(f32[264,128]{1,0:T(8,128)S(1)} %get-tuple-element.38.own_ref, f32[264,128]{1,0:T(8,128)S(1)} %collective-permute-done.6.other_ref), custom_call_target="tpu_custom_call" | custom-call | tf_op jit(solution)/shard_map/pallas_call | solution.py:191
  91.9 0.0 collective-permute-done.7.other_ref
  91.9 0.3 shard_map.55.own_ref
  92.1 1.3 %collective-permute-start.8 = (f32[136,128]{1,0:T(8,128)S(1)}, f32[136,128]{1,0:T(8,128)S(1)}, u32[]{:S(2)}, u32[]{:S(2)}) collective-permute-start(f32[136,128]{1,0:T(8,128)S(1)} %shard_map.55.own_ref), channel_id=1, source_target_pairs={{0,16},{8,24},{16,0},{24,8},{1,17},{9,25},{17,1},{25,9},{2,18},{10... | collective-permute-start | bytes 208904 | tf_op jit(solution)/shard_map/ppermute | solution.py:207
  93.4 1.7 %shard_map.47.weights_ref = f32[648,384]{1,0:T(8,128)S(1)} custom-call(f32[3,648,128]{2,1,0:T(8,128)S(1)} %get-tuple-element.24.scaled_ref, f32[3,2,128,128]{3,2,1,0:T(8,128)S(1)} %get-tuple-element.25.lower_ref), custom_call_target="tpu_custom_call" | custom-call | tf_op jit(solution)/shard_map/pallas_call | solution.py:191
  95.1 1.4 %collective-permute-done.8.other_ref = f32[136,128]{1,0:T(8,128)S(1)} collective-permute-done((f32[136,128]{1,0:T(8,128)S(1)}, f32[136,128]{1,0:T(8,128)S(1)}, u32[]{:S(2)}, u32[]{:S(2)}) %collective-permute-start.8) | collective-permute-done | bytes 69664 | tf_op jit(solution)/shard_map/ppermute | solution.py:207
  96.5 4.2 %shard_map.56 = (f32[8,128]{1,0:T(8,128)}, f32[8,128]{1,0:T(8,128)S(1)}) custom-call(f32[136,128]{1,0:T(8,128)S(1)} %shard_map.55.own_ref, f32[136,128]{1,0:T(8,128)S(1)} %collective-permute-done.8.other_ref), custom_call_target="tpu_custom_call" | custom-call | tf_op jit(solution)/shard_map/pallas_call | solution.py:191
  100.7 1.6 %shard_map.57 = f32[384,8]{1,0:T(8,128)S(1)} custom-call(f32[648,384]{1,0:T(8,128)S(1)} %shard_map.47.weights_ref, f32[520,128]{1,0:T(8,128)S(1)} %get-tuple-element.27.coef_ref.refs_0_, f32[392,128]{1,0:T(8,128)S(1)} %get-tuple-element.31.coef_ref.refs_1_, f32[264,128]{1,0:T(8,128)S(1)} %get-tuple-element.35.coef_ref.refs_2_, ...), custom_call_target="tpu_custom_call" | custom-call | tf_op jit(solution)/shard_map/pallas_call | solution.py:191
  102.3 0.7 copy.6
Async XLA Ops:
  0.8 0.7 copy-start.2
  1.5 1.2 %copy-start = (f32[5,384,128]{2,1,0:T(8,128)S(1)}, f32[5,384,128]{2,1,0:T(8,128)}, u32[]{:S(2)}) copy-start(f32[5,384,128]{2,1,0:T(8,128)} %bases_ref.1) | copy-start | bytes 2949124
  2.7 1.1 %copy-start.1 = (f32[384,384]{1,0:T(8,128)S(1)}, f32[384,384]{1,0:T(8,128)}, u32[]{:S(2)}) copy-start(f32[384,384]{1,0:T(8,128)} %leaf_ref.1) | copy-start | bytes 1769476
  25.6 7.0 %collective-permute-start.1 = (f32[1312,128]{1,0:T(8,128)S(1)}, f32[1312,128]{1,0:T(8,128)S(1)}, u32[]{:S(2)}, u32[]{:S(2)}) collective-permute-start(f32[1312,128]{1,0:T(8,128)S(1)} %get-tuple-element.28.own_ref), channel_id=1, source_target_pairs={{0,1},{1,0},{2,3},{3,2},{4,5},{5,4},{6,7},{7,6},{8,9},{9,8},{10,11... | collective-permute-start | bytes 2015240 | tf_op jit(solution)/shard_map/ppermute | solution.py:207
  26.1 2.2 %collective-permute-start = (f32[648,128]{1,0:T(8,128)S(1)}, f32[648,128]{1,0:T(8,128)S(1)}, u32[]{:S(2)}, u32[]{:S(2)}) collective-permute-start(f32[648,128]{1,0:T(8,128)S(1)} %get-tuple-element.26.own_ref), channel_id=1, source_target_pairs={{0,1},{1,0},{2,3},{3,2},{4,5},{5,4},{6,7},{7,6},{8,9},{9,8},{10,11... | collective-permute-start | bytes 995336 | tf_op jit(solution)/shard_map/ppermute | solution.py:207
  33.8 22.5 %collective-permute-start.3 = (f32[792,128]{1,0:T(8,128)S(1)}, f32[792,128]{1,0:T(8,128)S(1)}, u32[]{:S(2)}, u32[]{:S(2)}) collective-permute-start(f32[792,128]{1,0:T(8,128)S(1)} %get-tuple-element.32.own_ref), channel_id=1, source_target_pairs={{0,2},{1,3},{2,0},{3,1},{4,6},{5,7},{6,4},{7,5},{8,10},{9,11},{10,... | collective-permute-start | bytes 1216520 | tf_op jit(solution)/shard_map/ppermute | solution.py:207
  36.8 15.4 %collective-permute-start.2 = (f32[520,128]{1,0:T(8,128)S(1)}, f32[520,128]{1,0:T(8,128)S(1)}, u32[]{:S(2)}, u32[]{:S(2)}) collective-permute-start(f32[520,128]{1,0:T(8,128)S(1)} %get-tuple-element.30.own_ref), channel_id=1, source_target_pairs={{0,2},{1,3},{2,0},{3,1},{4,6},{5,7},{6,4},{7,5},{8,10},{9,11},{10,... | collective-permute-start | bytes 798728 | tf_op jit(solution)/shard_map/ppermute | solution.py:207
  57.2 24.8 %collective-permute-start.5 = (f32[400,128]{1,0:T(8,128)S(1)}, f32[400,128]{1,0:T(8,128)S(1)}, u32[]{:S(2)}, u32[]{:S(2)}) collective-permute-start(f32[400,128]{1,0:T(8,128)S(1)} %get-tuple-element.36.own_ref), channel_id=1, source_target_pairs={{0,4},{1,5},{2,6},{3,7},{4,0},{5,1},{6,2},{7,3},{8,12},{9,13},{10,... | collective-permute-start | bytes 614408 | tf_op jit(solution)/shard_map/ppermute | solution.py:207
  60.0 17.7 %collective-permute-start.4 = (f32[392,128]{1,0:T(8,128)S(1)}, f32[392,128]{1,0:T(8,128)S(1)}, u32[]{:S(2)}, u32[]{:S(2)}) collective-permute-start(f32[392,128]{1,0:T(8,128)S(1)} %get-tuple-element.34.own_ref), channel_id=1, source_target_pairs={{0,4},{1,5},{2,6},{3,7},{4,0},{5,1},{6,2},{7,3},{8,12},{9,13},{10,... | collective-permute-start | bytes 602120 | tf_op jit(solution)/shard_map/ppermute | solution.py:207
  82.5 5.4 %collective-permute-start.6 = (f32[264,128]{1,0:T(8,128)S(1)}, f32[264,128]{1,0:T(8,128)S(1)}, u32[]{:S(2)}, u32[]{:S(2)}) collective-permute-start(f32[264,128]{1,0:T(8,128)S(1)} %get-tuple-element.38.own_ref), channel_id=1, source_target_pairs={{0,8},{8,0},{16,24},{24,16},{1,9},{9,1},{17,25},{25,17},{2,10},{10... | collective-permute-start | bytes 405512 | tf_op jit(solution)/shard_map/ppermute | solution.py:207
  83.9 7.9 %collective-permute-start.7 = (f32[136,128]{1,0:T(8,128)S(1)}, f32[136,128]{1,0:T(8,128)S(1)}, u32[]{:S(2)}, u32[]{:S(2)}) collective-permute-start(f32[136,128]{1,0:T(8,128)S(1)} %get-tuple-element.40.own_ref), channel_id=1, source_target_pairs={{0,8},{8,0},{16,24},{24,16},{1,9},{9,1},{17,25},{25,17},{2,10},{10... | collective-permute-start | bytes 208904 | tf_op jit(solution)/shard_map/ppermute | solution.py:207
  92.1 4.4 %collective-permute-start.8 = (f32[136,128]{1,0:T(8,128)S(1)}, f32[136,128]{1,0:T(8,128)S(1)}, u32[]{:S(2)}, u32[]{:S(2)}) collective-permute-start(f32[136,128]{1,0:T(8,128)S(1)} %shard_map.55.own_ref), channel_id=1, source_target_pairs={{0,16},{8,24},{16,0},{24,8},{1,17},{9,25},{17,1},{25,9},{2,18},{10... | collective-permute-start | bytes 208904 | tf_op jit(solution)/shard_map/ppermute | solution.py:207
where the time goes:
time: 103 us
  Pallas kernels  48.6 us (47%)
  waiting for transfers between devices  39.7 us (39%)
  starting transfers between devices  10 us (10%)
  local copies, waits for them, and re-layouts  4.45 us (4%)
    pallas_call x12, Pallas kernels, call(): pl.pallas_call(kernel, out_shape=outs, in_specs=space, out_specs=[pl.Bloc...  48.6 us
    ppermute x9, waiting for transfers between devices, partner(): return lax.ppermute(value, axis, pairs)  39.7 us
    ppermute x9, starting transfers between devices, partner(): return lax.ppermute(value, axis, pairs)  10 us
    unnamed x7, local copies, waits for them, and re-layouts  3.74 us
  transfers between devices with their start and end apart: 9, of which 5 were waited for; matrix products, arithmetic and copies ran while one was open for 0% of the time, Pallas kernels for 18%

commit v1 on v0

v1 whole, which is shorter than its diff:
```python
import functools

import jax
import jax.numpy as jnp
from jax import lax
from jax.experimental import pallas as pl
from jax.experimental.pallas import tpu as pltpu
from jax.sharding import PartitionSpec as P

HIGHEST = lax.Precision.HIGHEST
F32 = jnp.float32
BF16 = jnp.bfloat16
STEP = 16
VMEM_LIMIT = 48 * 1024 * 1024


def dot(left, right):
    return jnp.dot(left, right, precision=HIGHEST, preferred_element_type=F32)


def dot_nt(left, right):
    return lax.dot_general(
        left, right, (((1,), (1,)), ((), ())), precision=HIGHEST, preferred_element_type=F32
    )


def split3(value):
    high = value.astype(BF16).astype(F32)
    rest = value - high
    middle = rest.astype(BF16).astype(F32)
    return high, middle, rest - middle


def reciprocal(value):
    guess = pltpu.reciprocal(value, approx=True)
    return guess * (2.0 - value * guess)


def sweep(matrix, first, last):
    size = matrix.shape[0]
    lane = lax.broadcasted_iota(jnp.int32, (STEP, size), 1)
    sub = lax.broadcasted_iota(jnp.int32, (STEP, size), 0)
    lane_all = lax.broadcasted_iota(jnp.int32, (size, size), 1)
    sub_all = lax.broadcasted_iota(jnp.int32, (size, size), 0)
    for start in range(first, last, STEP):
        stop = start + STEP
        rows = matrix[start:stop, :]
        pivots = [
            jnp.broadcast_to(rows[:, start + index : start + index + 1], (STEP, size))
            for index in range(STEP)
        ]
        inside = (lane >= start) & (lane < stop)
        panel = jnp.where(inside, jnp.where(lane - start == sub, 1.0, 0.0), rows)
        for index in range(STEP):
            scale = reciprocal(pivots[index][index : index + 1, :])
            factor = jnp.where(sub == index, -1.0, pivots[index])
            panel = jnp.where(sub == index, 0.0, panel) - factor * (panel[index : index + 1] * scale)
            for later in range(index + 1, STEP):
                row = pivots[later][index : index + 1] * scale
                pivots[later] = jnp.where(sub == index, 0.0, pivots[later]) - factor * row
        row_inside = (sub_all >= start) & (sub_all < stop)
        lane_inside = (lane_all >= start) & (lane_all < stop)
        column = jnp.where(row_inside, 0.0, matrix)[:, start:stop]
        base = jnp.where(row_inside | lane_inside, 0.0, matrix)
        c_high, c_mid, c_low = split3(column)
        p_high, p_mid, p_low = split3(panel)
        left = jnp.concatenate([c_high, c_high, c_mid, c_high, c_mid, c_low], axis=1).astype(BF16)
        right = jnp.concatenate([p_high, p_mid, p_high, p_low, p_mid, p_high], axis=0).astype(BF16)
        matrix = base - jnp.dot(left, right, preferred_element_type=F32)
        pieces = [matrix[:start]] if start else []
        pieces.append(panel)
        if stop < size:
            pieces.append(matrix[stop:])
        matrix = jnp.concatenate(pieces, axis=0)
    return matrix


def inverse(matrix):
    return sweep(matrix, 0, matrix.shape[0])


def add_eye(matrix):
    row = lax.broadcasted_iota(jnp.int32, matrix.shape, 0)
    column = lax.broadcasted_iota(jnp.int32, matrix.shape, 1)
    return matrix + jnp.where(row == column, 1.0, 0.0)


def leaf_kernel(levels, width, blocks, ranks_ref, place_ref, rhs_ref, leaf_hbm, bases_hbm, *refs):
    key_ref, rest_ref, scaled_ref, lower_ref, v_ref, leaf_ref, bases_ref, sem = refs
    nrhs = rhs_ref.shape[0]
    place = place_ref[0]
    sub = lax.broadcasted_iota(jnp.int32, (width, width), 0)
    rows = levels * width
    spans = [slice(block * width, (block + 1) * width) for block in range(blocks)]
    leaf_copies = [
        pltpu.make_async_copy(leaf_hbm.at[span], leaf_ref.at[span], sem.at[index])
        for index, span in enumerate(spans)
    ]
    bases_copy = pltpu.make_async_copy(bases_hbm, bases_ref, sem.at[blocks])
    for copy in leaf_copies:
        copy.start()
    bases_copy.start()
    leaf_copies[0].wait()
    part = sweep(leaf_ref[spans[0], spans[0]], 0, 2 * STEP)
    for copy in leaf_copies[1:]:
        copy.wait()
    bases_copy.wait()
    for block, span in enumerate(spans):
        for level in range(1, levels + 1):
            rank = ranks_ref[2 ** (levels - level) + lax.shift_right_logical(place, level) - 1]
            piece = bases_ref[level - 1, span, :].T
            v_ref[block, (level - 1) * width : level * width, :] = jnp.where(sub < rank, piece, 0.0)
        v_ref[block, rows : rows + nrhs, :] = rhs_ref[:, span]
    schur = {}
    for first in range(blocks):
        for second in range(first, blocks):
            schur[first, second] = leaf_ref[spans[first], spans[second]]
    for block in range(blocks):
        if block == 0:
            inv = sweep(part, 2 * STEP, width)
        else:
            inv = inverse(schur[block, block])
        values = v_ref[block]
        upper = {}
        for later in range(block + 1, blocks):
            upper[later] = dot(inv, schur[block, later])
            lower_ref[block, later - 1] = upper[later]
        for first in range(block + 1, blocks):
            for second in range(first, blocks):
                product = lax.dot_general(
                    schur[block, first],
                    upper[second],
                    (((0,), (0,)), ((), ())),
                    precision=HIGHEST,
                    preferred_element_type=F32,
                )
                schur[first, second] = schur[first, second] - product
        scaled = dot(values, inv)
        scaled_ref[block] = scaled
        for later in range(block + 1, blocks):
            v_ref[later] = v_ref[later] - dot(scaled, schur[block, later])
        offset = 0
        for level in range(1, levels + 1):
            low = (level - 1) * width
            product = dot_nt(values[low:], scaled[low : low + width])
            pieces = [(rest_ref, product)]
            if level == 1:
                pieces = [(key_ref, product[:width]), (rest_ref, product[width:])]
            for target, piece in pieces:
                span = slice(0, width)
                if target is rest_ref:
                    span = slice(offset, offset + piece.shape[0])
                    offset += piece.shape[0]
                if block == 0:
                    target[span, :] = piece
                else:
                    target[span, :] = target[span, :] + piece


def pivot_kernel(first, last, *refs):
    if first == 0:
        matrix = add_eye(refs[0][...] + refs[1][...])
    else:
        matrix = refs[0][...]
    refs[-1][...] = sweep(matrix, first, last)


def near_update(width, count, take, *refs):
    rest_ref, coef_ref, key_ref = refs[-3:]
    inv_ref = refs[-4]
    take(refs[:-4], rest_ref)
    rest = rest_ref[:count]
    coef_ref[...] = dot(rest, inv_ref[...])
    key_ref[...] = rest_ref[count : count + width] - dot_nt(coef_ref[:width], rest_ref[:width])


def take_full(refs, rest_ref):
    own_ref, other_ref = refs
    rows = rest_ref.shape[0]
    rest_ref[...] = own_ref[:rows] + other_ref[:rows]


def take_halves(plan, refs, rest_ref):
    place_ref, own_ref, near_ref, cross_ref = refs
    side = place_ref[0] & 1
    for index, source in ((side, near_ref), (side ^ 1, cross_ref)):
        span = pl.ds(plan.half_at(index), plan.half)
        rest_ref[span, :] = own_ref[span, :] + source[...]


def take_quarters(plan, refs, rest_ref):
    for index, source in enumerate(refs[1:]):
        span = pl.ds(plan.quarter_at((refs[0][0] & 3) ^ index), plan.quarter)
        rest_ref[span, :] = source[...]


def rank_update(width, count, below, rest_ref, coef_ref, put):
    offset = 0
    for level in range(below):
        low = level * width
        start = low + width if level == 0 else low
        if start < count:
            put(offset, dot_nt(coef_ref[start:, :], rest_ref[low : low + width, :]))
        offset += count - start


def far_update(plan, width, count, below, scatter, *refs):
    place_ref, rest_ref, coef_ref, *more = refs
    outs = more[-3:] if scatter else more[-1:]
    pair = more[: -len(outs)]
    skip = count + width

    def put(offset, product):
        span = slice(skip + offset, skip + offset + product.shape[0])
        if pair:
            value = pair[0][span, :] + pair[1][span, :]
        else:
            value = rest_ref[span, :]
        outs[0][offset : offset + product.shape[0], :] = value - product

    rank_update(width, count, below, rest_ref, coef_ref, put)
    if scatter:
        place = place_ref[0]
        outs[1][...] = outs[0][pl.ds(plan.half_at(place & 1), plan.half), :]
        outs[2][...] = outs[0][
            pl.ds(plan.near + plan.quarter_at((place & 3) ^ 2), plan.quarter), :
        ]


def quarter_update(plan, width, count, below, *refs):
    place_ref, rest_ref, coef_ref, own_ref, other_ref, out_ref, product_ref = refs

    def put(offset, product):
        product_ref[offset : offset + product.shape[0], :] = product

    rank_update(width, count, below, rest_ref, coef_ref, put)
    at = plan.quarter_at(place_ref[0] & 3)
    out_ref[...] = (
        own_ref[pl.ds(plan.near + at, plan.quarter), :]
        + other_ref[...]
        - product_ref[pl.ds(at, plan.quarter), :]
    )


def add_kernel(own_ref, other_ref, out_ref):
    out_ref[...] = own_ref[...] + other_ref[...]


def back_kernel(width, blocks, scaled_ref, lower_ref, out_ref):
    values = [None] * blocks
    for block in reversed(range(blocks)):
        value = scaled_ref[block]
        for later in range(block + 1, blocks):
            value = value - dot_nt(values[later], lower_ref[block, later - 1])
        values[block] = value
        out_ref[:, block * width : (block + 1) * width] = value


def final_kernel(levels, width, own_ref, other_ref, weights_ref, *refs):
    coef_refs, out_ref = refs[:-1], refs[-1]
    inv = inverse(add_eye(own_ref[:width] + other_ref[:width]))
    known = [dot(own_ref[width:] + other_ref[width:], inv)]
    for level in reversed(range(levels - 1)):
        coef = coef_refs[level]
        count = (levels - 1 - level) * width
        value = coef[count:, :]
        for index, later in enumerate(known):
            low = (len(known) - 1 - index) * width
            value = value - dot(later, coef[low : low + width, :])
        known.append(value)
    rows = levels * width
    result = weights_ref[rows:, :]
    for level in range(levels):
        result = result - dot(
            known[levels - 1 - level], weights_ref[level * width : (level + 1) * width, :]
        )
    out_ref[...] = result


def call(kernel, shapes, *operands, flops=0, smem=0, hbm=0, scratch=()):
    flops = flops or 2 * 10**9
    space = [pl.BlockSpec(memory_space=pltpu.SMEM)] * smem
    space += [pl.BlockSpec(memory_space=pltpu.VMEM)] * (len(operands) - smem - hbm)
    space += [pl.BlockSpec(memory_space=pltpu.HBM)] * hbm
    outs = [jax.ShapeDtypeStruct(shape, F32) for shape in shapes]
    return pl.pallas_call(
        kernel,
        out_shape=outs,
        in_specs=space,
        out_specs=[pl.BlockSpec(memory_space=pltpu.VMEM)] * len(outs),
        scratch_shapes=list(scratch),
        compiler_params=pltpu.CompilerParams(vmem_limit_bytes=VMEM_LIMIT),
        cost_estimate=pl.CostEstimate(flops=flops, bytes_accessed=flops // 300, transcendentals=0),
    )(*operands)


def flip(value, mask, axis="rowb"):
    pairs = [(source, source ^ mask) for source in range(lax.axis_size(axis))]
    return lax.ppermute(value, axis, pairs)


def partner(value, level, inner_bits):
    if level < inner_bits:
        return flip(value, 2**level)
    return flip(value, 2 ** (level - inner_bits), "rowa")


def up(value, step):
    return -(-value // step) * step


class Plan:
    def __init__(self, near, far):
        self.near, self.far = near, far
        self.half = up(near, 16) // 2
        self.quarter = up(far, 32) // 4

    def half_at(self, side):
        return pl.multiple_of(side * (self.near - self.half), 8)

    def quarter_at(self, index):
        return pl.multiple_of(jnp.minimum(index * self.quarter, self.far - self.quarter), 8)


def body(right_side, leaves, bases, ranks):
    levels = bases.shape[0]
    leaf_rows = leaves.shape[0]
    width = bases.shape[2]
    nrhs = right_side.shape[1]
    blocks = leaf_rows // width
    inner_bits = lax.axis_size("rowb").bit_length() - 1
    place = lax.axis_index("rowa") * lax.axis_size("rowb") + lax.axis_index("rowb")
    place = place.astype(jnp.int32).reshape(1)
    rows = levels * width + nrhs
    counts = [rows - level * width for level in range(levels)]
    spread = inner_bits >= 3 and levels >= 4
    plan = None
    if spread:
        plan = Plan(counts[1], sum(counts[2:]) - width)
    square = (width, width)
    middle = up(width // 2, STEP)
    key, rest, scaled, lower = call(
        functools.partial(leaf_kernel, levels, width, blocks),
        [square, (sum(counts) - width, width), (blocks, rows, width), (blocks, max(blocks - 1, 1)) + square],
        ranks,
        place,
        right_side.T,
        leaves,
        bases,
        smem=2,
        hbm=2,
        scratch=[
            pltpu.VMEM((blocks, rows, width), F32),
            pltpu.VMEM((leaf_rows, leaf_rows), F32),
            pltpu.VMEM((levels, leaf_rows, width), F32),
            pltpu.SemaphoreType.DMA((blocks + 1,)),
        ],
    )
    coefs = []
    mine = send = None
    for level in range(levels - 1):
        count = counts[level] - width
        below = levels - 1 - level
        other_key = partner(key, level, inner_bits)
        scatter = spread and level == 1
        gather = spread and level == 2
        if scatter:
            near = partner(mine, level, inner_bits)
            send, other_key = lax.optimization_barrier((send, other_key))
            far = partner(send, level, inner_bits)
        elif gather:
            other_quarter = partner(quarter, level, inner_bits)
        else:
            other_rest = partner(rest, level, inner_bits)
        if scatter or gather:
            (half,) = call(functools.partial(pivot_kernel, 0, middle), [square], key, other_key)
            if scatter:
                half, near = lax.optimization_barrier((half, near))
                take = functools.partial(take_halves, plan)
                pieces = [place, rest, near, flip(near, 1)]
            else:
                half, other_quarter = lax.optimization_barrier((half, other_quarter))
                (quarter,) = call(add_kernel, [quarter.shape], quarter, other_quarter)
                take = functools.partial(take_quarters, plan)
                pieces = [place, quarter] + [flip(quarter, mask) for mask in (1, 2, 3)]
            (inv,) = call(functools.partial(pivot_kernel, middle, width), [square], half)
        else:
            (inv,) = call(functools.partial(pivot_kernel, 0, width), [square], key, other_key)
            take = take_full
            pieces = [rest, other_rest]
        total, coef, key = call(
            functools.partial(near_update, width, count, take),
            [(plan.far if gather else counts[level], width), (count, width), square],
            *pieces,
            inv,
            smem=1 if scatter or gather else 0,
        )
        coefs.append(coef)
        if scatter:
            (quarter,) = call(
                functools.partial(quarter_update, plan, width, count, below),
                [(plan.quarter, width)],
                place,
                total,
                coef,
                rest,
                far,
                smem=1,
                scratch=[pltpu.VMEM((plan.far, width), F32)],
            )
            continue
        next_scatter = spread and level == 0
        shapes = [(sum(counts[level + 1 :]) - width, width)]
        if next_scatter:
            shapes += [(plan.half, width), (plan.quarter, width)]
        rest, *sent = call(
            functools.partial(far_update, plan, width, count, below, next_scatter),
            shapes,
            place,
            total,
            coef,
            *([] if gather else [rest, other_rest]),
            smem=1,
        )
        if next_scatter:
            mine, send = sent
    last = jnp.concatenate([key, rest], axis=0)
    other_last = partner(last, levels - 1, inner_bits)
    (weights,) = call(
        functools.partial(back_kernel, width, blocks), [(rows, leaf_rows)], scaled, lower
    )
    (result,) = call(
        functools.partial(final_kernel, levels, width),
        [(nrhs, leaf_rows)],
        last,
        other_last,
        weights,
        *coefs,
    )
    return result.T


def solution(mesh):
    placed = (
        P(("rowa", "rowb"), None),
        P(("rowa", "rowb"), None),
        P(None, ("rowa", "rowb"), None),
        P(),
    )
    return jax.shard_map(
        body, mesh=mesh, in_specs=placed, out_specs=P(("rowa", "rowb"), None), check_vma=False
    )
```

time: 103 us -> 83.9 us (0.81)
  waiting for transfers between devices: 39.7 us -> 15.4 us
  starting transfers between devices: 10 us -> 14.5 us
  Pallas kernels: 48.6 us -> 50.6 us
  local copies, waits for them, and re-layouts: 4.45 us -> 2.97 us
    ppermute x9 -> x14, waiting for transfers between devices: 39.7 us -> 15.4 us  [flip(): return lax.ppermute(value, axis, pairs)]
    ppermute x9 -> x14, starting transfers between devices: 10 us -> 14.5 us  [flip(): return lax.ppermute(value, axis, pairs)]
    pallas_call x12 -> x18, Pallas kernels: 48.6 us -> 50.6 us  [call(): pl.pallas_call(kernel, out_shape=outs, in_specs=space, out_specs=[pl.Bloc...]
    unnamed x7 -> x8, local copies, waits for them, and re-layouts: 3.74 us -> 2.97 us
  transfers between devices with their start and end apart: 9 -> 14, of which waited for: 5 -> 9; matrix products, arithmetic and copies ran while one was open for 0% -> 0% of each run, Pallas kernels for 18% -> 23%
where the time goes in v1:
time: 83.9 us; the launch traced here: 83.7 us
  Pallas kernels  50.6 us (60%)
  waiting for transfers between devices  15.4 us (18%)
  starting transfers between devices  14.5 us (17%)
  local copies, waits for them, and re-layouts  2.97 us (4%)
    pallas_call x18, Pallas kernels, call(): pl.pallas_call(kernel, out_shape=outs, in_specs=space, out_specs=[pl.Bloc...  50.6 us
    ppermute x14, waiting for transfers between devices, flip(): return lax.ppermute(value, axis, pairs)  15.4 us
    ppermute x14, starting transfers between devices, flip(): return lax.ppermute(value, axis, pairs)  14.5 us
    unnamed x8, local copies, waits for them, and re-layouts  2.97 us
  transfers between devices with their start and end apart: 14, of which 9 were waited for; matrix products, arithmetic and copies ran while one was open for 0% of the time, Pallas kernels for 23%

profile of v1, /device:TPU:0, one launch (start us, length us, event | category | flops | bytes accessed | tf_op | source)
XLA Modules:
  0.0 83.7 jit_solution(12552591091706384772)
XLA Ops:
  0.0 0.7 copy-done.2
  0.7 1.2 %copy-done = f32[5,384,128]{2,1,0:T(8,128)S(1)} copy-done((f32[5,384,128]{2,1,0:T(8,128)S(1)}, f32[5,384,128]{2,1,0:T(8,128)}, u32[]{:S(2)}) %copy-start) | copy-done | bytes 983064
  1.9 1.1 %copy-done.1 = f32[384,384]{1,0:T(8,128)S(1)} copy-done((f32[384,384]{1,0:T(8,128)S(1)}, f32[384,384]{1,0:T(8,128)}, u32[]{:S(2)}) %copy-start.1) | copy-done | bytes 589848
  3.0 22.6 %shard_map.46 = (f32[128,128]{1,0:T(8,128)S(1)}, f32[1832,128]{1,0:T(8,128)S(1)}, f32[3,648,128]{2,1,0:T(8,128)S(1)}, f32[3,2,128,128]{3,2,1,0:T(8,128)S(1)}) custom-call(s32[31]{0:T(128)S(1)} %copy-done.3, s32[1]{0:T(128)} %bitcast.place_ref.refs_0_, f32[8,384]{1,0:T(8,128)S(1)} %bitcast.3, f32[384,384]{1,0:T(8,128)S(1)} %copy-done.1, ...), custom_call_target="tpu_custom_call" | custom-call | flops 2000000000 | bytes 6666666 | tf_op jit(solution)/shard_map/pallas_call | solution.py:286
  25.6 0.5 collective-permute-start
  26.1 0.1 collective-permute-start.1
  26.2 2.1 %collective-permute-done.1.refs_1_ = f32[128,128]{1,0:T(8,128)S(1)} collective-permute-done((f32[128,128]{1,0:T(8,128)S(1)}, f32[128,128]{1,0:T(8,128)S(1)}, u32[]{:S(2)}, u32[]{:S(2)}) %collective-permute-start.1) | collective-permute-done | bytes 65568 | tf_op jit(solution)/shard_map/ppermute | solution.py:299
  28.4 3.7 %shard_map.47.refs_2_ = f32[128,128]{1,0:T(8,128)S(1)} custom-call(f32[128,128]{1,0:T(8,128)S(1)} %get-tuple-element.31.refs_0_, f32[128,128]{1,0:T(8,128)S(1)} %collective-permute-done.1.refs_1_), custom_call_target="tpu_custom_call" | custom-call | flops 2000000000 | bytes 6666666 | tf_op jit(solution)/shard_map/pallas_call | solution.py:286
  32.1 0.0 collective-permute-done.refs_1_.refs_4_
  32.1 0.8 %shard_map.48 = (f32[648,128]{1,0:T(8,128)S(1)}, f32[520,128]{1,0:T(8,128)S(1)}, f32[128,128]{1,0:T(8,128)S(1)}) custom-call(f32[1832,128]{1,0:T(8,128)S(1)} %get-tuple-element.30.refs_0_.refs_3_, f32[1832,128]{1,0:T(8,128)S(1)} %collective-permute-done.refs_1_.refs_4_, f32[128,128]{1,0:T(8,128)S(1)} %shard_map.47.refs_2_), custom_call_target="tpu_custom_call" | custom-call | flops 2000000000 | bytes 6666666 | tf_op jit(solution)/shard_map/pallas_call | solution.py:286
  32.9 3.0 %collective-permute-start.2 = (f32[128,128]{1,0:T(8,128)S(1)}, f32[128,128]{1,0:T(8,128)S(1)}, u32[]{:S(2)}, u32[]{:S(2)}) collective-permute-start(f32[128,128]{1,0:T(8,128)S(1)} %get-tuple-element.35.refs_0_), channel_id=1, source_target_pairs={{0,2},{1,3},{2,0},{3,1},{4,6},{5,7},{6,4},{7,5},{8,10},{9,11},{10,... | collective-permute-start | bytes 196616 | tf_op jit(solution)/shard_map/ppermute | solution.py:299
  35.9 1.2 %shard_map.49 = (f32[1184,128]{1,0:T(8,128)S(1)}, f32[264,128]{1,0:T(8,128)S(1)}, f32[168,128]{1,0:T(8,128)S(1)}) custom-call(s32[1]{0:T(128)} %bitcast.place_ref.refs_0_, f32[648,128]{1,0:T(8,128)S(1)} %get-tuple-element.32.refs_1_, f32[520,128]{1,0:T(8,128)S(1)} %get-tuple-element.33.refs_2_.refs_0_, f32[1832,128]{1,0:T(8,128)S(1)} %get-tuple-element.30.refs_0_.refs_3_, ...), custom_call_target="tpu_custom_call" | custom-call | flops 2000000000 | bytes 6666666 | tf_op jit(solution)/shard_map/pallas_call | solution.py:286
  37.1 0.1 collective-permute-start.3
  37.2 1.1 %collective-permute-done.2.refs_1_ = f32[128,128]{1,0:T(8,128)S(1)} collective-permute-done((f32[128,128]{1,0:T(8,128)S(1)}, f32[128,128]{1,0:T(8,128)S(1)}, u32[]{:S(2)}, u32[]{:S(2)}) %collective-permute-start.2) | collective-permute-done | bytes 65568 | tf_op jit(solution)/shard_map/ppermute | solution.py:299
  38.3 2.2 %collective-permute-start.5 = (f32[168,128]{1,0:T(8,128)S(1)}, f32[168,128]{1,0:T(8,128)S(1)}, u32[]{:S(2)}, u32[]{:S(2)}) collective-permute-start(f32[168,128]{1,0:T(8,128)S(1)} %get-tuple-element.43), channel_id=1, source_target_pairs={{0,2},{1,3},{2,0},{3,1},{4,6},{5,7},{6,4},{7,5},{8,10},{9,11},{10,... | collective-permute-start | bytes 258056 | tf_op jit(solution)/shard_map/ppermute | solution.py:299
  40.5 1.8 %shard_map.50.refs_0_ = f32[128,128]{1,0:T(8,128)S(1)} custom-call(f32[128,128]{1,0:T(8,128)S(1)} %get-tuple-element.35.refs_0_, f32[128,128]{1,0:T(8,128)S(1)} %collective-permute-done.2.refs_1_), custom_call_target="tpu_custom_call" | custom-call | flops 2000000000 | bytes 6666666 | tf_op jit(solution)/shard_map/pallas_call | solution.py:286
  42.3 1.1 %collective-permute-done.3.refs_2_ = f32[264,128]{1,0:T(8,128)S(1)} collective-permute-done((f32[264,128]{1,0:T(8,128)S(1)}, f32[264,128]{1,0:T(8,128)S(1)}, u32[]{:S(2)}, u32[]{:S(2)}) %collective-permute-start.3) | collective-permute-done | bytes 135200 | tf_op jit(solution)/shard_map/ppermute | solution.py:299
  43.5 0.0 collective-permute-start.4
  43.5 1.8 %shard_map.51.refs_4_ = f32[128,128]{1,0:T(8,128)S(1)} custom-call(f32[128,128]{1,0:T(8,128)S(1)} %shard_map.50.refs_0_), custom_call_target="tpu_custom_call" | custom-call | flops 2000000000 | bytes 6666666 | tf_op jit(solution)/shard_map/pallas_call | solution.py:286
  45.3 0.0 collective-permute-done.4.refs_3_
  45.3 0.8 shard_map.52
  46.1 2.7 %collective-permute-start.6 = (f32[128,128]{1,0:T(8,128)S(1)}, f32[128,128]{1,0:T(8,128)S(1)}, u32[]{:S(2)}, u32[]{:S(2)}) collective-permute-start(f32[128,128]{1,0:T(8,128)S(1)} %get-tuple-element.44.refs_0_), channel_id=1, source_target_pairs={{0,4},{1,5},{2,6},{3,7},{4,0},{5,1},{6,2},{7,3},{8,12},{9,13},{10,... | collective-permute-start | bytes 196616 | tf_op jit(solution)/shard_map/ppermute | solution.py:299
  48.7 0.0 collective-permute-done.5.refs_4_
  48.7 0.7 shard_map.53.own_ref
  49.5 0.4 collective-permute-start.7
  49.9 3.0 %collective-permute-done.6.refs_1_ = f32[128,128]{1,0:T(8,128)S(1)} collective-permute-done((f32[128,128]{1,0:T(8,128)S(1)}, f32[128,128]{1,0:T(8,128)S(1)}, u32[]{:S(2)}, u32[]{:S(2)}) %collective-permute-start.6) | collective-permute-done | bytes 65568 | tf_op jit(solution)/shard_map/ppermute | solution.py:299
  52.9 2.0 %shard_map.54.refs_0_ = f32[128,128]{1,0:T(8,128)S(1)} custom-call(f32[128,128]{1,0:T(8,128)S(1)} %get-tuple-element.44.refs_0_, f32[128,128]{1,0:T(8,128)S(1)} %collective-permute-done.6.refs_1_), custom_call_target="tpu_custom_call" | custom-call | flops 2000000000 | bytes 6666666 | tf_op jit(solution)/shard_map/pallas_call | solution.py:286
  54.9 2.0 %collective-permute-done.7.other_ref = f32[168,128]{1,0:T(8,128)S(1)} collective-permute-done((f32[168,128]{1,0:T(8,128)S(1)}, f32[168,128]{1,0:T(8,128)S(1)}, u32[]{:S(2)}, u32[]{:S(2)}) %collective-permute-start.7) | collective-permute-done | bytes 86048 | tf_op jit(solution)/shard_map/ppermute | solution.py:299
  56.9 0.1 collective-permute-start.10
  57.0 1.7 %collective-permute-start.9 = (f32[168,128]{1,0:T(8,128)S(1)}, f32[168,128]{1,0:T(8,128)S(1)}, u32[]{:S(2)}, u32[]{:S(2)}) collective-permute-start(f32[168,128]{1,0:T(8,128)S(1)} %shard_map.55.refs_1_), channel_id=1, source_target_pairs={{0,2},{1,3},{2,0},{3,1},{4,6},{5,7},{6,4},{7,5},{8,10},{9,11},{10,... | collective-permute-start | bytes 258056 | tf_op jit(solution)/shard_map/ppermute | solution.py:299
  58.7 0.2 collective-permute-start.8
  58.9 1.8 %shard_map.56.refs_5_ = f32[128,128]{1,0:T(8,128)S(1)} custom-call(f32[128,128]{1,0:T(8,128)S(1)} %shard_map.54.refs_0_), custom_call_target="tpu_custom_call" | custom-call | flops 2000000000 | bytes 6666666 | tf_op jit(solution)/shard_map/pallas_call | solution.py:286
  60.7 0.9 %collective-permute-done.10.refs_4_ = f32[168,128]{1,0:T(8,128)S(1)} collective-permute-done((f32[168,128]{1,0:T(8,128)S(1)}, f32[168,128]{1,0:T(8,128)S(1)}, u32[]{:S(2)}, u32[]{:S(2)}) %collective-permute-start.10) | collective-permute-done | bytes 86048 | tf_op jit(solution)/shard_map/ppermute | solution.py:299
  61.6 2.1 %collective-permute-done.9.refs_3_ = f32[168,128]{1,0:T(8,128)S(1)} collective-permute-done((f32[168,128]{1,0:T(8,128)S(1)}, f32[168,128]{1,0:T(8,128)S(1)}, u32[]{:S(2)}, u32[]{:S(2)}) %collective-permute-start.9) | collective-permute-done | bytes 86048 | tf_op jit(solution)/shard_map/ppermute | solution.py:299
  63.7 0.0 collective-permute-done.8.refs_2_
  63.7 0.7 shard_map.57
  64.4 1.6 %collective-permute-start.12 = (f32[128,128]{1,0:T(8,128)S(1)}, f32[128,128]{1,0:T(8,128)S(1)}, u32[]{:S(2)}, u32[]{:S(2)}) collective-permute-start(f32[128,128]{1,0:T(8,128)S(1)} %get-tuple-element.49.refs_0_), channel_id=1, source_target_pairs={{0,8},{8,0},{16,24},{24,16},{1,9},{9,1},{17,25},{25,17},{2,10},{10... | collective-permute-start | bytes 196616 | tf_op jit(solution)/shard_map/ppermute | solution.py:299
  65.9 0.4 shard_map.58.refs_0_.refs_3_
  66.3 0.6 collective-permute-start.11
  66.9 2.0 %collective-permute-done.12.refs_1_ = f32[128,128]{1,0:T(8,128)S(1)} collective-permute-done((f32[128,128]{1,0:T(8,128)S(1)}, f32[128,128]{1,0:T(8,128)S(1)}, u32[]{:S(2)}, u32[]{:S(2)}) %collective-permute-start.12) | collective-permute-done | bytes 65568 | tf_op jit(solution)/shard_map/ppermute | solution.py:299
  68.9 3.7 %shard_map.59.refs_2_ = f32[128,128]{1,0:T(8,128)S(1)} custom-call(f32[128,128]{1,0:T(8,128)S(1)} %get-tuple-element.49.refs_0_, f32[128,128]{1,0:T(8,128)S(1)} %collective-permute-done.12.refs_1_), custom_call_target="tpu_custom_call" | custom-call | flops 2000000000 | bytes 6666666 | tf_op jit(solution)/shard_map/pallas_call | solution.py:286
  72.6 0.0 collective-permute-done.11.refs_1_.refs_4_
  72.6 0.6 shard_map.60
  73.2 0.2 shard_map.61
  73.4 1.5 %collective-permute-start.13 = (f32[136,128]{1,0:T(8,128)S(1)}, f32[136,128]{1,0:T(8,128)S(1)}, u32[]{:S(2)}, u32[]{:S(2)}) collective-permute-start(f32[136,128]{1,0:T(8,128)S(1)} %pad_maximum_fusion.own_ref), channel_id=1, source_target_pairs={{0,16},{8,24},{16,0},{24,8},{1,17},{9,25},{17,1},{25,9},{2,18},{10... | collective-permute-start | bytes 208904 | tf_op jit(solution)/shard_map/ppermute | solution.py:299
  75.0 1.7 %shard_map.62.weights_ref = f32[648,384]{1,0:T(8,128)S(1)} custom-call(f32[3,648,128]{2,1,0:T(8,128)S(1)} %get-tuple-element.53.scaled_ref, f32[3,2,128,128]{3,2,1,0:T(8,128)S(1)} %get-tuple-element.54.lower_ref), custom_call_target="tpu_custom_call" | custom-call | flops 2000000000 | bytes 6666666 | tf_op jit(solution)/shard_map/pallas_call | solution.py:286
  76.7 1.1 %collective-permute-done.13.other_ref = f32[136,128]{1,0:T(8,128)S(1)} collective-permute-done((f32[136,128]{1,0:T(8,128)S(1)}, f32[136,128]{1,0:T(8,128)S(1)}, u32[]{:S(2)}, u32[]{:S(2)}) %collective-permute-start.13) | collective-permute-done | bytes 69664 | tf_op jit(solution)/shard_map/ppermute | solution.py:299
  77.8 5.9 %shard_map.63 = f32[8,384]{1,0:T(8,128)} custom-call(f32[136,128]{1,0:T(8,128)S(1)} %pad_maximum_fusion.own_ref, f32[136,128]{1,0:T(8,128)S(1)} %collective-permute-done.13.other_ref, f32[648,384]{1,0:T(8,128)S(1)} %shard_map.62.weights_ref, f32[520,128]{1,0:T(8,128)S(1)} %get-tuple-element.33.refs_2_.refs_0_, ...), custom_call_target="tpu_custom_call" | custom-call | flops 2000000000 | bytes 6666666 | tf_op jit(solution)/shard_map/pallas_call | solution.py:286
  (7 shorter events, 0.0 us)
Async XLA Ops:
  0.0 0.7 copy-start.2
  0.0 0.7 copy-start.3
  0.7 1.2 %copy-start = (f32[5,384,128]{2,1,0:T(8,128)S(1)}, f32[5,384,128]{2,1,0:T(8,128)}, u32[]{:S(2)}) copy-start(f32[5,384,128]{2,1,0:T(8,128)} %bases_hbm.1) | copy-start | bytes 2949124
  1.9 1.1 %copy-start.1 = (f32[384,384]{1,0:T(8,128)S(1)}, f32[384,384]{1,0:T(8,128)}, u32[]{:S(2)}) copy-start(f32[384,384]{1,0:T(8,128)} %leaf_hbm.1) | copy-start | bytes 1769476
  25.6 6.4 %collective-permute-start = (f32[1832,128]{1,0:T(8,128)S(1)}, f32[1832,128]{1,0:T(8,128)S(1)}, u32[]{:S(2)}, u32[]{:S(2)}) collective-permute-start(f32[1832,128]{1,0:T(8,128)S(1)} %get-tuple-element.30.refs_0_.refs_3_), channel_id=1, source_target_pairs={{0,1},{1,0},{2,3},{3,2},{4,5},{5,4},{6,7},{7,6},{8,9},{9,8},{10,11... | collective-permute-start | bytes 2813960 | tf_op jit(solution)/shard_map/ppermute | solution.py:299
  26.1 2.2 %collective-permute-start.1 = (f32[128,128]{1,0:T(8,128)S(1)}, f32[128,128]{1,0:T(8,128)S(1)}, u32[]{:S(2)}, u32[]{:S(2)}) collective-permute-start(f32[128,128]{1,0:T(8,128)S(1)} %get-tuple-element.31.refs_0_), channel_id=1, source_target_pairs={{0,1},{1,0},{2,3},{3,2},{4,5},{5,4},{6,7},{7,6},{8,9},{9,8},{10,11... | collective-permute-start | bytes 196616 | tf_op jit(solution)/shard_map/ppermute | solution.py:299
  32.9 5.4 %collective-permute-start.2 = (f32[128,128]{1,0:T(8,128)S(1)}, f32[128,128]{1,0:T(8,128)S(1)}, u32[]{:S(2)}, u32[]{:S(2)}) collective-permute-start(f32[128,128]{1,0:T(8,128)S(1)} %get-tuple-element.35.refs_0_), channel_id=1, source_target_pairs={{0,2},{1,3},{2,0},{3,1},{4,6},{5,7},{6,4},{7,5},{8,10},{9,11},{10,... | collective-permute-start | bytes 196616 | tf_op jit(solution)/shard_map/ppermute | solution.py:299
  37.1 6.3 %collective-permute-start.3 = (f32[264,128]{1,0:T(8,128)S(1)}, f32[264,128]{1,0:T(8,128)S(1)}, u32[]{:S(2)}, u32[]{:S(2)}) collective-permute-start(f32[264,128]{1,0:T(8,128)S(1)} %get-tuple-element.38), channel_id=1, source_target_pairs={{0,2},{1,3},{2,0},{3,1},{4,6},{5,7},{6,4},{7,5},{8,10},{9,11},{10,... | collective-permute-start | bytes 405512 | tf_op jit(solution)/shard_map/ppermute | solution.py:299
  38.3 10.4 %collective-permute-start.5 = (f32[168,128]{1,0:T(8,128)S(1)}, f32[168,128]{1,0:T(8,128)S(1)}, u32[]{:S(2)}, u32[]{:S(2)}) collective-permute-start(f32[168,128]{1,0:T(8,128)S(1)} %get-tuple-element.43), channel_id=1, source_target_pairs={{0,2},{1,3},{2,0},{3,1},{4,6},{5,7},{6,4},{7,5},{8,10},{9,11},{10,... | collective-permute-start | bytes 258056 | tf_op jit(solution)/shard_map/ppermute | solution.py:299
  43.5 1.8 %collective-permute-start.4 = (f32[264,128]{1,0:T(8,128)S(1)}, f32[264,128]{1,0:T(8,128)S(1)}, u32[]{:S(2)}, u32[]{:S(2)}) collective-permute-start(f32[264,128]{1,0:T(8,128)S(1)} %collective-permute-done.3.refs_2_), channel_id=1, source_target_pairs={{0,1},{1,0},{2,3},{3,2},{4,5},{5,4},{6,7},{7,6},{8,9},{9,8},{10,11... | collective-permute-start | bytes 405512 | tf_op jit(solution)/shard_map/ppermute | solution.py:299
  46.1 6.8 %collective-permute-start.6 = (f32[128,128]{1,0:T(8,128)S(1)}, f32[128,128]{1,0:T(8,128)S(1)}, u32[]{:S(2)}, u32[]{:S(2)}) collective-permute-start(f32[128,128]{1,0:T(8,128)S(1)} %get-tuple-element.44.refs_0_), channel_id=1, source_target_pairs={{0,4},{1,5},{2,6},{3,7},{4,0},{5,1},{6,2},{7,3},{8,12},{9,13},{10,... | collective-permute-start | bytes 196616 | tf_op jit(solution)/shard_map/ppermute | solution.py:299
  49.5 7.5 %collective-permute-start.7 = (f32[168,128]{1,0:T(8,128)S(1)}, f32[168,128]{1,0:T(8,128)S(1)}, u32[]{:S(2)}, u32[]{:S(2)}) collective-permute-start(f32[168,128]{1,0:T(8,128)S(1)} %shard_map.53.own_ref), channel_id=1, source_target_pairs={{0,4},{1,5},{2,6},{3,7},{4,0},{5,1},{6,2},{7,3},{8,12},{9,13},{10,... | collective-permute-start | bytes 258056 | tf_op jit(solution)/shard_map/ppermute | solution.py:299
  56.9 4.7 %collective-permute-start.10 = (f32[168,128]{1,0:T(8,128)S(1)}, f32[168,128]{1,0:T(8,128)S(1)}, u32[]{:S(2)}, u32[]{:S(2)}) collective-permute-start(f32[168,128]{1,0:T(8,128)S(1)} %shard_map.55.refs_1_), channel_id=1, source_target_pairs={{0,3},{1,2},{2,1},{3,0},{4,7},{5,6},{6,5},{7,4},{8,11},{9,10},{10,... | collective-permute-start | bytes 258056 | tf_op jit(solution)/shard_map/ppermute | solution.py:299
  57.0 6.7 %collective-permute-start.9 = (f32[168,128]{1,0:T(8,128)S(1)}, f32[168,128]{1,0:T(8,128)S(1)}, u32[]{:S(2)}, u32[]{:S(2)}) collective-permute-start(f32[168,128]{1,0:T(8,128)S(1)} %shard_map.55.refs_1_), channel_id=1, source_target_pairs={{0,2},{1,3},{2,0},{3,1},{4,6},{5,7},{6,4},{7,5},{8,10},{9,11},{10,... | collective-permute-start | bytes 258056 | tf_op jit(solution)/shard_map/ppermute | solution.py:299
  58.7 5.0 %collective-permute-start.8 = (f32[168,128]{1,0:T(8,128)S(1)}, f32[168,128]{1,0:T(8,128)S(1)}, u32[]{:S(2)}, u32[]{:S(2)}) collective-permute-start(f32[168,128]{1,0:T(8,128)S(1)} %shard_map.55.refs_1_), channel_id=1, source_target_pairs={{0,1},{1,0},{2,3},{3,2},{4,5},{5,4},{6,7},{7,6},{8,9},{9,8},{10,11... | collective-permute-start | bytes 258056 | tf_op jit(solution)/shard_map/ppermute | solution.py:299
  64.4 4.5 %collective-permute-start.12 = (f32[128,128]{1,0:T(8,128)S(1)}, f32[128,128]{1,0:T(8,128)S(1)}, u32[]{:S(2)}, u32[]{:S(2)}) collective-permute-start(f32[128,128]{1,0:T(8,128)S(1)} %get-tuple-element.49.refs_0_), channel_id=1, source_target_pairs={{0,8},{8,0},{16,24},{24,16},{1,9},{9,1},{17,25},{25,17},{2,10},{10... | collective-permute-start | bytes 196616 | tf_op jit(solution)/shard_map/ppermute | solution.py:299
  66.3 6.3 %collective-permute-start.11 = (f32[272,128]{1,0:T(8,128)S(1)}, f32[272,128]{1,0:T(8,128)S(1)}, u32[]{:S(2)}, u32[]{:S(2)}) collective-permute-start(f32[272,128]{1,0:T(8,128)S(1)} %shard_map.58.refs_0_.refs_3_), channel_id=1, source_target_pairs={{0,8},{8,0},{16,24},{24,16},{1,9},{9,1},{17,25},{25,17},{2,10},{10... | collective-permute-start | bytes 417800 | tf_op jit(solution)/shard_map/ppermute | solution.py:299
  73.4 4.3 %collective-permute-start.13 = (f32[136,128]{1,0:T(8,128)S(1)}, f32[136,128]{1,0:T(8,128)S(1)}, u32[]{:S(2)}, u32[]{:S(2)}) collective-permute-start(f32[136,128]{1,0:T(8,128)S(1)} %pad_maximum_fusion.own_ref), channel_id=1, source_target_pairs={{0,16},{8,24},{16,0},{24,8},{1,17},{9,25},{17,1},{25,9},{2,18},{10... | collective-permute-start | bytes 208904 | tf_op jit(solution)/shard_map/ppermute | solution.py:299

commit v2 on v1

--- a/solution.py
+++ b/solution.py
@@ -7,76 +7,143 @@
 from jax.experimental.pallas import tpu as pltpu
 from jax.sharding import PartitionSpec as P
 
-HIGHEST = lax.Precision.HIGHEST
 F32 = jnp.float32
 BF16 = jnp.bfloat16
 STEP = 16
 VMEM_LIMIT = 48 * 1024 * 1024
 
 
+def split3(value):
+    high = value.astype(BF16)
+    rest = value - high.astype(F32)
+    middle = rest.astype(BF16)
+    return high, middle, (rest - middle.astype(F32)).astype(BF16)
+
+
+def left6(value):
+    high, middle, low = split3(value)
+    return jnp.concatenate([high, high, middle, high, middle, low], axis=1)
+
+
+def right6(value, axis):
+    high, middle, low = split3(value)
+    return jnp.concatenate([high, middle, high, low, middle, high], axis=axis)
+
+
+def pad_rows(value):
+    extra = -value.shape[0] % 16
+    if not extra:
+        return value
+    return jnp.concatenate([value, jnp.zeros((extra, value.shape[1]), value.dtype)], axis=0)
+
+
 def dot(left, right):
-    return jnp.dot(left, right, precision=HIGHEST, preferred_element_type=F32)
+    product = jnp.dot(left6(pad_rows(left)), right6(right, 0), preferred_element_type=F32)
+    return product[: left.shape[0]]
 
 
 def dot_nt(left, right):
-    return lax.dot_general(
-        left, right, (((1,), (1,)), ((), ())), precision=HIGHEST, preferred_element_type=F32
-    )
-
-
-def split3(value):
-    high = value.astype(BF16).astype(F32)
-    rest = value - high
-    middle = rest.astype(BF16).astype(F32)
-    return high, middle, rest - middle
-
-
-def reciprocal(value):
-    guess = pltpu.reciprocal(value, approx=True)
-    return guess * (2.0 - value * guess)
-
-
-def sweep(matrix, first, last):
+    product = dot6_nt(left6(pad_rows(left)), right6(right, 1))
+    return product[: left.shape[0]]
+
+
+def dot6_nt(left, right):
+    return lax.dot_general(left, right, (((1,), (1,)), ((), ())), preferred_element_type=F32)
+
+
+def spread_row(value, index):
+    return jnp.broadcast_to(value[index : index + 1, :], value.shape)
+
+
+def eliminate(panel, pivots):
+    sub = lax.broadcasted_iota(jnp.int32, panel[0].shape, 0)
+    pieces = range(len(panel))
+    pivot = spread_row(pivots[0][0], 0)
+    for step in range(STEP):
+        piece, index = divmod(step, 8)
+        scale = pltpu.reciprocal(pivot, approx=True)
+        if step + 1 < STEP:
+            next_piece, next_index = divmod(step + 1, 8)
+            cross = spread_row(pivots[step][next_piece], next_index) * spread_row(
+                pivots[step + 1][piece], index
+            )
+            pivot = spread_row(pivots[step + 1][next_piece], next_index) - cross * scale
+        own = sub == index
+        factors = [
+            (jnp.where(own, -1.0, pivots[step][at]) if at == piece else pivots[step][at]) * scale
+            for at in pieces
+        ]
+
+        def reduce(column):
+            row = spread_row(column[piece], index)
+            return [
+                (jnp.where(own, 0.0, column[at]) if at == piece else column[at]) - factors[at] * row
+                for at in pieces
+            ]
+
+        panel = reduce(panel)
+        for later in range(step + 1, STEP):
+            pivots[later] = reduce(pivots[later])
+    return panel
+
+
+def sweep(matrix, first, last, tick=lambda: None):
     size = matrix.shape[0]
-    lane = lax.broadcasted_iota(jnp.int32, (STEP, size), 1)
-    sub = lax.broadcasted_iota(jnp.int32, (STEP, size), 0)
+    pieces = range(STEP // 8)
+    lane = lax.broadcasted_iota(jnp.int32, (8, size), 1)
+    sub = lax.broadcasted_iota(jnp.int32, (8, size), 0)
     lane_all = lax.broadcasted_iota(jnp.int32, (size, size), 1)
     sub_all = lax.broadcasted_iota(jnp.int32, (size, size), 0)
+    rows = [matrix[first + 8 * at : first + 8 * at + 8] for at in pieces]
     for start in range(first, last, STEP):
         stop = start + STEP
-        rows = matrix[start:stop, :]
+        more = stop < size
         pivots = [
-            jnp.broadcast_to(rows[:, start + index : start + index + 1], (STEP, size))
+            [jnp.broadcast_to(rows[at][:, start + index : start + index + 1], (8, size)) for at in pieces]
             for index in range(STEP)
         ]
         inside = (lane >= start) & (lane < stop)
-        panel = jnp.where(inside, jnp.where(lane - start == sub, 1.0, 0.0), rows)
-        for index in range(STEP):
-            scale = reciprocal(pivots[index][index : index + 1, :])
-            factor = jnp.where(sub == index, -1.0, pivots[index])
-            panel = jnp.where(sub == index, 0.0, panel) - factor * (panel[index : index + 1] * scale)
-            for later in range(index + 1, STEP):
-                row = pivots[later][index : index + 1] * scale
-                pivots[later] = jnp.where(sub == index, 0.0, pivots[later]) - factor * row
+        panel = [
+            jnp.where(inside, jnp.where(lane - start == sub + 8 * at, 1.0, 0.0), rows[at])
+            for at in pieces
+        ]
         row_inside = (sub_all >= start) & (sub_all < stop)
         lane_inside = (lane_all >= start) & (lane_all < stop)
         column = jnp.where(row_inside, 0.0, matrix)[:, start:stop]
         base = jnp.where(row_inside | lane_inside, 0.0, matrix)
-        c_high, c_mid, c_low = split3(column)
-        p_high, p_mid, p_low = split3(panel)
-        left = jnp.concatenate([c_high, c_high, c_mid, c_high, c_mid, c_low], axis=1).astype(BF16)
-        right = jnp.concatenate([p_high, p_mid, p_high, p_low, p_mid, p_high], axis=0).astype(BF16)
-        matrix = base - jnp.dot(left, right, preferred_element_type=F32)
-        pieces = [matrix[:start]] if start else []
-        pieces.append(panel)
-        if stop < size:
-            pieces.append(matrix[stop:])
-        matrix = jnp.concatenate(pieces, axis=0)
+        following = []
+        if more:
+            following = [matrix[stop + 8 * at : stop + 8 * at + 8] for at in pieces]
+        ahead = [
+            [jnp.broadcast_to(piece[:, start + index : start + index + 1], (8, size)) for piece in following]
+            for index in range(STEP)
+        ]
+        tick()
+        panel = eliminate(panel, pivots)
+        if more:
+            rows = []
+            for at in pieces:
+                terms = [
+                    ahead[index][at] * spread_row(panel[index // 8], index % 8)
+                    for index in range(STEP)
+                ]
+                while len(terms) > 1:
+                    terms = [terms[at2] + terms[at2 + 1] for at2 in range(0, len(terms), 2)]
+                rows.append(base[stop + 8 * at : stop + 8 * at + 8] - terms[0])
+        joined = jnp.concatenate(panel, axis=0)
+        matrix = base - jnp.dot(left6(column), right6(joined, 0), preferred_element_type=F32)
+        parts = [matrix[:start]] if start else []
+        parts.append(joined)
+        if more:
+            parts += rows
+        if stop + (STEP if more else 0) < size:
+            parts.append(matrix[stop + STEP :])
+        matrix = jnp.concatenate(parts, axis=0)
     return matrix
 
 
-def inverse(matrix):
-    return sweep(matrix, 0, matrix.shape[0])
+def inverse(matrix, tick=lambda: None):
+    return sweep(matrix, 0, matrix.shape[0], tick)
 
 
 def add_eye(matrix):
@@ -86,11 +153,12 @@
 
 
 def leaf_kernel(levels, width, blocks, ranks_ref, place_ref, rhs_ref, leaf_hbm, bases_hbm, *refs):
-    key_ref, rest_ref, scaled_ref, lower_ref, v_ref, leaf_ref, bases_ref, sem = refs
+    key_ref, rest_ref, scaled_ref, lower_ref, v_ref, v6_ref, s6_ref, leaf_ref, bases_ref, sem = refs
     nrhs = rhs_ref.shape[0]
     place = place_ref[0]
-    sub = lax.broadcasted_iota(jnp.int32, (width, width), 0)
     rows = levels * width
+    count = rows + nrhs
+    padded = v6_ref.shape[0]
     spans = [slice(block * width, (block + 1) * width) for block in range(blocks)]
     leaf_copies = [
         pltpu.make_async_copy(leaf_hbm.at[span], leaf_ref.at[span], sem.at[index])
@@ -100,61 +168,113 @@
     for copy in leaf_copies:
         copy.start()
     bases_copy.start()
+
+    tasks = []
+    quota = [0]
+
+    def tick():
+        for _ in range(min(quota[0], len(tasks))):
+            tasks.pop(0)()
+
+    def run(steps):
+        quota[0] = -(-len(tasks) // steps)
+
+    def arrive():
+        for copy in leaf_copies[1:]:
+            copy.wait()
+        bases_copy.wait()
+
+    def load(block, level):
+        sub = lax.broadcasted_iota(jnp.int32, (width, width), 0)
+        rank = ranks_ref[2 ** (levels - level) + lax.shift_right_logical(place, level) - 1]
+        piece = jnp.where(sub < rank, bases_ref[level - 1, spans[block], :].T, 0.0)
+        span = slice((level - 1) * width, level * width)
+        v_ref[block, span, :] = piece
+        if block == 0:
+            v6_ref[span, :] = left6(piece)
+
+    def load_rhs():
+        for block, span in enumerate(spans):
+            piece = rhs_ref[:, span]
+            piece = jnp.concatenate([piece, jnp.zeros((padded - count, width), F32)], axis=0)
+            v_ref[block, rows:padded, :] = piece
+            if block == 0:
+                v6_ref[rows:padded, :] = left6(piece)
+
+    chunk = up(padded // 3, 16)
+    chunks = [slice(at, min(at + chunk, padded)) for at in range(0, padded, chunk)]
+
+    def split_values(block, span):
+        v6_ref[span, :] = left6(v_ref[block, span, :])
+
+    def apply(block, weights, span):
+        product = jnp.dot(v6_ref[span, :], weights, preferred_element_type=F32)
+        scaled = product[:, :width]
+        scaled_ref[block, span, :] = scaled
+        stop = min(span.stop, rows)
+        if span.start < stop:
+            s6_ref[span.start : stop, :] = right6(scaled[: stop - span.start], 1)
+        for later in range(block + 1, blocks):
+            at = (later - block) * width
+            v_ref[later, span, :] = v_ref[later, span, :] - product[:, at : at + width]
+
+    def store(block, target, span, value):
+        target[span, :] = value if block == 0 else target[span, :] + value
+
+    def gram(block, level):
+        low = level * width
+        pair = min(2, levels - level)
+        product = dot6_nt(v6_ref[low:, :], s6_ref[low : low + pair * width, :])
+        for index in range(pair):
+            value = product[index * width : count - low, index * width : (index + 1) * width]
+            offset = sum(count - done * width for done in range(level + index)) - width
+            if offset < 0:
+                store(block, key_ref, slice(0, width), value[:width])
+                value = value[width:]
+                offset = 0
+            store(block, rest_ref, slice(offset, offset + value.shape[0]), value)
+
     leaf_copies[0].wait()
-    part = sweep(leaf_ref[spans[0], spans[0]], 0, 2 * STEP)
-    for copy in leaf_copies[1:]:
-        copy.wait()
-    bases_copy.wait()
-    for block, span in enumerate(spans):
-        for level in range(1, levels + 1):
-            rank = ranks_ref[2 ** (levels - level) + lax.shift_right_logical(place, level) - 1]
-            piece = bases_ref[level - 1, span, :].T
-            v_ref[block, (level - 1) * width : level * width, :] = jnp.where(sub < rank, piece, 0.0)
-        v_ref[block, rows : rows + nrhs, :] = rhs_ref[:, span]
-    schur = {}
-    for first in range(blocks):
-        for second in range(first, blocks):
-            schur[first, second] = leaf_ref[spans[first], spans[second]]
+    tasks.append(arrive)
+    tasks += [functools.partial(load, 0, level) for level in range(1, levels + 1)]
+    tasks.append(load_rhs)
+    for block in range(1, blocks):
+        tasks += [functools.partial(load, block, level) for level in range(1, levels + 1)]
+    schur = {(0, 0): leaf_ref[spans[0], spans[0]]}
     for block in range(blocks):
+        run(width // STEP)
+        inv = inverse(schur[block, block], tick)
+        while tasks:
+            tasks.pop(0)()
         if block == 0:
-            inv = sweep(part, 2 * STEP, width)
-        else:
-            inv = inverse(schur[block, block])
-        values = v_ref[block]
-        upper = {}
-        for later in range(block + 1, blocks):
-            upper[later] = dot(inv, schur[block, later])
-            lower_ref[block, later - 1] = upper[later]
-        for first in range(block + 1, blocks):
-            for second in range(first, blocks):
-                product = lax.dot_general(
-                    schur[block, first],
-                    upper[second],
-                    (((0,), (0,)), ((), ())),
-                    precision=HIGHEST,
-                    preferred_element_type=F32,
-                )
-                schur[first, second] = schur[first, second] - product
-        scaled = dot(values, inv)
-        scaled_ref[block] = scaled
-        for later in range(block + 1, blocks):
-            v_ref[later] = v_ref[later] - dot(scaled, schur[block, later])
-        offset = 0
-        for level in range(1, levels + 1):
-            low = (level - 1) * width
-            product = dot_nt(values[low:], scaled[low : low + width])
-            pieces = [(rest_ref, product)]
-            if level == 1:
-                pieces = [(key_ref, product[:width]), (rest_ref, product[width:])]
-            for target, piece in pieces:
-                span = slice(0, width)
-                if target is rest_ref:
-                    span = slice(offset, offset + piece.shape[0])
-                    offset += piece.shape[0]
-                if block == 0:
-                    target[span, :] = piece
-                else:
-                    target[span, :] = target[span, :] + piece
+            for first in range(blocks):
+                for second in range(blocks):
+                    if first or second:
+                        schur[first, second] = leaf_ref[spans[first], spans[second]]
+        rest = range(block + 1, blocks)
+        weights = right6(inv, 0)
+        if rest:
+            right = jnp.concatenate([schur[block, later] for later in rest], axis=1)
+            upper = dot(inv, right)
+            split = right6(upper, 0)
+            for index, later in enumerate(rest):
+                lower_ref[block, later - 1] = upper[:, index * width : (index + 1) * width]
+
+            def reduce(first, block=block, rest=rest, split=split):
+                product = jnp.dot(left6(schur[first, block]), split, preferred_element_type=F32)
+                for index, later in enumerate(rest):
+                    at = slice(index * width, (index + 1) * width)
+                    schur[first, later] = schur[first, later] - product[:, at]
+
+            reduce(block + 1)
+            tasks += [functools.partial(reduce, first) for first in rest[1:]]
+            weights = jnp.concatenate([weights, split], axis=1)
+        if block:
+            tasks += [functools.partial(split_values, block, span) for span in chunks]
+        tasks += [functools.partial(apply, block, weights, span) for span in chunks]
+        tasks += [functools.partial(gram, block, level) for level in range(0, levels, 2)]
+    while tasks:
+        tasks.pop(0)()
 
 
 def pivot_kernel(first, last, *refs):
@@ -269,7 +389,7 @@
             value = value - dot(later, coef[low : low + width, :])
         known.append(value)
     rows = levels * width
-    result = weights_ref[rows:, :]
+    result = weights_ref[rows : rows + known[0].shape[0], :]
     for level in range(levels):
         result = result - dot(
             known[levels - 1 - level], weights_ref[level * width : (level + 1) * width, :]
@@ -332,6 +452,7 @@
     place = lax.axis_index("rowa") * lax.axis_size("rowb") + lax.axis_index("rowb")
     place = place.astype(jnp.int32).reshape(1)
     rows = levels * width + nrhs
+    padded = up(rows, 16)
     counts = [rows - level * width for level in range(levels)]
     spread = inner_bits >= 3 and levels >= 4
     plan = None
@@ -341,7 +462,12 @@
     middle = up(width // 2, STEP)
     key, rest, scaled, lower = call(
         functools.partial(leaf_kernel, levels, width, blocks),
-        [square, (sum(counts) - width, width), (blocks, rows, width), (blocks, max(blocks - 1, 1)) + square],
+        [
+            square,
+            (sum(counts) - width, width),
+            (blocks, padded, width),
+            (blocks, max(blocks - 1, 1)) + square,
+        ],
         ranks,
         place,
         right_side.T,
@@ -350,7 +476,9 @@
         smem=2,
         hbm=2,
         scratch=[
-            pltpu.VMEM((blocks, rows, width), F32),
+            pltpu.VMEM((blocks, padded, width), F32),
+            pltpu.VMEM((padded, 6 * width), BF16),
+            pltpu.VMEM((levels * width, 6 * width), BF16),
             pltpu.VMEM((leaf_rows, leaf_rows), F32),
             pltpu.VMEM((levels, leaf_rows, width), F32),
             pltpu.SemaphoreType.DMA((blocks + 1,)),
@@ -427,7 +555,7 @@
     last = jnp.concatenate([key, rest], axis=0)
     other_last = partner(last, levels - 1, inner_bits)
     (weights,) = call(
-        functools.partial(back_kernel, width, blocks), [(rows, leaf_rows)], scaled, lower
+        functools.partial(back_kernel, width, blocks), [(padded, leaf_rows)], scaled, lower
     )
     (result,) = call(
         functools.partial(final_kernel, levels, width),

time: 83.9 us -> 68.7 us (0.82)
  Pallas kernels: 50.6 us -> 33 us
  waiting for transfers between devices: 15.4 us -> 17.5 us
    pallas_call x18, Pallas kernels: 50.6 us -> 33 us  [call(): pl.pallas_call(kernel, out_shape=outs, in_specs=space, out_specs=[pl.Bloc...]
    ppermute x14, waiting for transfers between devices: 15.4 us -> 17.5 us  [flip(): return lax.ppermute(value, axis, pairs)]
  transfers between devices with their start and end apart: 14 -> 14, of which waited for: 9 -> 9; matrix products, arithmetic and copies ran while one was open for 0% -> 0% of each run, Pallas kernels for 23% -> 21%
where the time goes in v2:
time: 68.7 us; the launch traced here: 68.5 us
  Pallas kernels  33 us (48%)
  waiting for transfers between devices  17.5 us (25%)
  starting transfers between devices  14.8 us (22%)
  local copies, waits for them, and re-layouts  2.97 us (4%)
    pallas_call x18, Pallas kernels, call(): pl.pallas_call(kernel, out_shape=outs, in_specs=space, out_specs=[pl.Bloc...  33 us
    ppermute x14, waiting for transfers between devices, flip(): return lax.ppermute(value, axis, pairs)  17.5 us
    ppermute x14, starting transfers between devices, flip(): return lax.ppermute(value, axis, pairs)  14.8 us
    unnamed x8, local copies, waits for them, and re-layouts  2.97 us
  transfers between devices with their start and end apart: 14, of which 9 were waited for; matrix products, arithmetic and copies ran while one was open for 0% of the time, Pallas kernels for 21%

profile of v2, /device:TPU:0, one launch (start us, length us, event | category | flops | bytes accessed | tf_op | source)
XLA Modules:
  0.0 68.5 jit_solution(5134605145574845986)
XLA Ops:
  0.0 0.7 %copy-done.2 = f32[384,8]{0,1:T(8,128)S(1)} copy-done((f32[384,8]{0,1:T(8,128)S(1)}, f32[384,8]{0,1:T(8,128)}, u32[]{:S(2)}) %copy-start.2) | copy-done | bytes 12312
  0.7 1.2 %copy-done = f32[5,384,128]{2,1,0:T(8,128)S(1)} copy-done((f32[5,384,128]{2,1,0:T(8,128)S(1)}, f32[5,384,128]{2,1,0:T(8,128)}, u32[]{:S(2)}) %copy-start) | copy-done | bytes 983064
  1.9 1.1 %copy-done.1 = f32[384,384]{1,0:T(8,128)S(1)} copy-done((f32[384,384]{1,0:T(8,128)S(1)}, f32[384,384]{1,0:T(8,128)}, u32[]{:S(2)}) %copy-start.1) | copy-done | bytes 589848
  3.0 12.5 %shard_map.46 = (f32[128,128]{1,0:T(8,128)S(1)}, f32[1832,128]{1,0:T(8,128)S(1)}, f32[3,656,128]{2,1,0:T(8,128)S(1)}, f32[3,2,128,128]{3,2,1,0:T(8,128)S(1)}) custom-call(s32[31]{0:T(128)S(1)} %copy-done.3, s32[1]{0:T(128)} %bitcast.place_ref.refs_0_, f32[8,384]{1,0:T(8,128)S(1)} %bitcast.3, f32[384,384]{1,0:T(8,128)S(1)} %copy-done.1, ...), custom_call_target="tpu_custom_call" | custom-call | flops 2000000000 | bytes 6666666 | tf_op jit(solution)/shard_map/pallas_call | solution.py:406
  15.4 0.5 collective-permute-start
  16.0 0.1 collective-permute-start.1
  16.1 2.1 %collective-permute-done.1.refs_1_ = f32[128,128]{1,0:T(8,128)S(1)} collective-permute-done((f32[128,128]{1,0:T(8,128)S(1)}, f32[128,128]{1,0:T(8,128)S(1)}, u32[]{:S(2)}, u32[]{:S(2)}) %collective-permute-start.1) | collective-permute-done | bytes 65568 | tf_op jit(solution)/shard_map/ppermute | solution.py:419
  18.2 2.8 %shard_map.47.refs_2_ = f32[128,128]{1,0:T(8,128)S(1)} custom-call(f32[128,128]{1,0:T(8,128)S(1)} %get-tuple-element.31.refs_0_, f32[128,128]{1,0:T(8,128)S(1)} %collective-permute-done.1.refs_1_), custom_call_target="tpu_custom_call" | custom-call | flops 2000000000 | bytes 6666666 | tf_op jit(solution)/shard_map/pallas_call | solution.py:406
  21.0 0.0 collective-permute-done.refs_1_.refs_4_
  21.0 0.5 shard_map.48
  21.5 3.0 %collective-permute-start.2 = (f32[128,128]{1,0:T(8,128)S(1)}, f32[128,128]{1,0:T(8,128)S(1)}, u32[]{:S(2)}, u32[]{:S(2)}) collective-permute-start(f32[128,128]{1,0:T(8,128)S(1)} %get-tuple-element.35.refs_0_), channel_id=1, source_target_pairs={{0,2},{1,3},{2,0},{3,1},{4,6},{5,7},{6,4},{7,5},{8,10},{9,11},{10,... | collective-permute-start | bytes 196616 | tf_op jit(solution)/shard_map/ppermute | solution.py:419
  24.5 0.9 %shard_map.49 = (f32[1184,128]{1,0:T(8,128)S(1)}, f32[264,128]{1,0:T(8,128)S(1)}, f32[168,128]{1,0:T(8,128)S(1)}) custom-call(s32[1]{0:T(128)} %bitcast.place_ref.refs_0_, f32[648,128]{1,0:T(8,128)S(1)} %get-tuple-element.32.refs_1_, f32[520,128]{1,0:T(8,128)S(1)} %get-tuple-element.33.refs_2_.refs_0_, f32[1832,128]{1,0:T(8,128)S(1)} %get-tuple-element.30.refs_0_.refs_3_, ...), custom_call_target="tpu_custom_call" | custom-call | flops 2000000000 | bytes 6666666 | tf_op jit(solution)/shard_map/pallas_call | solution.py:406
  25.4 0.1 collective-permute-start.3
  25.5 1.4 %collective-permute-done.2.refs_1_ = f32[128,128]{1,0:T(8,128)S(1)} collective-permute-done((f32[128,128]{1,0:T(8,128)S(1)}, f32[128,128]{1,0:T(8,128)S(1)}, u32[]{:S(2)}, u32[]{:S(2)}) %collective-permute-start.2) | collective-permute-done | bytes 65568 | tf_op jit(solution)/shard_map/ppermute | solution.py:419
  26.9 2.4 %collective-permute-start.5 = (f32[168,128]{1,0:T(8,128)S(1)}, f32[168,128]{1,0:T(8,128)S(1)}, u32[]{:S(2)}, u32[]{:S(2)}) collective-permute-start(f32[168,128]{1,0:T(8,128)S(1)} %get-tuple-element.43), channel_id=1, source_target_pairs={{0,2},{1,3},{2,0},{3,1},{4,6},{5,7},{6,4},{7,5},{8,10},{9,11},{10,... | collective-permute-start | bytes 258056 | tf_op jit(solution)/shard_map/ppermute | solution.py:419
  29.3 1.4 %shard_map.50.refs_0_ = f32[128,128]{1,0:T(8,128)S(1)} custom-call(f32[128,128]{1,0:T(8,128)S(1)} %get-tuple-element.35.refs_0_, f32[128,128]{1,0:T(8,128)S(1)} %collective-permute-done.2.refs_1_), custom_call_target="tpu_custom_call" | custom-call | flops 2000000000 | bytes 6666666 | tf_op jit(solution)/shard_map/pallas_call | solution.py:406
  30.8 1.0 %collective-permute-done.3.refs_2_ = f32[264,128]{1,0:T(8,128)S(1)} collective-permute-done((f32[264,128]{1,0:T(8,128)S(1)}, f32[264,128]{1,0:T(8,128)S(1)}, u32[]{:S(2)}, u32[]{:S(2)}) %collective-permute-start.3) | collective-permute-done | bytes 135200 | tf_op jit(solution)/shard_map/ppermute | solution.py:419
  31.8 0.0 collective-permute-start.4
  31.8 1.4 %shard_map.51.refs_4_ = f32[128,128]{1,0:T(8,128)S(1)} custom-call(f32[128,128]{1,0:T(8,128)S(1)} %shard_map.50.refs_0_), custom_call_target="tpu_custom_call" | custom-call | flops 2000000000 | bytes 6666666 | tf_op jit(solution)/shard_map/pallas_call | solution.py:406
  33.2 0.0 collective-permute-done.4.refs_3_
  33.2 0.5 shard_map.52
  33.7 2.7 %collective-permute-start.6 = (f32[128,128]{1,0:T(8,128)S(1)}, f32[128,128]{1,0:T(8,128)S(1)}, u32[]{:S(2)}, u32[]{:S(2)}) collective-permute-start(f32[128,128]{1,0:T(8,128)S(1)} %get-tuple-element.44.refs_0_), channel_id=1, source_target_pairs={{0,4},{1,5},{2,6},{3,7},{4,0},{5,1},{6,2},{7,3},{8,12},{9,13},{10,... | collective-permute-start | bytes 196616 | tf_op jit(solution)/shard_map/ppermute | solution.py:419
  36.4 0.0 collective-permute-done.5.refs_4_
  36.4 0.5 shard_map.53.own_ref
  36.9 0.4 collective-permute-start.7
  37.3 3.3 %collective-permute-done.6.refs_1_ = f32[128,128]{1,0:T(8,128)S(1)} collective-permute-done((f32[128,128]{1,0:T(8,128)S(1)}, f32[128,128]{1,0:T(8,128)S(1)}, u32[]{:S(2)}, u32[]{:S(2)}) %collective-permute-start.6) | collective-permute-done | bytes 65568 | tf_op jit(solution)/shard_map/ppermute | solution.py:419
  40.6 1.4 %shard_map.54.refs_0_ = f32[128,128]{1,0:T(8,128)S(1)} custom-call(f32[128,128]{1,0:T(8,128)S(1)} %get-tuple-element.44.refs_0_, f32[128,128]{1,0:T(8,128)S(1)} %collective-permute-done.6.refs_1_), custom_call_target="tpu_custom_call" | custom-call | flops 2000000000 | bytes 6666666 | tf_op jit(solution)/shard_map/pallas_call | solution.py:406
  42.0 2.3 %collective-permute-done.7.other_ref = f32[168,128]{1,0:T(8,128)S(1)} collective-permute-done((f32[168,128]{1,0:T(8,128)S(1)}, f32[168,128]{1,0:T(8,128)S(1)}, u32[]{:S(2)}, u32[]{:S(2)}) %collective-permute-start.7) | collective-permute-done | bytes 86048 | tf_op jit(solution)/shard_map/ppermute | solution.py:419
  44.4 0.1 collective-permute-start.10
  44.4 1.5 %collective-permute-start.9 = (f32[168,128]{1,0:T(8,128)S(1)}, f32[168,128]{1,0:T(8,128)S(1)}, u32[]{:S(2)}, u32[]{:S(2)}) collective-permute-start(f32[168,128]{1,0:T(8,128)S(1)} %shard_map.55.refs_1_), channel_id=1, source_target_pairs={{0,2},{1,3},{2,0},{3,1},{4,6},{5,7},{6,4},{7,5},{8,10},{9,11},{10,... | collective-permute-start | bytes 258056 | tf_op jit(solution)/shard_map/ppermute | solution.py:419
  46.0 0.3 collective-permute-start.8
  46.3 1.4 %shard_map.56.refs_5_ = f32[128,128]{1,0:T(8,128)S(1)} custom-call(f32[128,128]{1,0:T(8,128)S(1)} %shard_map.54.refs_0_), custom_call_target="tpu_custom_call" | custom-call | flops 2000000000 | bytes 6666666 | tf_op jit(solution)/shard_map/pallas_call | solution.py:406
  47.7 1.4 %collective-permute-done.10.refs_4_ = f32[168,128]{1,0:T(8,128)S(1)} collective-permute-done((f32[168,128]{1,0:T(8,128)S(1)}, f32[168,128]{1,0:T(8,128)S(1)}, u32[]{:S(2)}, u32[]{:S(2)}) %collective-permute-start.10) | collective-permute-done | bytes 86048 | tf_op jit(solution)/shard_map/ppermute | solution.py:419
  49.2 2.0 %collective-permute-done.9.refs_3_ = f32[168,128]{1,0:T(8,128)S(1)} collective-permute-done((f32[168,128]{1,0:T(8,128)S(1)}, f32[168,128]{1,0:T(8,128)S(1)}, u32[]{:S(2)}, u32[]{:S(2)}) %collective-permute-start.9) | collective-permute-done | bytes 86048 | tf_op jit(solution)/shard_map/ppermute | solution.py:419
  51.1 0.0 collective-permute-done.8.refs_2_
  51.1 0.5 shard_map.57
  51.6 1.5 %collective-permute-start.12 = (f32[128,128]{1,0:T(8,128)S(1)}, f32[128,128]{1,0:T(8,128)S(1)}, u32[]{:S(2)}, u32[]{:S(2)}) collective-permute-start(f32[128,128]{1,0:T(8,128)S(1)} %get-tuple-element.49.refs_0_), channel_id=1, source_target_pairs={{0,8},{8,0},{16,24},{24,16},{1,9},{9,1},{17,25},{25,17},{2,10},{10... | collective-permute-start | bytes 196616 | tf_op jit(solution)/shard_map/ppermute | solution.py:419
  53.2 0.3 shard_map.58.refs_0_.refs_3_
  53.5 0.6 collective-permute-start.11
  54.1 2.1 %collective-permute-done.12.refs_1_ = f32[128,128]{1,0:T(8,128)S(1)} collective-permute-done((f32[128,128]{1,0:T(8,128)S(1)}, f32[128,128]{1,0:T(8,128)S(1)}, u32[]{:S(2)}, u32[]{:S(2)}) %collective-permute-start.12) | collective-permute-done | bytes 65568 | tf_op jit(solution)/shard_map/ppermute | solution.py:419
  56.1 2.8 %shard_map.59.refs_2_ = f32[128,128]{1,0:T(8,128)S(1)} custom-call(f32[128,128]{1,0:T(8,128)S(1)} %get-tuple-element.49.refs_0_, f32[128,128]{1,0:T(8,128)S(1)} %collective-permute-done.12.refs_1_), custom_call_target="tpu_custom_call" | custom-call | flops 2000000000 | bytes 6666666 | tf_op jit(solution)/shard_map/pallas_call | solution.py:406
  58.9 0.0 collective-permute-done.11.refs_1_.refs_4_
  58.9 0.4 shard_map.60
  59.3 0.1 shard_map.61
  59.5 1.6 %collective-permute-start.13 = (f32[136,128]{1,0:T(8,128)S(1)}, f32[136,128]{1,0:T(8,128)S(1)}, u32[]{:S(2)}, u32[]{:S(2)}) collective-permute-start(f32[136,128]{1,0:T(8,128)S(1)} %pad_maximum_fusion.own_ref), channel_id=1, source_target_pairs={{0,16},{8,24},{16,0},{24,8},{1,17},{9,25},{17,1},{25,9},{2,18},{10... | collective-permute-start | bytes 208904 | tf_op jit(solution)/shard_map/ppermute | solution.py:419
  61.1 1.0 %shard_map.62.weights_ref = f32[656,384]{1,0:T(8,128)S(1)} custom-call(f32[3,656,128]{2,1,0:T(8,128)S(1)} %get-tuple-element.53.scaled_ref, f32[3,2,128,128]{3,2,1,0:T(8,128)S(1)} %get-tuple-element.54.lower_ref), custom_call_target="tpu_custom_call" | custom-call | flops 2000000000 | bytes 6666666 | tf_op jit(solution)/shard_map/pallas_call | solution.py:406
  62.1 1.8 %collective-permute-done.13.other_ref = f32[136,128]{1,0:T(8,128)S(1)} collective-permute-done((f32[136,128]{1,0:T(8,128)S(1)}, f32[136,128]{1,0:T(8,128)S(1)}, u32[]{:S(2)}, u32[]{:S(2)}) %collective-permute-start.13) | collective-permute-done | bytes 69664 | tf_op jit(solution)/shard_map/ppermute | solution.py:419
  63.9 4.6 %shard_map.63 = f32[8,384]{1,0:T(8,128)} custom-call(f32[136,128]{1,0:T(8,128)S(1)} %pad_maximum_fusion.own_ref, f32[136,128]{1,0:T(8,128)S(1)} %collective-permute-done.13.other_ref, f32[656,384]{1,0:T(8,128)S(1)} %shard_map.62.weights_ref, f32[520,128]{1,0:T(8,128)S(1)} %get-tuple-element.33.refs_2_.refs_0_, ...), custom_call_target="tpu_custom_call" | custom-call | flops 2000000000 | bytes 6666666 | tf_op jit(solution)/shard_map/pallas_call | solution.py:406
  (7 shorter events, 0.1 us)
Async XLA Ops:
  0.0 0.7 %copy-start.2 = (f32[384,8]{0,1:T(8,128)S(1)}, f32[384,8]{0,1:T(8,128)}, u32[]{:S(2)}) copy-start(f32[384,8]{0,1:T(8,128)} %param.4) | copy-start | bytes 36868
  0.0 0.7 %copy-start.3 = (s32[31]{0:T(128)S(1)}, s32[31]{0:T(128)}, u32[]{:S(2)}) copy-start(s32[31]{0:T(128)} %ranks_ref.1) | copy-start | bytes 376
  0.7 1.2 %copy-start = (f32[5,384,128]{2,1,0:T(8,128)S(1)}, f32[5,384,128]{2,1,0:T(8,128)}, u32[]{:S(2)}) copy-start(f32[5,384,128]{2,1,0:T(8,128)} %bases_hbm.1) | copy-start | bytes 2949124
  1.9 1.1 %copy-start.1 = (f32[384,384]{1,0:T(8,128)S(1)}, f32[384,384]{1,0:T(8,128)}, u32[]{:S(2)}) copy-start(f32[384,384]{1,0:T(8,128)} %leaf_hbm.1) | copy-start | bytes 1769476
  15.4 5.5 %collective-permute-start = (f32[1832,128]{1,0:T(8,128)S(1)}, f32[1832,128]{1,0:T(8,128)S(1)}, u32[]{:S(2)}, u32[]{:S(2)}) collective-permute-start(f32[1832,128]{1,0:T(8,128)S(1)} %get-tuple-element.30.refs_0_.refs_3_), channel_id=1, source_target_pairs={{0,1},{1,0},{2,3},{3,2},{4,5},{5,4},{6,7},{7,6},{8,9},{9,8},{10,11... | collective-permute-start | bytes 2813960 | tf_op jit(solution)/shard_map/ppermute | solution.py:419
  16.0 2.2 %collective-permute-start.1 = (f32[128,128]{1,0:T(8,128)S(1)}, f32[128,128]{1,0:T(8,128)S(1)}, u32[]{:S(2)}, u32[]{:S(2)}) collective-permute-start(f32[128,128]{1,0:T(8,128)S(1)} %get-tuple-element.31.refs_0_), channel_id=1, source_target_pairs={{0,1},{1,0},{2,3},{3,2},{4,5},{5,4},{6,7},{7,6},{8,9},{9,8},{10,11... | collective-permute-start | bytes 196616 | tf_op jit(solution)/shard_map/ppermute | solution.py:419
  21.5 5.4 %collective-permute-start.2 = (f32[128,128]{1,0:T(8,128)S(1)}, f32[128,128]{1,0:T(8,128)S(1)}, u32[]{:S(2)}, u32[]{:S(2)}) collective-permute-start(f32[128,128]{1,0:T(8,128)S(1)} %get-tuple-element.35.refs_0_), channel_id=1, source_target_pairs={{0,2},{1,3},{2,0},{3,1},{4,6},{5,7},{6,4},{7,5},{8,10},{9,11},{10,... | collective-permute-start | bytes 196616 | tf_op jit(solution)/shard_map/ppermute | solution.py:419
  25.4 6.3 %collective-permute-start.3 = (f32[264,128]{1,0:T(8,128)S(1)}, f32[264,128]{1,0:T(8,128)S(1)}, u32[]{:S(2)}, u32[]{:S(2)}) collective-permute-start(f32[264,128]{1,0:T(8,128)S(1)} %get-tuple-element.38), channel_id=1, source_target_pairs={{0,2},{1,3},{2,0},{3,1},{4,6},{5,7},{6,4},{7,5},{8,10},{9,11},{10,... | collective-permute-start | bytes 405512 | tf_op jit(solution)/shard_map/ppermute | solution.py:419
  26.9 9.5 %collective-permute-start.5 = (f32[168,128]{1,0:T(8,128)S(1)}, f32[168,128]{1,0:T(8,128)S(1)}, u32[]{:S(2)}, u32[]{:S(2)}) collective-permute-start(f32[168,128]{1,0:T(8,128)S(1)} %get-tuple-element.43), channel_id=1, source_target_pairs={{0,2},{1,3},{2,0},{3,1},{4,6},{5,7},{6,4},{7,5},{8,10},{9,11},{10,... | collective-permute-start | bytes 258056 | tf_op jit(solution)/shard_map/ppermute | solution.py:419
  31.8 1.4 %collective-permute-start.4 = (f32[264,128]{1,0:T(8,128)S(1)}, f32[264,128]{1,0:T(8,128)S(1)}, u32[]{:S(2)}, u32[]{:S(2)}) collective-permute-start(f32[264,128]{1,0:T(8,128)S(1)} %collective-permute-done.3.refs_2_), channel_id=1, source_target_pairs={{0,1},{1,0},{2,3},{3,2},{4,5},{5,4},{6,7},{7,6},{8,9},{9,8},{10,11... | collective-permute-start | bytes 405512 | tf_op jit(solution)/shard_map/ppermute | solution.py:419
  33.7 6.9 %collective-permute-start.6 = (f32[128,128]{1,0:T(8,128)S(1)}, f32[128,128]{1,0:T(8,128)S(1)}, u32[]{:S(2)}, u32[]{:S(2)}) collective-permute-start(f32[128,128]{1,0:T(8,128)S(1)} %get-tuple-element.44.refs_0_), channel_id=1, source_target_pairs={{0,4},{1,5},{2,6},{3,7},{4,0},{5,1},{6,2},{7,3},{8,12},{9,13},{10,... | collective-permute-start | bytes 196616 | tf_op jit(solution)/shard_map/ppermute | solution.py:419
  36.9 7.5 %collective-permute-start.7 = (f32[168,128]{1,0:T(8,128)S(1)}, f32[168,128]{1,0:T(8,128)S(1)}, u32[]{:S(2)}, u32[]{:S(2)}) collective-permute-start(f32[168,128]{1,0:T(8,128)S(1)} %shard_map.53.own_ref), channel_id=1, source_target_pairs={{0,4},{1,5},{2,6},{3,7},{4,0},{5,1},{6,2},{7,3},{8,12},{9,13},{10,... | collective-permute-start | bytes 258056 | tf_op jit(solution)/shard_map/ppermute | solution.py:419
  44.4 4.8 %collective-permute-start.10 = (f32[168,128]{1,0:T(8,128)S(1)}, f32[168,128]{1,0:T(8,128)S(1)}, u32[]{:S(2)}, u32[]{:S(2)}) collective-permute-start(f32[168,128]{1,0:T(8,128)S(1)} %shard_map.55.refs_1_), channel_id=1, source_target_pairs={{0,3},{1,2},{2,1},{3,0},{4,7},{5,6},{6,5},{7,4},{8,11},{9,10},{10,... | collective-permute-start | bytes 258056 | tf_op jit(solution)/shard_map/ppermute | solution.py:419
  44.4 6.7 %collective-permute-start.9 = (f32[168,128]{1,0:T(8,128)S(1)}, f32[168,128]{1,0:T(8,128)S(1)}, u32[]{:S(2)}, u32[]{:S(2)}) collective-permute-start(f32[168,128]{1,0:T(8,128)S(1)} %shard_map.55.refs_1_), channel_id=1, source_target_pairs={{0,2},{1,3},{2,0},{3,1},{4,6},{5,7},{6,4},{7,5},{8,10},{9,11},{10,... | collective-permute-start | bytes 258056 | tf_op jit(solution)/shard_map/ppermute | solution.py:419
  46.0 5.1 %collective-permute-start.8 = (f32[168,128]{1,0:T(8,128)S(1)}, f32[168,128]{1,0:T(8,128)S(1)}, u32[]{:S(2)}, u32[]{:S(2)}) collective-permute-start(f32[168,128]{1,0:T(8,128)S(1)} %shard_map.55.refs_1_), channel_id=1, source_target_pairs={{0,1},{1,0},{2,3},{3,2},{4,5},{5,4},{6,7},{7,6},{8,9},{9,8},{10,11... | collective-permute-start | bytes 258056 | tf_op jit(solution)/shard_map/ppermute | solution.py:419
  51.6 4.5 %collective-permute-start.12 = (f32[128,128]{1,0:T(8,128)S(1)}, f32[128,128]{1,0:T(8,128)S(1)}, u32[]{:S(2)}, u32[]{:S(2)}) collective-permute-start(f32[128,128]{1,0:T(8,128)S(1)} %get-tuple-element.49.refs_0_), channel_id=1, source_target_pairs={{0,8},{8,0},{16,24},{24,16},{1,9},{9,1},{17,25},{25,17},{2,10},{10... | collective-permute-start | bytes 196616 | tf_op jit(solution)/shard_map/ppermute | solution.py:419
  53.5 5.5 %collective-permute-start.11 = (f32[272,128]{1,0:T(8,128)S(1)}, f32[272,128]{1,0:T(8,128)S(1)}, u32[]{:S(2)}, u32[]{:S(2)}) collective-permute-start(f32[272,128]{1,0:T(8,128)S(1)} %shard_map.58.refs_0_.refs_3_), channel_id=1, source_target_pairs={{0,8},{8,0},{16,24},{24,16},{1,9},{9,1},{17,25},{25,17},{2,10},{10... | collective-permute-start | bytes 417800 | tf_op jit(solution)/shard_map/ppermute | solution.py:419
  59.5 4.4 %collective-permute-start.13 = (f32[136,128]{1,0:T(8,128)S(1)}, f32[136,128]{1,0:T(8,128)S(1)}, u32[]{:S(2)}, u32[]{:S(2)}) collective-permute-start(f32[136,128]{1,0:T(8,128)S(1)} %pad_maximum_fusion.own_ref), channel_id=1, source_target_pairs={{0,16},{8,24},{16,0},{24,8},{1,17},{9,25},{17,1},{25,9},{2,18},{10... | collective-permute-start | bytes 208904 | tf_op jit(solution)/shard_map/ppermute | solution.py:419

commit v3 on v2

--- a/solution.py
+++ b/solution.py
@@ -11,6 +11,7 @@
 BF16 = jnp.bfloat16
 STEP = 16
 VMEM_LIMIT = 48 * 1024 * 1024
+LEAF_LIMIT = 48 * 1024 * 1024
 
 
 def split3(value):
@@ -152,8 +153,25 @@
     return matrix + jnp.where(row == column, 1.0, 0.0)
 
 
-def leaf_kernel(levels, width, blocks, ranks_ref, place_ref, rhs_ref, leaf_hbm, bases_hbm, *refs):
-    key_ref, rest_ref, scaled_ref, lower_ref, v_ref, v6_ref, s6_ref, leaf_ref, bases_ref, sem = refs
+def gram_pair(levels, width, count, level, v6_ref, s6_ref):
+    low = level * width
+    pair = min(2, levels - level)
+    product = dot6_nt(v6_ref[low:, :], s6_ref[low : low + pair * width, :])
+    result = []
+    for index in range(pair):
+        value = product[index * width : count - low, index * width : (index + 1) * width]
+        offset = sum(count - done * width for done in range(level + index)) - width
+        if offset < 0:
+            result.append((offset, value[:width]))
+            value = value[width:]
+            offset = 0
+        result.append((offset, value))
+    return result
+
+
+def leaf_kernel(levels, width, blocks, ranks_ref, place_ref, rhs_hbm, leaf_hbm, bases_hbm, *refs):
+    key_ref, rest_ref, scaled_ref, lower_ref, v6_ref, s6_ref, v_ref, *refs = refs
+    rhs_ref, leaf_ref, bases_ref, sem = refs
     nrhs = rhs_ref.shape[0]
     place = place_ref[0]
     rows = levels * width
@@ -164,10 +182,12 @@
         pltpu.make_async_copy(leaf_hbm.at[span], leaf_ref.at[span], sem.at[index])
         for index, span in enumerate(spans)
     ]
-    bases_copy = pltpu.make_async_copy(bases_hbm, bases_ref, sem.at[blocks])
-    for copy in leaf_copies:
+    other_copies = [
+        pltpu.make_async_copy(bases_hbm, bases_ref, sem.at[blocks]),
+        pltpu.make_async_copy(rhs_hbm, rhs_ref, sem.at[blocks + 1]),
+    ]
+    for copy in leaf_copies + other_copies:
         copy.start()
-    bases_copy.start()
 
     tasks = []
     quota = [0]
@@ -180,9 +200,8 @@
         quota[0] = -(-len(tasks) // steps)
 
     def arrive():
-        for copy in leaf_copies[1:]:
+        for copy in leaf_copies[1:] + other_copies:
             copy.wait()
-        bases_copy.wait()
 
     def load(block, level):
         sub = lax.broadcasted_iota(jnp.int32, (width, width), 0)
@@ -218,21 +237,11 @@
             at = (later - block) * width
             v_ref[later, span, :] = v_ref[later, span, :] - product[:, at : at + width]
 
-    def store(block, target, span, value):
-        target[span, :] = value if block == 0 else target[span, :] + value
-
     def gram(block, level):
-        low = level * width
-        pair = min(2, levels - level)
-        product = dot6_nt(v6_ref[low:, :], s6_ref[low : low + pair * width, :])
-        for index in range(pair):
-            value = product[index * width : count - low, index * width : (index + 1) * width]
-            offset = sum(count - done * width for done in range(level + index)) - width
-            if offset < 0:
-                store(block, key_ref, slice(0, width), value[:width])
-                value = value[width:]
-                offset = 0
-            store(block, rest_ref, slice(offset, offset + value.shape[0]), value)
+        for offset, value in gram_pair(levels, width, count, level, v6_ref, s6_ref):
+            target = key_ref if offset < 0 else rest_ref
+            span = slice(max(offset, 0), max(offset, 0) + value.shape[0])
+            target[span, :] = value if block == 0 else target[span, :] + value
 
     leaf_copies[0].wait()
     tasks.append(arrive)
@@ -272,9 +281,22 @@
         if block:
             tasks += [functools.partial(split_values, block, span) for span in chunks]
         tasks += [functools.partial(apply, block, weights, span) for span in chunks]
-        tasks += [functools.partial(gram, block, level) for level in range(0, levels, 2)]
+        if block < blocks - 1:
+            tasks += [functools.partial(gram, block, level) for level in range(0, levels, 2)]
     while tasks:
         tasks.pop(0)()
+    key = dot6_nt(v6_ref[:width, :], s6_ref[:width, :])
+    key_ref[...] = key_ref[...] + key if blocks > 1 else key
+    if blocks == 1:
+        rest_ref[...] = jnp.zeros_like(rest_ref)
+
+
+def gram_kernel(levels, width, count, part_ref, v6_ref, s6_ref, rest_ref):
+    for level in range(0, levels, 2):
+        for offset, value in gram_pair(levels, width, count, level, v6_ref, s6_ref):
+            if offset >= 0:
+                span = slice(offset, offset + value.shape[0])
+                rest_ref[span, :] = part_ref[span, :] + value
 
 
 def pivot_kernel(first, last, *refs):
@@ -289,8 +311,11 @@
     rest_ref, coef_ref, key_ref = refs[-3:]
     inv_ref = refs[-4]
     take(refs[:-4], rest_ref)
-    rest = rest_ref[:count]
-    coef_ref[...] = dot(rest, inv_ref[...])
+    coef_ref[...] = dot(rest_ref[:count], inv_ref[...])
+    next_key(width, count, rest_ref, coef_ref, key_ref)
+
+
+def next_key(width, count, rest_ref, coef_ref, key_ref):
     key_ref[...] = rest_ref[count : count + width] - dot_nt(coef_ref[:width], rest_ref[:width])
 
 
@@ -304,66 +329,110 @@
     place_ref, own_ref, near_ref, cross_ref = refs
     side = place_ref[0] & 1
     for index, source in ((side, near_ref), (side ^ 1, cross_ref)):
-        span = pl.ds(plan.half_at(index), plan.half)
+        span = pl.ds(plan.near2_at(index), plan.near2)
         rest_ref[span, :] = own_ref[span, :] + source[...]
 
 
 def take_quarters(plan, refs, rest_ref):
-    for index, source in enumerate(refs[1:]):
-        span = pl.ds(plan.quarter_at((refs[0][0] & 3) ^ index), plan.quarter)
-        rest_ref[span, :] = source[...]
-
-
-def rank_update(width, count, below, rest_ref, coef_ref, put):
+    place_ref, joined_ref, cross_ref = refs
+    for index in range(4):
+        source, at = (joined_ref, cross_ref)[index & 1], (index // 2) * plan.near3
+        span = pl.ds(plan.near3_at((place_ref[0] & 3) ^ index), plan.near3)
+        rest_ref[span, :] = source[at : at + plan.near3, :]
+
+
+def rank_update(width, count, below, first, last, rest_ref, coef_ref, put):
     offset = 0
     for level in range(below):
         low = level * width
         start = low + width if level == 0 else low
-        if start < count:
-            put(offset, dot_nt(coef_ref[start:, :], rest_ref[low : low + width, :]))
-        offset += count - start
-
-
-def far_update(plan, width, count, below, scatter, *refs):
-    place_ref, rest_ref, coef_ref, *more = refs
-    outs = more[-3:] if scatter else more[-1:]
-    pair = more[: -len(outs)]
+        size = count - start
+        begin, end = max(first - offset, 0), min(last - offset, size)
+        if begin < end:
+            product = dot_nt(coef_ref[start + begin : start + end, :], rest_ref[low : low + width, :])
+            put(offset + begin, product)
+        offset += size
+
+
+def far_update(width, count, below, own_ref, other_ref, rest_ref, coef_ref, out_ref):
     skip = count + width
 
     def put(offset, product):
         span = slice(skip + offset, skip + offset + product.shape[0])
-        if pair:
-            value = pair[0][span, :] + pair[1][span, :]
-        else:
-            value = rest_ref[span, :]
-        outs[0][offset : offset + product.shape[0], :] = value - product
-
-    rank_update(width, count, below, rest_ref, coef_ref, put)
-    if scatter:
-        place = place_ref[0]
-        outs[1][...] = outs[0][pl.ds(plan.half_at(place & 1), plan.half), :]
-        outs[2][...] = outs[0][
-            pl.ds(plan.near + plan.quarter_at((place & 3) ^ 2), plan.quarter), :
-        ]
+        out_ref[offset : offset + product.shape[0], :] = own_ref[span, :] + other_ref[span, :] - product
+
+    rank_update(width, count, below, 0, out_ref.shape[0], rest_ref, coef_ref, put)
+
+
+def part_update(plan, width, count, below, first, place_ref, *refs):
+    own_ref, other_ref, rest_ref, coef_ref, out_ref, send_ref = refs
+    skip = count + width
+    place = place_ref[0]
+
+    def put(offset, product):
+        span = slice(skip + offset, skip + offset + product.shape[0])
+        at = offset - first
+        out_ref[at : at + product.shape[0], :] = own_ref[span, :] + other_ref[span, :] - product
+
+    rank_update(width, count, below, first, first + out_ref.shape[0], rest_ref, coef_ref, put)
+    if first == 0:
+        send_ref[...] = out_ref[pl.ds(plan.near2_at(place & 1), plan.near2), :]
+    else:
+        send_ref[: plan.near3, :] = out_ref[pl.ds(plan.near3_at((place & 3) ^ 2), plan.near3), :]
+        send_ref[plan.near3 :, :] = out_ref[pl.ds(plan.rows3 + plan.far3_at(place & 1), plan.far3), :]
 
 
 def quarter_update(plan, width, count, below, *refs):
-    place_ref, rest_ref, coef_ref, own_ref, other_ref, out_ref, product_ref = refs
+    place_ref, own_ref, near_ref, cross_ref, far_own_ref, far_ref, inv_ref = refs[:7]
+    rest_ref, coef_ref, out_ref, product_ref = refs[7:]
+    take_halves(plan, (place_ref, own_ref, near_ref, cross_ref), rest_ref)
+    coef_ref[...] = dot(rest_ref[:count], inv_ref[...])
 
     def put(offset, product):
         product_ref[offset : offset + product.shape[0], :] = product
 
-    rank_update(width, count, below, rest_ref, coef_ref, put)
-    at = plan.quarter_at(place_ref[0] & 3)
+    rank_update(width, count, below, 0, plan.rows3, rest_ref, coef_ref, put)
+    span = pl.ds(plan.near3_at(place_ref[0] & 3), plan.near3)
+    out_ref[...] = far_own_ref[span, :] + far_ref[: plan.near3, :] - product_ref[span, :]
+
+
+def half_update(plan, width, count, below, *refs):
+    place_ref, rest_ref, coef_ref, own_ref, far_ref, out_ref, product_ref = refs
+
+    def put(offset, product):
+        at = offset - plan.rows3
+        product_ref[at : at + product.shape[0], :] = product
+
+    rank_update(width, count, below, plan.rows3, plan.far, rest_ref, coef_ref, put)
+    at = plan.far3_at(place_ref[0] & 1)
     out_ref[...] = (
-        own_ref[pl.ds(plan.near + at, plan.quarter), :]
-        + other_ref[...]
-        - product_ref[pl.ds(at, plan.quarter), :]
-    )
+        own_ref[pl.ds(plan.rows3 + at, plan.far3), :]
+        + far_ref[plan.near3 :, :]
+        - product_ref[pl.ds(at, plan.far3), :]
+    )
+
+
+def joined_update(plan, width, count, below, *refs):
+    place_ref, half_ref, cross_ref, rest_ref, coef_ref, out_ref, total_ref = refs
+    side = place_ref[0] & 1
+    for index, source in ((side, half_ref), (side ^ 1, cross_ref)):
+        total_ref[pl.ds(plan.far3_at(index), plan.far3), :] = source[...]
+
+    def put(offset, product):
+        span = slice(offset, offset + product.shape[0])
+        out_ref[span, :] = total_ref[span, :] - product
+
+    rank_update(width, count, below, 0, out_ref.shape[0], rest_ref, coef_ref, put)
 
 
 def add_kernel(own_ref, other_ref, out_ref):
     out_ref[...] = own_ref[...] + other_ref[...]
+
+
+def join_kernel(first_ref, second_ref, out_ref):
+    rows = first_ref.shape[0]
+    out_ref[:rows] = first_ref[...]
+    out_ref[rows:] = second_ref[...]
 
 
 def back_kernel(width, blocks, scaled_ref, lower_ref, out_ref):
@@ -376,40 +445,47 @@
         out_ref[:, block * width : (block + 1) * width] = value
 
 
-def final_kernel(levels, width, own_ref, other_ref, weights_ref, *refs):
+def fold_kernel(levels, width, nrhs, weights_ref, *refs):
     coef_refs, out_ref = refs[:-1], refs[-1]
-    inv = inverse(add_eye(own_ref[:width] + other_ref[:width]))
-    known = [dot(own_ref[width:] + other_ref[width:], inv)]
+    known = [None] * (levels - 1)
     for level in reversed(range(levels - 1)):
         coef = coef_refs[level]
-        count = (levels - 1 - level) * width
-        value = coef[count:, :]
-        for index, later in enumerate(known):
-            low = (len(known) - 1 - index) * width
-            value = value - dot(later, coef[low : low + width, :])
-        known.append(value)
-    rows = levels * width
-    result = weights_ref[rows : rows + known[0].shape[0], :]
-    for level in range(levels):
-        result = result - dot(
-            known[levels - 1 - level], weights_ref[level * width : (level + 1) * width, :]
-        )
-    out_ref[...] = result
-
-
-def call(kernel, shapes, *operands, flops=0, smem=0, hbm=0, scratch=()):
-    flops = flops or 2 * 10**9
+        value = coef[(levels - 2 - level) * width :, :]
+        above = range(level + 1, levels - 1)
+        if above:
+            value = value - dot(
+                jnp.concatenate([known[later] for later in above], axis=1),
+                coef[: len(above) * width, :],
+            )
+        known[level] = value
+    low = (levels - 1) * width
+    out_ref[...] = weights_ref[low : low + width + nrhs, :] - dot(
+        jnp.concatenate(known, axis=1), weights_ref[:low, :]
+    )
+
+
+def final_kernel(width, own_ref, other_ref, folded_ref, out_ref):
+    inv = inverse(add_eye(own_ref[:width] + other_ref[:width]))
+    coef = dot(own_ref[width:] + other_ref[width:], inv)
+    out_ref[...] = folded_ref[width:, :] - dot(coef, folded_ref[:width, :])
+
+
+def call(kernel, shapes, *operands, cost=1.5, smem=0, hbm=0, scratch=(), limit=VMEM_LIMIT):
+    flops = int(cost * 10**9)
     space = [pl.BlockSpec(memory_space=pltpu.SMEM)] * smem
     space += [pl.BlockSpec(memory_space=pltpu.VMEM)] * (len(operands) - smem - hbm)
     space += [pl.BlockSpec(memory_space=pltpu.HBM)] * hbm
-    outs = [jax.ShapeDtypeStruct(shape, F32) for shape in shapes]
+    outs = [
+        shape if isinstance(shape, jax.ShapeDtypeStruct) else jax.ShapeDtypeStruct(shape, F32)
+        for shape in shapes
+    ]
     return pl.pallas_call(
         kernel,
         out_shape=outs,
         in_specs=space,
         out_specs=[pl.BlockSpec(memory_space=pltpu.VMEM)] * len(outs),
         scratch_shapes=list(scratch),
-        compiler_params=pltpu.CompilerParams(vmem_limit_bytes=VMEM_LIMIT),
+        compiler_params=pltpu.CompilerParams(vmem_limit_bytes=limit),
         cost_estimate=pl.CostEstimate(flops=flops, bytes_accessed=flops // 300, transcendentals=0),
     )(*operands)
 
@@ -430,16 +506,20 @@
 
 
 class Plan:
-    def __init__(self, near, far):
-        self.near, self.far = near, far
-        self.half = up(near, 16) // 2
-        self.quarter = up(far, 32) // 4
-
-    def half_at(self, side):
-        return pl.multiple_of(side * (self.near - self.half), 8)
-
-    def quarter_at(self, index):
-        return pl.multiple_of(jnp.minimum(index * self.quarter, self.far - self.quarter), 8)
+    def __init__(self, near, rows3, last3):
+        self.near, self.rows3, self.last3, self.far = near, rows3, last3, rows3 + last3
+        self.near2 = up(near, 16) // 2
+        self.near3 = up(rows3, 32) // 4
+        self.far3 = up(last3, 16) // 2
+
+    def near2_at(self, side):
+        return pl.multiple_of(side * (self.near - self.near2), 8)
+
+    def near3_at(self, index):
+        return pl.multiple_of(jnp.minimum(index * self.near3, self.rows3 - self.near3), 8)
+
+    def far3_at(self, side):
+        return pl.multiple_of(side * (self.last3 - self.far3), 8)
 
 
 def body(right_side, leaves, bases, ranks):
@@ -457,113 +537,172 @@
     spread = inner_bits >= 3 and levels >= 4
     plan = None
     if spread:
-        plan = Plan(counts[1], sum(counts[2:]) - width)
+        plan = Plan(counts[1], counts[2], sum(counts[3:]) - width)
     square = (width, width)
     middle = up(width // 2, STEP)
-    key, rest, scaled, lower = call(
+    key, part, scaled, lower, values6, scaled6 = call(
         functools.partial(leaf_kernel, levels, width, blocks),
         [
             square,
             (sum(counts) - width, width),
             (blocks, padded, width),
             (blocks, max(blocks - 1, 1)) + square,
+            jax.ShapeDtypeStruct((padded, 6 * width), BF16),
+            jax.ShapeDtypeStruct((levels * width, 6 * width), BF16),
         ],
         ranks,
         place,
-        right_side.T,
-        leaves,
-        bases,
+        *[pltpu.with_memory_space_constraint(each, pltpu.HBM) for each in (right_side.T, leaves, bases)],
         smem=2,
-        hbm=2,
+        hbm=3,
+        limit=LEAF_LIMIT,
         scratch=[
             pltpu.VMEM((blocks, padded, width), F32),
-            pltpu.VMEM((padded, 6 * width), BF16),
-            pltpu.VMEM((levels * width, 6 * width), BF16),
+            pltpu.VMEM((nrhs, leaf_rows), F32),
             pltpu.VMEM((leaf_rows, leaf_rows), F32),
             pltpu.VMEM((levels, leaf_rows, width), F32),
-            pltpu.SemaphoreType.DMA((blocks + 1,)),
+            pltpu.SemaphoreType.DMA((blocks + 2,)),
         ],
     )
+    (rest,) = call(
+        functools.partial(gram_kernel, levels, width, rows),
+        [(sum(counts) - width, width)],
+        part,
+        values6,
+        scaled6,
+    )
+    (weights,) = call(
+        functools.partial(back_kernel, width, blocks), [(padded, leaf_rows)], scaled, lower
+    )
     coefs = []
-    mine = send = None
     for level in range(levels - 1):
         count = counts[level] - width
         below = levels - 1 - level
-        other_key = partner(key, level, inner_bits)
-        scatter = spread and level == 1
-        gather = spread and level == 2
-        if scatter:
+        following = sum(counts[level + 1 :]) - width
+        if spread and level == 1:
+            other_key = partner(key, level, inner_bits)
             near = partner(mine, level, inner_bits)
-            send, other_key = lax.optimization_barrier((send, other_key))
             far = partner(send, level, inner_bits)
-        elif gather:
-            other_quarter = partner(quarter, level, inner_bits)
-        else:
-            other_rest = partner(rest, level, inner_bits)
-        if scatter or gather:
             (half,) = call(functools.partial(pivot_kernel, 0, middle), [square], key, other_key)
-            if scatter:
-                half, near = lax.optimization_barrier((half, near))
-                take = functools.partial(take_halves, plan)
-                pieces = [place, rest, near, flip(near, 1)]
-            else:
-                half, other_quarter = lax.optimization_barrier((half, other_quarter))
-                (quarter,) = call(add_kernel, [quarter.shape], quarter, other_quarter)
-                take = functools.partial(take_quarters, plan)
-                pieces = [place, quarter] + [flip(quarter, mask) for mask in (1, 2, 3)]
+            half, near = lax.optimization_barrier((half, near))
+            cross = flip(near, 1)
             (inv,) = call(functools.partial(pivot_kernel, middle, width), [square], half)
-        else:
-            (inv,) = call(functools.partial(pivot_kernel, 0, width), [square], key, other_key)
-            take = take_full
-            pieces = [rest, other_rest]
-        total, coef, key = call(
-            functools.partial(near_update, width, count, take),
-            [(plan.far if gather else counts[level], width), (count, width), square],
-            *pieces,
-            inv,
-            smem=1 if scatter or gather else 0,
-        )
-        coefs.append(coef)
-        if scatter:
-            (quarter,) = call(
+            total, coef, quarter = call(
                 functools.partial(quarter_update, plan, width, count, below),
-                [(plan.quarter, width)],
+                [(plan.near, width), (count, width), (plan.near3, width)],
+                place,
+                rest_near,
+                near,
+                cross,
+                rest_far,
+                far,
+                inv,
+                smem=1,
+                scratch=[pltpu.VMEM((plan.rows3, width), F32)],
+            )
+            (key,) = call(functools.partial(next_key, width, count), [square], total, coef, cost=0.3)
+            (last_half,) = call(
+                functools.partial(half_update, plan, width, count, below),
+                [(plan.far3, width)],
                 place,
                 total,
                 coef,
-                rest,
+                rest_far,
                 far,
                 smem=1,
-                scratch=[pltpu.VMEM((plan.far, width), F32)],
+                scratch=[pltpu.VMEM((plan.last3, width), F32)],
             )
-            continue
-        next_scatter = spread and level == 0
-        shapes = [(sum(counts[level + 1 :]) - width, width)]
-        if next_scatter:
-            shapes += [(plan.half, width), (plan.quarter, width)]
-        rest, *sent = call(
-            functools.partial(far_update, plan, width, count, below, next_scatter),
-            shapes,
-            place,
-            total,
-            coef,
-            *([] if gather else [rest, other_rest]),
-            smem=1,
-        )
-        if next_scatter:
-            mine, send = sent
+        elif spread and level == 2:
+            other_quarter = partner(quarter, level, inner_bits)
+            other_key = partner(key, level, inner_bits)
+            other_half = partner(last_half, level, inner_bits)
+            quarter, weights = lax.optimization_barrier((quarter, weights))
+            (quarter,) = call(add_kernel, [quarter.shape], quarter, other_quarter, cost=0.1)
+            other_key, _ = lax.optimization_barrier((other_key, quarter))
+            opposite = flip(quarter, 2)
+            (half,) = call(functools.partial(pivot_kernel, 0, middle), [square], key, other_key)
+            half, opposite = lax.optimization_barrier((half, opposite))
+            (joined,) = call(join_kernel, [(2 * plan.near3, width)], quarter, opposite, cost=0.1)
+            joined_cross = flip(joined, 1)
+            (inv,) = call(functools.partial(pivot_kernel, middle, width), [square], half)
+            inv, other_half = lax.optimization_barrier((inv, other_half))
+            (last_half,) = call(add_kernel, [last_half.shape], last_half, other_half, cost=0.1)
+            cross = flip(last_half, 1)
+            total, coef, key = call(
+                functools.partial(
+                    near_update, width, count, functools.partial(take_quarters, plan)
+                ),
+                [(plan.rows3, width), (count, width), square],
+                place,
+                joined,
+                joined_cross,
+                inv,
+                smem=1,
+            )
+            (rest,) = call(
+                functools.partial(joined_update, plan, width, count, below),
+                [(following, width)],
+                place,
+                last_half,
+                cross,
+                total,
+                coef,
+                smem=1,
+                scratch=[pltpu.VMEM((plan.last3, width), F32)],
+            )
+        else:
+            other_key = partner(key, level, inner_bits)
+            sent_rest = rest
+            if level == 0:
+                sent_rest, other_key = lax.optimization_barrier((rest, other_key))
+            other_rest = partner(sent_rest, level, inner_bits)
+            (inv,) = call(functools.partial(pivot_kernel, 0, width), [square], key, other_key)
+            total, coef, key = call(
+                functools.partial(near_update, width, count, take_full),
+                [(counts[level], width), (count, width), square],
+                rest,
+                other_rest,
+                inv,
+            )
+            if spread and level == 0:
+                parts = []
+                for first, size, sent in (
+                    (0, plan.near, plan.near2),
+                    (plan.near, plan.far, plan.near3 + plan.far3),
+                ):
+                    parts += call(
+                        functools.partial(part_update, plan, width, count, below, first),
+                        [(size, width), (sent, width)],
+                        place,
+                        rest,
+                        other_rest,
+                        total,
+                        coef,
+                        cost=0.4,
+                        smem=1,
+                    )
+                    total, _ = lax.optimization_barrier((total, parts[-1]))
+                rest_near, mine, rest_far, send = parts
+            else:
+                (rest,) = call(
+                    functools.partial(far_update, width, count, below),
+                    [(following, width)],
+                    rest,
+                    other_rest,
+                    total,
+                    coef,
+                )
+        coefs.append(coef)
     last = jnp.concatenate([key, rest], axis=0)
     other_last = partner(last, levels - 1, inner_bits)
-    (weights,) = call(
-        functools.partial(back_kernel, width, blocks), [(padded, leaf_rows)], scaled, lower
-    )
-    (result,) = call(
-        functools.partial(final_kernel, levels, width),
-        [(nrhs, leaf_rows)],
-        last,
-        other_last,
+    (folded,) = call(
+        functools.partial(fold_kernel, levels, width, nrhs),
+        [(width + nrhs, leaf_rows)],
         weights,
         *coefs,
+    )
+    (result,) = call(
+        functools.partial(final_kernel, width), [(nrhs, leaf_rows)], last, other_last, folded
     )
     return result.T
 

time: 68.7 us -> 63.1 us (0.918)
  waiting for transfers between devices: 17.5 us -> 8.97 us
  starting transfers between devices: 14.8 us -> 18.5 us
  local copies, waits for them, and re-layouts: 2.97 us -> 0.65 us
  Pallas kernels: 33 us -> 34.6 us
    ppermute x14 -> x15, waiting for transfers between devices: 17.5 us -> 8.97 us  [flip(): return lax.ppermute(value, axis, pairs)]
    ppermute x14 -> x15, starting transfers between devices: 14.8 us -> 18.5 us  [flip(): return lax.ppermute(value, axis, pairs)]
    unnamed x8 -> x2, local copies, waits for them, and re-layouts: 2.97 us -> 0.65 us
    pallas_call x18 -> x24, Pallas kernels: 33 us -> 34.6 us  [call(): pl.pallas_call(kernel, out_shape=outs, in_specs=space, out_specs=[pl.Bloc...]
  transfers between devices with their start and end apart: 14 -> 15, of which waited for: 9 -> 8; matrix products, arithmetic and copies ran while one was open for 0% -> 0% of each run, Pallas kernels for 21% -> 26%
where the time goes in v3:
time: 63.1 us; the launch traced here: 62.9 us
  Pallas kernels  34.6 us (55%)
  starting transfers between devices  18.5 us (29%)
  waiting for transfers between devices  8.97 us (14%)
  local copies, waits for them, and re-layouts  0.65 us (1%)
    pallas_call x24, Pallas kernels, call(): pl.pallas_call(kernel, out_shape=outs, in_specs=space, out_specs=[pl.Bloc...  34.6 us
    ppermute x15, starting transfers between devices, flip(): return lax.ppermute(value, axis, pairs)  18.5 us
    ppermute x15, waiting for transfers between devices, flip(): return lax.ppermute(value, axis, pairs)  8.97 us
  transfers between devices with their start and end apart: 15, of which 8 were waited for; matrix products, arithmetic and copies ran while one was open for 0% of the time, Pallas kernels for 26%

profile of v3, /device:TPU:0, one launch (start us, length us, event | category | flops | bytes accessed | tf_op | source)
XLA Modules:
  0.0 62.9 jit_solution(6189145624833861168)
XLA Ops:
  0.0 0.7 %copy-done = s32[31]{0:T(128)S(1)} copy-done((s32[31]{0:T(128)S(1)}, s32[31]{0:T(128)}, u32[]{:S(2)}) %copy-start) | copy-done | bytes 148
  0.7 12.3 %shard_map.46 = (f32[128,128]{1,0:T(8,128)S(1)}, f32[1832,128]{1,0:T(8,128)S(1)}, f32[3,656,128]{2,1,0:T(8,128)S(1)}, f32[3,2,128,128]{3,2,1,0:T(8,128)S(1)}, bf...) custom-call(s32[31]{0:T(128)S(1)} %copy-done, s32[1]{0:T(128)} %bitcast.place_ref.refs_0_, f32[8,384]{1,0:T(8,128)} %bitcast.3, ...), custom_call_target="tpu_custom_call" | custom-call | flops 1500000000 | bytes 5000000 | tf_op jit(solution)/shard_map/pallas_call | solution.py:482
  13.0 0.5 collective-permute-start
  13.5 0.7 %shard_map.47.refs_0_ = f32[1832,128]{1,0:T(8,128)S(1)} custom-call(f32[1832,128]{1,0:T(8,128)S(1)} %get-tuple-element.39.part_ref, bf16[656,768]{1,0:T(8,128)(2,1)S(1)} %get-tuple-element.40.v6_ref, bf16[640,768]{1,0:T(8,128)(2,1)S(1)} %get-tuple-element.41.s6_ref), custom_call_target="tpu_custom_call" | custom-call | flops 1500000000 | bytes 5000000 | tf_op jit(solution)/shard_map/pallas_call | solution.py:482
  14.2 0.2 collective-permute-done.refs_1_
  14.4 0.4 collective-permute-start.1
  14.8 1.0 %shard_map.57.weights_ref = f32[656,384]{1,0:T(8,128)S(1)} custom-call(f32[3,656,128]{2,1,0:T(8,128)S(1)} %get-tuple-element.58.scaled_ref, f32[3,2,128,128]{3,2,1,0:T(8,128)S(1)} %get-tuple-element.59.lower_ref), custom_call_target="tpu_custom_call" | custom-call | flops 1500000000 | bytes 5000000 | tf_op jit(solution)/shard_map/pallas_call | solution.py:482
  15.7 3.0 %shard_map.48.refs_2_ = f32[128,128]{1,0:T(8,128)S(1)} custom-call(f32[128,128]{1,0:T(8,128)S(1)} %get-tuple-element.42.refs_0_, f32[128,128]{1,0:T(8,128)S(1)} %collective-permute-done.refs_1_), custom_call_target="tpu_custom_call" | custom-call | flops 1500000000 | bytes 5000000 | tf_op jit(solution)/shard_map/pallas_call | solution.py:482
  18.7 0.0 collective-permute-done.1.refs_1_
  18.7 0.5 shard_map.49
  19.3 2.8 %collective-permute-start.2 = (f32[128,128]{1,0:T(8,128)S(1)}, f32[128,128]{1,0:T(8,128)S(1)}, u32[]{:S(2)}, u32[]{:S(2)}) collective-permute-start(f32[128,128]{1,0:T(8,128)S(1)} %get-tuple-element.48.refs_0_), channel_id=1, source_target_pairs={{0,2},{1,3},{2,0},{3,1},{4,6},{5,7},{6,4},{7,5},{8,10},{9,11},{10,... | collective-permute-start | bytes 196616 | tf_op jit(solution)/shard_map/ppermute | solution.py:495
  22.1 0.4 shard_map.50
  22.5 0.1 collective-permute-start.3
  22.6 0.5 shard_map.52
  23.1 2.1 %collective-permute-start.5 = (f32[240,128]{1,0:T(8,128)S(1)}, f32[240,128]{1,0:T(8,128)S(1)}, u32[]{:S(2)}, u32[]{:S(2)}) collective-permute-start(f32[240,128]{1,0:T(8,128)S(1)} %get-tuple-element.53), channel_id=1, source_target_pairs={{0,2},{1,3},{2,0},{3,1},{4,6},{5,7},{6,4},{7,5},{8,10},{9,11},{10,... | collective-permute-start | bytes 368648 | tf_op jit(solution)/shard_map/ppermute | solution.py:495
  25.1 0.0 collective-permute-done.2.refs_1_
  25.1 1.4 %shard_map.51.refs_0_ = f32[128,128]{1,0:T(8,128)S(1)} custom-call(f32[128,128]{1,0:T(8,128)S(1)} %get-tuple-element.48.refs_0_, f32[128,128]{1,0:T(8,128)S(1)} %collective-permute-done.2.refs_1_), custom_call_target="tpu_custom_call" | custom-call | flops 1500000000 | bytes 5000000 | tf_op jit(solution)/shard_map/pallas_call | solution.py:482
  26.6 2.4 %collective-permute-done.3.refs_2_ = f32[264,128]{1,0:T(8,128)S(1)} collective-permute-done((f32[264,128]{1,0:T(8,128)S(1)}, f32[264,128]{1,0:T(8,128)S(1)}, u32[]{:S(2)}, u32[]{:S(2)}) %collective-permute-start.3) | collective-permute-done | bytes 135200 | tf_op jit(solution)/shard_map/ppermute | solution.py:495
  29.0 1.4 %shard_map.53.refs_6_ = f32[128,128]{1,0:T(8,128)S(1)} custom-call(f32[128,128]{1,0:T(8,128)S(1)} %shard_map.51.refs_0_), custom_call_target="tpu_custom_call" | custom-call | flops 1500000000 | bytes 5000000 | tf_op jit(solution)/shard_map/pallas_call | solution.py:482
  30.4 0.3 collective-permute-done.5.refs_5_.refs_4_
  30.7 0.0 collective-permute-done.4.refs_3_
  30.7 0.9 %shard_map.54 = (f32[520,128]{1,0:T(8,128)S(1)}, f32[392,128]{1,0:T(8,128)S(1)}, f32[104,128]{1,0:T(8,128)S(1)}) custom-call(s32[1]{0:T(128)} %bitcast.place_ref.refs_0_, f32[520,128]{1,0:T(8,128)S(1)} %get-tuple-element.47.refs_1_, f32[264,128]{1,0:T(8,128)S(1)} %collective-permute-done.3.refs_2_, f32[264,128]{1,0:T(8,128)S(1)} %collective-permute-done.4.refs_3_, ...), custom_call_target="tpu_custom_call" | custom-call | flops 1500000000 | bytes 5000000 | tf_op jit(solution)/shard_map/pallas_call | solution.py:482
  31.6 2.6 %collective-permute-start.7 = (f32[104,128]{1,0:T(8,128)S(1)}, f32[104,128]{1,0:T(8,128)S(1)}, u32[]{:S(2)}, u32[]{:S(2)}) collective-permute-start(f32[104,128]{1,0:T(8,128)S(1)} %get-tuple-element.60.own_ref), channel_id=1, source_target_pairs={{0,4},{1,5},{2,6},{3,7},{4,0},{5,1},{6,2},{7,3},{8,12},{9,13},{10,... | collective-permute-start | bytes 159752 | tf_op jit(solution)/shard_map/ppermute | solution.py:495
  34.2 0.2 shard_map.56.refs_0_
  34.5 0.4 collective-permute-start.6
  34.9 0.3 shard_map.55.own_ref
  35.2 2.7 %collective-permute-start.9 = (f32[136,128]{1,0:T(8,128)S(1)}, f32[136,128]{1,0:T(8,128)S(1)}, u32[]{:S(2)}, u32[]{:S(2)}) collective-permute-start(f32[136,128]{1,0:T(8,128)S(1)} %shard_map.55.own_ref), channel_id=1, source_target_pairs={{0,4},{1,5},{2,6},{3,7},{4,0},{5,1},{6,2},{7,3},{8,12},{9,13},{10,... | collective-permute-start | bytes 208904 | tf_op jit(solution)/shard_map/ppermute | solution.py:495
  37.9 2.6 %collective-permute-start.8 = (f32[104,128]{1,0:T(8,128)S(1)}, f32[104,128]{1,0:T(8,128)S(1)}, u32[]{:S(2)}, u32[]{:S(2)}) collective-permute-start(f32[104,128]{1,0:T(8,128)S(1)} %shard_map.58.first_ref), channel_id=1, source_target_pairs={{0,2},{1,3},{2,0},{3,1},{4,6},{5,7},{6,4},{7,5},{8,10},{9,11},{10,... | collective-permute-start | bytes 159752 | tf_op jit(solution)/shard_map/ppermute | solution.py:495
  40.4 2.3 %collective-permute-done.6.refs_1_ = f32[128,128]{1,0:T(8,128)S(1)} collective-permute-done((f32[128,128]{1,0:T(8,128)S(1)}, f32[128,128]{1,0:T(8,128)S(1)}, u32[]{:S(2)}, u32[]{:S(2)}) %collective-permute-start.6) | collective-permute-done | bytes 65568 | tf_op jit(solution)/shard_map/ppermute | solution.py:495
  42.8 1.4 %shard_map.59.refs_0_ = f32[128,128]{1,0:T(8,128)S(1)} custom-call(f32[128,128]{1,0:T(8,128)S(1)} %shard_map.56.refs_0_, f32[128,128]{1,0:T(8,128)S(1)} %collective-permute-done.6.refs_1_), custom_call_target="tpu_custom_call" | custom-call | flops 1500000000 | bytes 5000000 | tf_op jit(solution)/shard_map/pallas_call | solution.py:482
  44.2 0.1 collective-permute-done.8.second_ref
  44.3 0.1 collective-permute-start.11
  44.4 1.4 %shard_map.60.refs_3_ = f32[128,128]{1,0:T(8,128)S(1)} custom-call(f32[128,128]{1,0:T(8,128)S(1)} %shard_map.59.refs_0_), custom_call_target="tpu_custom_call" | custom-call | flops 1500000000 | bytes 5000000 | tf_op jit(solution)/shard_map/pallas_call | solution.py:482
  45.9 0.6 collective-permute-start.10
  46.4 0.0 collective-permute-done.11.refs_2_
  46.4 0.5 shard_map.63
  47.0 1.6 %collective-permute-start.13 = (f32[128,128]{1,0:T(8,128)S(1)}, f32[128,128]{1,0:T(8,128)S(1)}, u32[]{:S(2)}, u32[]{:S(2)}) collective-permute-start(f32[128,128]{1,0:T(8,128)S(1)} %get-tuple-element.68.refs_0_), channel_id=1, source_target_pairs={{0,8},{8,0},{16,24},{24,16},{1,9},{9,1},{17,25},{25,17},{2,10},{10... | collective-permute-start | bytes 196616 | tf_op jit(solution)/shard_map/ppermute | solution.py:495
  48.5 0.3 shard_map.64.refs_0_.own_ref
  48.8 0.6 collective-permute-start.12
  49.4 2.0 %collective-permute-done.13.refs_1_ = f32[128,128]{1,0:T(8,128)S(1)} collective-permute-done((f32[128,128]{1,0:T(8,128)S(1)}, f32[128,128]{1,0:T(8,128)S(1)}, u32[]{:S(2)}, u32[]{:S(2)}) %collective-permute-start.13) | collective-permute-done | bytes 65568 | tf_op jit(solution)/shard_map/ppermute | solution.py:495
  51.4 2.8 %shard_map.65.refs_2_ = f32[128,128]{1,0:T(8,128)S(1)} custom-call(f32[128,128]{1,0:T(8,128)S(1)} %get-tuple-element.68.refs_0_, f32[128,128]{1,0:T(8,128)S(1)} %collective-permute-done.13.refs_1_), custom_call_target="tpu_custom_call" | custom-call | flops 1500000000 | bytes 5000000 | tf_op jit(solution)/shard_map/pallas_call | solution.py:482
  54.2 0.1 collective-permute-done.12.refs_1_.other_ref
  54.3 0.4 shard_map.66
  54.7 0.1 shard_map.67
  54.9 1.6 %collective-permute-start.14 = (f32[136,128]{1,0:T(8,128)S(1)}, f32[136,128]{1,0:T(8,128)S(1)}, u32[]{:S(2)}, u32[]{:S(2)}) collective-permute-start(f32[136,128]{1,0:T(8,128)S(1)} %pad_maximum_fusion.own_ref), channel_id=1, source_target_pairs={{0,16},{8,24},{16,0},{24,8},{1,17},{9,25},{17,1},{25,9},{2,18},{10... | collective-permute-start | bytes 208904 | tf_op jit(solution)/shard_map/ppermute | solution.py:495
  56.5 1.3 %shard_map.68.folded_ref = f32[136,384]{1,0:T(8,128)S(1)} custom-call(f32[656,384]{1,0:T(8,128)S(1)} %shard_map.57.weights_ref, f32[520,128]{1,0:T(8,128)S(1)} %get-tuple-element.46.refs_3_.refs_0_, f32[392,128]{1,0:T(8,128)S(1)} %get-tuple-element.56.refs_2_.coef_ref.refs_1_, f32[264,128]{1,0:T(8,128)S(1)} %get-tuple-element.67.refs_4_.refs_2_, ...), custom_call_target="tpu_custom_call" | custom-call | flops 1500000000 | bytes 5000000 | tf_op jit(solution)/shard_map/pallas_call | solution.py:482
  57.8 1.5 %collective-permute-done.14.other_ref = f32[136,128]{1,0:T(8,128)S(1)} collective-permute-done((f32[136,128]{1,0:T(8,128)S(1)}, f32[136,128]{1,0:T(8,128)S(1)}, u32[]{:S(2)}, u32[]{:S(2)}) %collective-permute-start.14) | collective-permute-done | bytes 69664 | tf_op jit(solution)/shard_map/ppermute | solution.py:495
  59.2 3.7 %shard_map.69 = f32[8,384]{1,0:T(8,128)} custom-call(f32[136,128]{1,0:T(8,128)S(1)} %pad_maximum_fusion.own_ref, f32[136,128]{1,0:T(8,128)S(1)} %collective-permute-done.14.other_ref, f32[136,384]{1,0:T(8,128)S(1)} %shard_map.68.folded_ref), custom_call_target="tpu_custom_call" | custom-call | flops 1500000000 | bytes 5000000 | tf_op jit(solution)/shard_map/pallas_call | solution.py:482
  (9 shorter events, 0.1 us)
Async XLA Ops:
  0.0 0.7 %copy-start = (s32[31]{0:T(128)S(1)}, s32[31]{0:T(128)}, u32[]{:S(2)}) copy-start(s32[31]{0:T(128)} %ranks_ref.1) | copy-start | bytes 376
  13.0 1.4 %collective-permute-start = (f32[128,128]{1,0:T(8,128)S(1)}, f32[128,128]{1,0:T(8,128)S(1)}, u32[]{:S(2)}, u32[]{:S(2)}) collective-permute-start(f32[128,128]{1,0:T(8,128)S(1)} %get-tuple-element.42.refs_0_), channel_id=1, source_target_pairs={{0,1},{1,0},{2,3},{3,2},{4,5},{5,4},{6,7},{7,6},{8,9},{9,8},{10,11... | collective-permute-start | bytes 196616 | tf_op jit(solution)/shard_map/ppermute | solution.py:495
  14.4 4.3 %collective-permute-start.1 = (f32[1832,128]{1,0:T(8,128)S(1)}, f32[1832,128]{1,0:T(8,128)S(1)}, u32[]{:S(2)}, u32[]{:S(2)}) collective-permute-start(f32[1832,128]{1,0:T(8,128)S(1)} %shard_map.47.refs_0_), channel_id=1, source_target_pairs={{0,1},{1,0},{2,3},{3,2},{4,5},{5,4},{6,7},{7,6},{8,9},{9,8},{10,11... | collective-permute-start | bytes 2813960 | tf_op jit(solution)/shard_map/ppermute | solution.py:495
  19.3 5.9 %collective-permute-start.2 = (f32[128,128]{1,0:T(8,128)S(1)}, f32[128,128]{1,0:T(8,128)S(1)}, u32[]{:S(2)}, u32[]{:S(2)}) collective-permute-start(f32[128,128]{1,0:T(8,128)S(1)} %get-tuple-element.48.refs_0_), channel_id=1, source_target_pairs={{0,2},{1,3},{2,0},{3,1},{4,6},{5,7},{6,4},{7,5},{8,10},{9,11},{10,... | collective-permute-start | bytes 196616 | tf_op jit(solution)/shard_map/ppermute | solution.py:495
  22.5 6.5 %collective-permute-start.3 = (f32[264,128]{1,0:T(8,128)S(1)}, f32[264,128]{1,0:T(8,128)S(1)}, u32[]{:S(2)}, u32[]{:S(2)}) collective-permute-start(f32[264,128]{1,0:T(8,128)S(1)} %get-tuple-element.49), channel_id=1, source_target_pairs={{0,2},{1,3},{2,0},{3,1},{4,6},{5,7},{6,4},{7,5},{8,10},{9,11},{10,... | collective-permute-start | bytes 405512 | tf_op jit(solution)/shard_map/ppermute | solution.py:495
  23.1 7.7 %collective-permute-start.5 = (f32[240,128]{1,0:T(8,128)S(1)}, f32[240,128]{1,0:T(8,128)S(1)}, u32[]{:S(2)}, u32[]{:S(2)}) collective-permute-start(f32[240,128]{1,0:T(8,128)S(1)} %get-tuple-element.53), channel_id=1, source_target_pairs={{0,2},{1,3},{2,0},{3,1},{4,6},{5,7},{6,4},{7,5},{8,10},{9,11},{10,... | collective-permute-start | bytes 368648 | tf_op jit(solution)/shard_map/ppermute | solution.py:495
  29.0 1.8 %collective-permute-start.4 = (f32[264,128]{1,0:T(8,128)S(1)}, f32[264,128]{1,0:T(8,128)S(1)}, u32[]{:S(2)}, u32[]{:S(2)}) collective-permute-start(f32[264,128]{1,0:T(8,128)S(1)} %collective-permute-done.3.refs_2_), channel_id=1, source_target_pairs={{0,1},{1,0},{2,3},{3,2},{4,5},{5,4},{6,7},{7,6},{8,9},{9,8},{10,11... | collective-permute-start | bytes 405512 | tf_op jit(solution)/shard_map/ppermute | solution.py:495
  31.6 6.2 %collective-permute-start.7 = (f32[104,128]{1,0:T(8,128)S(1)}, f32[104,128]{1,0:T(8,128)S(1)}, u32[]{:S(2)}, u32[]{:S(2)}) collective-permute-start(f32[104,128]{1,0:T(8,128)S(1)} %get-tuple-element.60.own_ref), channel_id=1, source_target_pairs={{0,4},{1,5},{2,6},{3,7},{4,0},{5,1},{6,2},{7,3},{8,12},{9,13},{10,... | collective-permute-start | bytes 159752 | tf_op jit(solution)/shard_map/ppermute | solution.py:495
  34.5 8.3 %collective-permute-start.6 = (f32[128,128]{1,0:T(8,128)S(1)}, f32[128,128]{1,0:T(8,128)S(1)}, u32[]{:S(2)}, u32[]{:S(2)}) collective-permute-start(f32[128,128]{1,0:T(8,128)S(1)} %shard_map.56.refs_0_), channel_id=1, source_target_pairs={{0,4},{1,5},{2,6},{3,7},{4,0},{5,1},{6,2},{7,3},{8,12},{9,13},{10,... | collective-permute-start | bytes 196616 | tf_op jit(solution)/shard_map/ppermute | solution.py:495
  35.2 10.7 %collective-permute-start.9 = (f32[136,128]{1,0:T(8,128)S(1)}, f32[136,128]{1,0:T(8,128)S(1)}, u32[]{:S(2)}, u32[]{:S(2)}) collective-permute-start(f32[136,128]{1,0:T(8,128)S(1)} %shard_map.55.own_ref), channel_id=1, source_target_pairs={{0,4},{1,5},{2,6},{3,7},{4,0},{5,1},{6,2},{7,3},{8,12},{9,13},{10,... | collective-permute-start | bytes 208904 | tf_op jit(solution)/shard_map/ppermute | solution.py:495
  37.9 6.5 %collective-permute-start.8 = (f32[104,128]{1,0:T(8,128)S(1)}, f32[104,128]{1,0:T(8,128)S(1)}, u32[]{:S(2)}, u32[]{:S(2)}) collective-permute-start(f32[104,128]{1,0:T(8,128)S(1)} %shard_map.58.first_ref), channel_id=1, source_target_pairs={{0,2},{1,3},{2,0},{3,1},{4,6},{5,7},{6,4},{7,5},{8,10},{9,11},{10,... | collective-permute-start | bytes 159752 | tf_op jit(solution)/shard_map/ppermute | solution.py:495
  44.3 2.1 %collective-permute-start.11 = (f32[208,128]{1,0:T(8,128)S(1)}, f32[208,128]{1,0:T(8,128)S(1)}, u32[]{:S(2)}, u32[]{:S(2)}) collective-permute-start(f32[208,128]{1,0:T(8,128)S(1)} %shard_map.62.refs_1_), channel_id=1, source_target_pairs={{0,1},{1,0},{2,3},{3,2},{4,5},{5,4},{6,7},{7,6},{8,9},{9,8},{10,11... | collective-permute-start | bytes 319496 | tf_op jit(solution)/shard_map/ppermute | solution.py:495
  45.9 2.6 %collective-permute-start.10 = (f32[136,128]{1,0:T(8,128)S(1)}, f32[136,128]{1,0:T(8,128)S(1)}, u32[]{:S(2)}, u32[]{:S(2)}) collective-permute-start(f32[136,128]{1,0:T(8,128)S(1)} %shard_map.61.refs_1_), channel_id=1, source_target_pairs={{0,1},{1,0},{2,3},{3,2},{4,5},{5,4},{6,7},{7,6},{8,9},{9,8},{10,11... | collective-permute-start | bytes 208904 | tf_op jit(solution)/shard_map/ppermute | solution.py:495
  47.0 4.5 %collective-permute-start.13 = (f32[128,128]{1,0:T(8,128)S(1)}, f32[128,128]{1,0:T(8,128)S(1)}, u32[]{:S(2)}, u32[]{:S(2)}) collective-permute-start(f32[128,128]{1,0:T(8,128)S(1)} %get-tuple-element.68.refs_0_), channel_id=1, source_target_pairs={{0,8},{8,0},{16,24},{24,16},{1,9},{9,1},{17,25},{25,17},{2,10},{10... | collective-permute-start | bytes 196616 | tf_op jit(solution)/shard_map/ppermute | solution.py:495
  48.8 5.5 %collective-permute-start.12 = (f32[272,128]{1,0:T(8,128)S(1)}, f32[272,128]{1,0:T(8,128)S(1)}, u32[]{:S(2)}, u32[]{:S(2)}) collective-permute-start(f32[272,128]{1,0:T(8,128)S(1)} %shard_map.64.refs_0_.own_ref), channel_id=1, source_target_pairs={{0,8},{8,0},{16,24},{24,16},{1,9},{9,1},{17,25},{25,17},{2,10},{10... | collective-permute-start | bytes 417800 | tf_op jit(solution)/shard_map/ppermute | solution.py:495
  54.9 4.4 %collective-permute-start.14 = (f32[136,128]{1,0:T(8,128)S(1)}, f32[136,128]{1,0:T(8,128)S(1)}, u32[]{:S(2)}, u32[]{:S(2)}) collective-permute-start(f32[136,128]{1,0:T(8,128)S(1)} %pad_maximum_fusion.own_ref), channel_id=1, source_target_pairs={{0,16},{8,24},{16,0},{24,8},{1,17},{9,25},{17,1},{25,9},{2,18},{10... | collective-permute-start | bytes 208904 | tf_op jit(solution)/shard_map/ppermute | solution.py:495

commit v4 on v3

--- a/solution.py
+++ b/solution.py
@@ -169,9 +169,9 @@
     return result
 
 
-def leaf_kernel(levels, width, blocks, ranks_ref, place_ref, rhs_hbm, leaf_hbm, bases_hbm, *refs):
+def leaf_kernel(levels, width, blocks, place_ref, ranks_hbm, rhs_hbm, leaf_hbm, bases_hbm, *refs):
     key_ref, rest_ref, scaled_ref, lower_ref, v6_ref, s6_ref, v_ref, *refs = refs
-    rhs_ref, leaf_ref, bases_ref, sem = refs
+    ranks_ref, rhs_ref, leaf_ref, bases_ref, sem = refs
     nrhs = rhs_ref.shape[0]
     place = place_ref[0]
     rows = levels * width
@@ -185,6 +185,7 @@
     other_copies = [
         pltpu.make_async_copy(bases_hbm, bases_ref, sem.at[blocks]),
         pltpu.make_async_copy(rhs_hbm, rhs_ref, sem.at[blocks + 1]),
+        pltpu.make_async_copy(ranks_hbm, ranks_ref, sem.at[blocks + 2]),
     ]
     for copy in leaf_copies + other_copies:
         copy.start()
@@ -315,6 +316,13 @@
     next_key(width, count, rest_ref, coef_ref, key_ref)
 
 
+def last_update(width, count, own_ref, other_ref, inv_ref, coef_ref, last_ref):
+    rest = own_ref[:count] + other_ref[:count]
+    coef_ref[...] = dot(rest, inv_ref[...])
+    total = own_ref[count:] + other_ref[count:]
+    last_ref[...] = total - dot_nt(coef_ref[...], rest[:width])
+
+
 def next_key(width, count, rest_ref, coef_ref, key_ref):
     key_ref[...] = rest_ref[count : count + width] - dot_nt(coef_ref[:width], rest_ref[:width])
 
@@ -365,7 +373,7 @@
 
 
 def part_update(plan, width, count, below, first, place_ref, *refs):
-    own_ref, other_ref, rest_ref, coef_ref, out_ref, send_ref = refs
+    own_ref, other_ref, rest_ref, coef_ref, out_ref, *send_refs = refs
     skip = count + width
     place = place_ref[0]
 
@@ -376,10 +384,10 @@
 
     rank_update(width, count, below, first, first + out_ref.shape[0], rest_ref, coef_ref, put)
     if first == 0:
-        send_ref[...] = out_ref[pl.ds(plan.near2_at(place & 1), plan.near2), :]
+        send_refs[0][...] = out_ref[pl.ds(plan.near2_at(place & 1), plan.near2), :]
     else:
-        send_ref[: plan.near3, :] = out_ref[pl.ds(plan.near3_at((place & 3) ^ 2), plan.near3), :]
-        send_ref[plan.near3 :, :] = out_ref[pl.ds(plan.rows3 + plan.far3_at(place & 1), plan.far3), :]
+        send_refs[0][...] = out_ref[pl.ds(plan.near3_at((place & 3) ^ 2), plan.near3), :]
+        send_refs[1][...] = out_ref[pl.ds(plan.rows3 + plan.far3_at(place & 1), plan.far3), :]
 
 
 def quarter_update(plan, width, count, below, *refs):
@@ -393,7 +401,7 @@
 
     rank_update(width, count, below, 0, plan.rows3, rest_ref, coef_ref, put)
     span = pl.ds(plan.near3_at(place_ref[0] & 3), plan.near3)
-    out_ref[...] = far_own_ref[span, :] + far_ref[: plan.near3, :] - product_ref[span, :]
+    out_ref[...] = far_own_ref[span, :] + far_ref[...] - product_ref[span, :]
 
 
 def half_update(plan, width, count, below, *refs):
@@ -407,7 +415,7 @@
     at = plan.far3_at(place_ref[0] & 1)
     out_ref[...] = (
         own_ref[pl.ds(plan.rows3 + at, plan.far3), :]
-        + far_ref[plan.near3 :, :]
+        + far_ref[...]
         - product_ref[pl.ds(at, plan.far3), :]
     )
 
@@ -550,18 +558,21 @@
             jax.ShapeDtypeStruct((padded, 6 * width), BF16),
             jax.ShapeDtypeStruct((levels * width, 6 * width), BF16),
         ],
-        ranks,
         place,
-        *[pltpu.with_memory_space_constraint(each, pltpu.HBM) for each in (right_side.T, leaves, bases)],
-        smem=2,
-        hbm=3,
+        *[
+            pltpu.with_memory_space_constraint(each, pltpu.HBM)
+            for each in (ranks, right_side.T, leaves, bases)
+        ],
+        smem=1,
+        hbm=4,
         limit=LEAF_LIMIT,
         scratch=[
             pltpu.VMEM((blocks, padded, width), F32),
+            pltpu.SMEM(ranks.shape, jnp.int32),
             pltpu.VMEM((nrhs, leaf_rows), F32),
             pltpu.VMEM((leaf_rows, leaf_rows), F32),
             pltpu.VMEM((levels, leaf_rows, width), F32),
-            pltpu.SemaphoreType.DMA((blocks + 2,)),
+            pltpu.SemaphoreType.DMA((blocks + 3,)),
         ],
     )
     (rest,) = call(
@@ -571,9 +582,10 @@
         values6,
         scaled6,
     )
-    (weights,) = call(
-        functools.partial(back_kernel, width, blocks), [(padded, leaf_rows)], scaled, lower
-    )
+    if not spread:
+        (weights,) = call(
+            functools.partial(back_kernel, width, blocks), [(padded, leaf_rows)], scaled, lower
+        )
     coefs = []
     for level in range(levels - 1):
         count = counts[level] - width
@@ -584,6 +596,8 @@
             near = partner(mine, level, inner_bits)
             far = partner(send, level, inner_bits)
             (half,) = call(functools.partial(pivot_kernel, 0, middle), [square], key, other_key)
+            send_last, half = lax.optimization_barrier((send_last, half))
+            far_last = partner(send_last, level, inner_bits)
             half, near = lax.optimization_barrier((half, near))
             cross = flip(near, 1)
             (inv,) = call(functools.partial(pivot_kernel, middle, width), [square], half)
@@ -601,25 +615,35 @@
                 scratch=[pltpu.VMEM((plan.rows3, width), F32)],
             )
             (key,) = call(functools.partial(next_key, width, count), [square], total, coef, cost=0.3)
+        elif spread and level == 2:
+            other_quarter = partner(quarter, level, inner_bits)
+            other_key = partner(key, level, inner_bits)
+            scaled, key = lax.optimization_barrier((scaled, key))
+            (weights,) = call(
+                functools.partial(back_kernel, width, blocks),
+                [(padded, leaf_rows)],
+                scaled,
+                lower,
+                cost=1.0,
+            )
+            quarter, weights = lax.optimization_barrier((quarter, weights))
+            (quarter,) = call(add_kernel, [quarter.shape], quarter, other_quarter, cost=0.1)
+            opposite = flip(quarter, 2)
+            far_last, _ = lax.optimization_barrier((far_last, quarter))
             (last_half,) = call(
-                functools.partial(half_update, plan, width, count, below),
+                functools.partial(half_update, plan, width, counts[1] - width, levels - 2),
                 [(plan.far3, width)],
                 place,
                 total,
-                coef,
+                coefs[1],
                 rest_far,
-                far,
+                far_last,
+                cost=0.3,
                 smem=1,
                 scratch=[pltpu.VMEM((plan.last3, width), F32)],
             )
-        elif spread and level == 2:
-            other_quarter = partner(quarter, level, inner_bits)
-            other_key = partner(key, level, inner_bits)
             other_half = partner(last_half, level, inner_bits)
-            quarter, weights = lax.optimization_barrier((quarter, weights))
-            (quarter,) = call(add_kernel, [quarter.shape], quarter, other_quarter, cost=0.1)
-            other_key, _ = lax.optimization_barrier((other_key, quarter))
-            opposite = flip(quarter, 2)
+            other_key, _ = lax.optimization_barrier((other_key, last_half))
             (half,) = call(functools.partial(pivot_kernel, 0, middle), [square], key, other_key)
             half, opposite = lax.optimization_barrier((half, opposite))
             (joined,) = call(join_kernel, [(2 * plan.near3, width)], quarter, opposite, cost=0.1)
@@ -657,6 +681,16 @@
                 sent_rest, other_key = lax.optimization_barrier((rest, other_key))
             other_rest = partner(sent_rest, level, inner_bits)
             (inv,) = call(functools.partial(pivot_kernel, 0, width), [square], key, other_key)
+            if level == levels - 2:
+                coef, last = call(
+                    functools.partial(last_update, width, count),
+                    [(count, width), (counts[level + 1], width)],
+                    rest,
+                    other_rest,
+                    inv,
+                )
+                coefs.append(coef)
+                continue
             total, coef, key = call(
                 functools.partial(near_update, width, count, take_full),
                 [(counts[level], width), (count, width), square],
@@ -667,12 +701,12 @@
             if spread and level == 0:
                 parts = []
                 for first, size, sent in (
-                    (0, plan.near, plan.near2),
-                    (plan.near, plan.far, plan.near3 + plan.far3),
+                    (0, plan.near, [plan.near2]),
+                    (plan.near, plan.far, [plan.near3, plan.far3]),
                 ):
                     parts += call(
                         functools.partial(part_update, plan, width, count, below, first),
-                        [(size, width), (sent, width)],
+                        [(each, width) for each in [size] + sent],
                         place,
                         rest,
                         other_rest,
@@ -682,7 +716,7 @@
                         smem=1,
                     )
                     total, _ = lax.optimization_barrier((total, parts[-1]))
-                rest_near, mine, rest_far, send = parts
+                rest_near, mine, rest_far, send, send_last = parts
             else:
                 (rest,) = call(
                     functools.partial(far_update, width, count, below),
@@ -693,7 +727,6 @@
                     coef,
                 )
         coefs.append(coef)
-    last = jnp.concatenate([key, rest], axis=0)
     other_last = partner(last, levels - 1, inner_bits)
     (folded,) = call(
         functools.partial(fold_kernel, levels, width, nrhs),

time: 63.1 us -> 61.1 us (0.968)
  waiting for transfers between devices: 8.97 us -> 6.24 us
  starting transfers between devices: 18.5 us -> 20.5 us
  local copies, waits for them, and re-layouts: 0.65 us -> 0 us
    ppermute x15 -> x16, waiting for transfers between devices: 8.97 us -> 6.24 us  [flip(): return lax.ppermute(value, axis, pairs)]
    ppermute x15 -> x16, starting transfers between devices: 18.5 us -> 20.5 us  [flip(): return lax.ppermute(value, axis, pairs)]
    unnamed x2 -> x0, local copies, waits for them, and re-layouts: 0.65 us -> none
    pallas_call x24 -> x23, Pallas kernels: 34.6 us -> 34 us  [call(): pl.pallas_call(kernel, out_shape=outs, in_specs=space, out_specs=[pl.Bloc...]
  transfers between devices with their start and end apart: 15 -> 16, of which waited for: 8 -> 6; matrix products, arithmetic and copies ran while one was open for 0% -> 0% of each run, Pallas kernels for 26% -> 29%
where the time goes in v4:
time: 61.1 us; the launch traced here: 60.9 us
  Pallas kernels  34 us (56%)
  starting transfers between devices  20.5 us (34%)
  waiting for transfers between devices  6.24 us (10%)
    pallas_call x23, Pallas kernels, call(): pl.pallas_call(kernel, out_shape=outs, in_specs=space, out_specs=[pl.Bloc...  34 us
    ppermute x16, starting transfers between devices, flip(): return lax.ppermute(value, axis, pairs)  20.5 us
    ppermute x16, waiting for transfers between devices, flip(): return lax.ppermute(value, axis, pairs)  6.24 us
  transfers between devices with their start and end apart: 16, of which 6 were waited for; matrix products, arithmetic and copies ran while one was open for 0% of the time, Pallas kernels for 29%

profile of v4, /device:TPU:0, one launch (start us, length us, event | category | flops | bytes accessed | tf_op | source)
XLA Modules:
  0.0 60.9 jit_solution(2652076754377091086)
XLA Ops:
  0.0 11.8 %shard_map.46 = (f32[128,128]{1,0:T(8,128)S(1)}, f32[1832,128]{1,0:T(8,128)S(1)}, f32[3,656,128]{2,1,0:T(8,128)S(1)}, f32[3,2,128,128]{3,2,1,0:T(8,128)S(1)}, bf...) custom-call(s32[1]{0:T(128)} %bitcast.place_ref.refs_0_, s32[31]{0:T(128)} %ranks_hbm.1, f32[8,384]{1,0:T(8,128)} %bitcast.3, ...), custom_call_target="tpu_custom_call" | custom-call | flops 1500000000 | bytes 5000000 | tf_op jit(solution)/shard_map/pallas_call | solution.py:490
  11.9 0.5 collective-permute-start
  12.4 0.7 %shard_map.47.refs_0_ = f32[1832,128]{1,0:T(8,128)S(1)} custom-call(f32[1832,128]{1,0:T(8,128)S(1)} %get-tuple-element.44.part_ref, bf16[656,768]{1,0:T(8,128)(2,1)S(1)} %get-tuple-element.45.v6_ref, bf16[640,768]{1,0:T(8,128)(2,1)S(1)} %get-tuple-element.46.s6_ref), custom_call_target="tpu_custom_call" | custom-call | flops 1500000000 | bytes 5000000 | tf_op jit(solution)/shard_map/pallas_call | solution.py:490
  13.1 0.2 collective-permute-done.refs_1_
  13.3 0.4 collective-permute-start.1
  13.6 2.8 %shard_map.48.refs_2_ = f32[128,128]{1,0:T(8,128)S(1)} custom-call(f32[128,128]{1,0:T(8,128)S(1)} %get-tuple-element.47.refs_0_, f32[128,128]{1,0:T(8,128)S(1)} %collective-permute-done.refs_1_), custom_call_target="tpu_custom_call" | custom-call | flops 1500000000 | bytes 5000000 | tf_op jit(solution)/shard_map/pallas_call | solution.py:490
  16.4 0.0 collective-permute-done.1.refs_1_
  16.4 0.5 shard_map.49
  17.0 2.8 %collective-permute-start.2 = (f32[128,128]{1,0:T(8,128)S(1)}, f32[128,128]{1,0:T(8,128)S(1)}, u32[]{:S(2)}, u32[]{:S(2)}) collective-permute-start(f32[128,128]{1,0:T(8,128)S(1)} %get-tuple-element.56.refs_0_), channel_id=1, source_target_pairs={{0,2},{1,3},{2,0},{3,1},{4,6},{5,7},{6,4},{7,5},{8,10},{9,11},{10,... | collective-permute-start | bytes 196616 | tf_op jit(solution)/shard_map/ppermute | solution.py:503
  19.8 0.6 shard_map.50
  20.4 0.1 collective-permute-start.3
  20.4 0.5 shard_map.51
  20.9 2.1 %collective-permute-start.5 = (f32[104,128]{1,0:T(8,128)S(1)}, f32[104,128]{1,0:T(8,128)S(1)}, u32[]{:S(2)}, u32[]{:S(2)}) collective-permute-start(f32[104,128]{1,0:T(8,128)S(1)} %get-tuple-element.60), channel_id=1, source_target_pairs={{0,2},{1,3},{2,0},{3,1},{4,6},{5,7},{6,4},{7,5},{8,10},{9,11},{10,... | collective-permute-start | bytes 159752 | tf_op jit(solution)/shard_map/ppermute | solution.py:503
  23.0 0.0 collective-permute-done.2.refs_1_
  23.0 1.4 %shard_map.52.refs_0_ = f32[128,128]{1,0:T(8,128)S(1)} custom-call(f32[128,128]{1,0:T(8,128)S(1)} %get-tuple-element.56.refs_0_, f32[128,128]{1,0:T(8,128)S(1)} %collective-permute-done.2.refs_1_), custom_call_target="tpu_custom_call" | custom-call | flops 1500000000 | bytes 5000000 | tf_op jit(solution)/shard_map/pallas_call | solution.py:490
  24.4 1.7 %collective-permute-start.6 = (f32[136,128]{1,0:T(8,128)S(1)}, f32[136,128]{1,0:T(8,128)S(1)}, u32[]{:S(2)}, u32[]{:S(2)}) collective-permute-start(f32[136,128]{1,0:T(8,128)S(1)} %get-tuple-element.64), channel_id=1, source_target_pairs={{0,2},{1,3},{2,0},{3,1},{4,6},{5,7},{6,4},{7,5},{8,10},{9,11},{10,... | collective-permute-start | bytes 208904 | tf_op jit(solution)/shard_map/ppermute | solution.py:503
  26.2 0.4 collective-permute-done.3.refs_2_
  26.5 0.0 collective-permute-start.4
  26.6 1.4 %shard_map.53.refs_6_ = f32[128,128]{1,0:T(8,128)S(1)} custom-call(f32[128,128]{1,0:T(8,128)S(1)} %shard_map.52.refs_0_), custom_call_target="tpu_custom_call" | custom-call | flops 1500000000 | bytes 5000000 | tf_op jit(solution)/shard_map/pallas_call | solution.py:490
  28.0 0.0 collective-permute-done.5.refs_5_
  28.0 0.9 %shard_map.54 = (f32[520,128]{1,0:T(8,128)S(1)}, f32[392,128]{1,0:T(8,128)S(1)}, f32[104,128]{1,0:T(8,128)S(1)}) custom-call(s32[1]{0:T(128)} %bitcast.place_ref.refs_0_, f32[520,128]{1,0:T(8,128)S(1)} %get-tuple-element.52.refs_1_, f32[264,128]{1,0:T(8,128)S(1)} %collective-permute-done.3.refs_2_, f32[264,128]{1,0:T(8,128)S(1)} %collective-permute-done.4.refs_3_, ...), custom_call_target="tpu_custom_call" | custom-call | flops 1500000000 | bytes 5000000 | tf_op jit(solution)/shard_map/pallas_call | solution.py:490
  28.9 2.7 %collective-permute-start.7 = (f32[104,128]{1,0:T(8,128)S(1)}, f32[104,128]{1,0:T(8,128)S(1)}, u32[]{:S(2)}, u32[]{:S(2)}) collective-permute-start(f32[104,128]{1,0:T(8,128)S(1)} %get-tuple-element.69.own_ref), channel_id=1, source_target_pairs={{0,4},{1,5},{2,6},{3,7},{4,0},{5,1},{6,2},{7,3},{8,12},{9,13},{10,... | collective-permute-start | bytes 159752 | tf_op jit(solution)/shard_map/ppermute | solution.py:503
  31.5 0.2 shard_map.55.refs_0_
  31.8 0.4 collective-permute-start.8
  32.2 1.0 %shard_map.56.weights_ref = f32[656,384]{1,0:T(8,128)S(1)} custom-call(f32[3,656,128]{2,1,0:T(8,128)S(1)} %get-tuple-element.67.scaled_ref, f32[3,2,128,128]{3,2,1,0:T(8,128)S(1)} %get-tuple-element.68.lower_ref), custom_call_target="tpu_custom_call" | custom-call | flops 1000000000 | bytes 3333333 | tf_op jit(solution)/shard_map/pallas_call | solution.py:490
  33.1 2.1 %collective-permute-done.7.other_ref = f32[104,128]{1,0:T(8,128)S(1)} collective-permute-done((f32[104,128]{1,0:T(8,128)S(1)}, f32[104,128]{1,0:T(8,128)S(1)}, u32[]{:S(2)}, u32[]{:S(2)}) %collective-permute-start.7) | collective-permute-done | bytes 53280 | tf_op jit(solution)/shard_map/ppermute | solution.py:503
  35.2 2.0 %collective-permute-start.9 = (f32[104,128]{1,0:T(8,128)S(1)}, f32[104,128]{1,0:T(8,128)S(1)}, u32[]{:S(2)}, u32[]{:S(2)}) collective-permute-start(f32[104,128]{1,0:T(8,128)S(1)} %shard_map.57.first_ref), channel_id=1, source_target_pairs={{0,2},{1,3},{2,0},{3,1},{4,6},{5,7},{6,4},{7,5},{8,10},{9,11},{10,... | collective-permute-start | bytes 159752 | tf_op jit(solution)/shard_map/ppermute | solution.py:503
  37.2 0.3 shard_map.58.own_ref
  37.6 3.5 %collective-permute-start.10 = (f32[136,128]{1,0:T(8,128)S(1)}, f32[136,128]{1,0:T(8,128)S(1)}, u32[]{:S(2)}, u32[]{:S(2)}) collective-permute-start(f32[136,128]{1,0:T(8,128)S(1)} %shard_map.58.own_ref), channel_id=1, source_target_pairs={{0,4},{1,5},{2,6},{3,7},{4,0},{5,1},{6,2},{7,3},{8,12},{9,13},{10,... | collective-permute-start | bytes 208904 | tf_op jit(solution)/shard_map/ppermute | solution.py:503
  41.1 0.0 collective-permute-done.8.refs_1_
  41.1 1.4 %shard_map.59.refs_0_ = f32[128,128]{1,0:T(8,128)S(1)} custom-call(f32[128,128]{1,0:T(8,128)S(1)} %shard_map.55.refs_0_, f32[128,128]{1,0:T(8,128)S(1)} %collective-permute-done.8.refs_1_), custom_call_target="tpu_custom_call" | custom-call | flops 1500000000 | bytes 5000000 | tf_op jit(solution)/shard_map/pallas_call | solution.py:490
  42.5 0.1 collective-permute-start.12
  42.6 1.4 %shard_map.60.refs_3_ = f32[128,128]{1,0:T(8,128)S(1)} custom-call(f32[128,128]{1,0:T(8,128)S(1)} %shard_map.59.refs_0_), custom_call_target="tpu_custom_call" | custom-call | flops 1500000000 | bytes 5000000 | tf_op jit(solution)/shard_map/pallas_call | solution.py:490
  44.1 0.6 collective-permute-start.11
  44.6 0.0 collective-permute-done.12.refs_2_
  44.6 0.5 shard_map.63
  45.1 1.5 %collective-permute-start.14 = (f32[128,128]{1,0:T(8,128)S(1)}, f32[128,128]{1,0:T(8,128)S(1)}, u32[]{:S(2)}, u32[]{:S(2)}) collective-permute-start(f32[128,128]{1,0:T(8,128)S(1)} %get-tuple-element.79.refs_0_), channel_id=1, source_target_pairs={{0,8},{8,0},{16,24},{24,16},{1,9},{9,1},{17,25},{25,17},{2,10},{10... | collective-permute-start | bytes 196616 | tf_op jit(solution)/shard_map/ppermute | solution.py:503
  46.7 0.0 collective-permute-done.11.refs_2_
  46.7 0.3 shard_map.64.own_ref
  47.0 0.6 %collective-permute-start.13 = (f32[272,128]{1,0:T(8,128)S(1)}, f32[272,128]{1,0:T(8,128)S(1)}, u32[]{:S(2)}, u32[]{:S(2)}) collective-permute-start(f32[272,128]{1,0:T(8,128)S(1)} %shard_map.64.own_ref), channel_id=1, source_target_pairs={{0,8},{8,0},{16,24},{24,16},{1,9},{9,1},{17,25},{25,17},{2,10},{10... | collective-permute-start | bytes 417800 | tf_op jit(solution)/shard_map/ppermute | solution.py:503
  47.6 2.0 %collective-permute-done.14.refs_1_ = f32[128,128]{1,0:T(8,128)S(1)} collective-permute-done((f32[128,128]{1,0:T(8,128)S(1)}, f32[128,128]{1,0:T(8,128)S(1)}, u32[]{:S(2)}, u32[]{:S(2)}) %collective-permute-start.14) | collective-permute-done | bytes 65568 | tf_op jit(solution)/shard_map/ppermute | solution.py:503
  49.6 2.8 %shard_map.65.inv_ref = f32[128,128]{1,0:T(8,128)S(1)} custom-call(f32[128,128]{1,0:T(8,128)S(1)} %get-tuple-element.79.refs_0_, f32[128,128]{1,0:T(8,128)S(1)} %collective-permute-done.14.refs_1_), custom_call_target="tpu_custom_call" | custom-call | flops 1500000000 | bytes 5000000 | tf_op jit(solution)/shard_map/pallas_call | solution.py:490
  52.4 0.1 collective-permute-done.13.other_ref
  52.5 0.4 shard_map.66
  52.9 1.6 %collective-permute-start.15 = (f32[136,128]{1,0:T(8,128)S(1)}, f32[136,128]{1,0:T(8,128)S(1)}, u32[]{:S(2)}, u32[]{:S(2)}) collective-permute-start(f32[136,128]{1,0:T(8,128)S(1)} %get-tuple-element.80.own_ref), channel_id=1, source_target_pairs={{0,16},{8,24},{16,0},{24,8},{1,17},{9,25},{17,1},{25,9},{2,18},{10... | collective-permute-start | bytes 208904 | tf_op jit(solution)/shard_map/ppermute | solution.py:503
  54.4 1.3 %shard_map.67.folded_ref = f32[136,384]{1,0:T(8,128)S(1)} custom-call(f32[656,384]{1,0:T(8,128)S(1)} %shard_map.56.weights_ref, f32[520,128]{1,0:T(8,128)S(1)} %get-tuple-element.51.refs_3_.refs_0_, f32[392,128]{1,0:T(8,128)S(1)} %get-tuple-element.63.coef_ref.refs_2_.refs_1_, f32[264,128]{1,0:T(8,128)S(1)} %get-tuple-element.78.refs_4_.refs_2_, ...), custom_call_target="tpu_custom_call" | custom-call | flops 1500000000 | bytes 5000000 | tf_op jit(solution)/shard_map/pallas_call | solution.py:490
  55.8 1.5 %collective-permute-done.15.other_ref = f32[136,128]{1,0:T(8,128)S(1)} collective-permute-done((f32[136,128]{1,0:T(8,128)S(1)}, f32[136,128]{1,0:T(8,128)S(1)}, u32[]{:S(2)}, u32[]{:S(2)}) %collective-permute-start.15) | collective-permute-done | bytes 69664 | tf_op jit(solution)/shard_map/ppermute | solution.py:503
  57.2 3.7 %shard_map.68 = f32[8,384]{1,0:T(8,128)} custom-call(f32[136,128]{1,0:T(8,128)S(1)} %get-tuple-element.80.own_ref, f32[136,128]{1,0:T(8,128)S(1)} %collective-permute-done.15.other_ref, f32[136,384]{1,0:T(8,128)S(1)} %shard_map.67.folded_ref), custom_call_target="tpu_custom_call" | custom-call | flops 1500000000 | bytes 5000000 | tf_op jit(solution)/shard_map/pallas_call | solution.py:490
  (7 shorter events, 0.0 us)
Async XLA Ops:
  11.9 1.4 %collective-permute-start = (f32[128,128]{1,0:T(8,128)S(1)}, f32[128,128]{1,0:T(8,128)S(1)}, u32[]{:S(2)}, u32[]{:S(2)}) collective-permute-start(f32[128,128]{1,0:T(8,128)S(1)} %get-tuple-element.47.refs_0_), channel_id=1, source_target_pairs={{0,1},{1,0},{2,3},{3,2},{4,5},{5,4},{6,7},{7,6},{8,9},{9,8},{10,11... | collective-permute-start | bytes 196616 | tf_op jit(solution)/shard_map/ppermute | solution.py:503
  13.3 3.1 %collective-permute-start.1 = (f32[1832,128]{1,0:T(8,128)S(1)}, f32[1832,128]{1,0:T(8,128)S(1)}, u32[]{:S(2)}, u32[]{:S(2)}) collective-permute-start(f32[1832,128]{1,0:T(8,128)S(1)} %shard_map.47.refs_0_), channel_id=1, source_target_pairs={{0,1},{1,0},{2,3},{3,2},{4,5},{5,4},{6,7},{7,6},{8,9},{9,8},{10,11... | collective-permute-start | bytes 2813960 | tf_op jit(solution)/shard_map/ppermute | solution.py:503
  17.0 6.0 %collective-permute-start.2 = (f32[128,128]{1,0:T(8,128)S(1)}, f32[128,128]{1,0:T(8,128)S(1)}, u32[]{:S(2)}, u32[]{:S(2)}) collective-permute-start(f32[128,128]{1,0:T(8,128)S(1)} %get-tuple-element.56.refs_0_), channel_id=1, source_target_pairs={{0,2},{1,3},{2,0},{3,1},{4,6},{5,7},{6,4},{7,5},{8,10},{9,11},{10,... | collective-permute-start | bytes 196616 | tf_op jit(solution)/shard_map/ppermute | solution.py:503
  20.4 6.2 %collective-permute-start.3 = (f32[264,128]{1,0:T(8,128)S(1)}, f32[264,128]{1,0:T(8,128)S(1)}, u32[]{:S(2)}, u32[]{:S(2)}) collective-permute-start(f32[264,128]{1,0:T(8,128)S(1)} %get-tuple-element.53), channel_id=1, source_target_pairs={{0,2},{1,3},{2,0},{3,1},{4,6},{5,7},{6,4},{7,5},{8,10},{9,11},{10,... | collective-permute-start | bytes 405512 | tf_op jit(solution)/shard_map/ppermute | solution.py:503
  20.9 7.1 %collective-permute-start.5 = (f32[104,128]{1,0:T(8,128)S(1)}, f32[104,128]{1,0:T(8,128)S(1)}, u32[]{:S(2)}, u32[]{:S(2)}) collective-permute-start(f32[104,128]{1,0:T(8,128)S(1)} %get-tuple-element.60), channel_id=1, source_target_pairs={{0,2},{1,3},{2,0},{3,1},{4,6},{5,7},{6,4},{7,5},{8,10},{9,11},{10,... | collective-permute-start | bytes 159752 | tf_op jit(solution)/shard_map/ppermute | solution.py:503
  24.4 12.8 %collective-permute-start.6 = (f32[136,128]{1,0:T(8,128)S(1)}, f32[136,128]{1,0:T(8,128)S(1)}, u32[]{:S(2)}, u32[]{:S(2)}) collective-permute-start(f32[136,128]{1,0:T(8,128)S(1)} %get-tuple-element.64), channel_id=1, source_target_pairs={{0,2},{1,3},{2,0},{3,1},{4,6},{5,7},{6,4},{7,5},{8,10},{9,11},{10,... | collective-permute-start | bytes 208904 | tf_op jit(solution)/shard_map/ppermute | solution.py:503
  26.5 1.4 %collective-permute-start.4 = (f32[264,128]{1,0:T(8,128)S(1)}, f32[264,128]{1,0:T(8,128)S(1)}, u32[]{:S(2)}, u32[]{:S(2)}) collective-permute-start(f32[264,128]{1,0:T(8,128)S(1)} %collective-permute-done.3.refs_2_), channel_id=1, source_target_pairs={{0,1},{1,0},{2,3},{3,2},{4,5},{5,4},{6,7},{7,6},{8,9},{9,8},{10,11... | collective-permute-start | bytes 405512 | tf_op jit(solution)/shard_map/ppermute | solution.py:503
  28.9 6.3 %collective-permute-start.7 = (f32[104,128]{1,0:T(8,128)S(1)}, f32[104,128]{1,0:T(8,128)S(1)}, u32[]{:S(2)}, u32[]{:S(2)}) collective-permute-start(f32[104,128]{1,0:T(8,128)S(1)} %get-tuple-element.69.own_ref), channel_id=1, source_target_pairs={{0,4},{1,5},{2,6},{3,7},{4,0},{5,1},{6,2},{7,3},{8,12},{9,13},{10,... | collective-permute-start | bytes 159752 | tf_op jit(solution)/shard_map/ppermute | solution.py:503
  31.8 9.3 %collective-permute-start.8 = (f32[128,128]{1,0:T(8,128)S(1)}, f32[128,128]{1,0:T(8,128)S(1)}, u32[]{:S(2)}, u32[]{:S(2)}) collective-permute-start(f32[128,128]{1,0:T(8,128)S(1)} %shard_map.55.refs_0_), channel_id=1, source_target_pairs={{0,4},{1,5},{2,6},{3,7},{4,0},{5,1},{6,2},{7,3},{8,12},{9,13},{10,... | collective-permute-start | bytes 196616 | tf_op jit(solution)/shard_map/ppermute | solution.py:503
  35.2 7.3 %collective-permute-start.9 = (f32[104,128]{1,0:T(8,128)S(1)}, f32[104,128]{1,0:T(8,128)S(1)}, u32[]{:S(2)}, u32[]{:S(2)}) collective-permute-start(f32[104,128]{1,0:T(8,128)S(1)} %shard_map.57.first_ref), channel_id=1, source_target_pairs={{0,2},{1,3},{2,0},{3,1},{4,6},{5,7},{6,4},{7,5},{8,10},{9,11},{10,... | collective-permute-start | bytes 159752 | tf_op jit(solution)/shard_map/ppermute | solution.py:503
  37.6 6.5 %collective-permute-start.10 = (f32[136,128]{1,0:T(8,128)S(1)}, f32[136,128]{1,0:T(8,128)S(1)}, u32[]{:S(2)}, u32[]{:S(2)}) collective-permute-start(f32[136,128]{1,0:T(8,128)S(1)} %shard_map.58.own_ref), channel_id=1, source_target_pairs={{0,4},{1,5},{2,6},{3,7},{4,0},{5,1},{6,2},{7,3},{8,12},{9,13},{10,... | collective-permute-start | bytes 208904 | tf_op jit(solution)/shard_map/ppermute | solution.py:503
  42.5 2.1 %collective-permute-start.12 = (f32[208,128]{1,0:T(8,128)S(1)}, f32[208,128]{1,0:T(8,128)S(1)}, u32[]{:S(2)}, u32[]{:S(2)}) collective-permute-start(f32[208,128]{1,0:T(8,128)S(1)} %shard_map.62.refs_1_), channel_id=1, source_target_pairs={{0,1},{1,0},{2,3},{3,2},{4,5},{5,4},{6,7},{7,6},{8,9},{9,8},{10,11... | collective-permute-start | bytes 319496 | tf_op jit(solution)/shard_map/ppermute | solution.py:503
  44.1 2.6 %collective-permute-start.11 = (f32[136,128]{1,0:T(8,128)S(1)}, f32[136,128]{1,0:T(8,128)S(1)}, u32[]{:S(2)}, u32[]{:S(2)}) collective-permute-start(f32[136,128]{1,0:T(8,128)S(1)} %shard_map.61.refs_1_), channel_id=1, source_target_pairs={{0,1},{1,0},{2,3},{3,2},{4,5},{5,4},{6,7},{7,6},{8,9},{9,8},{10,11... | collective-permute-start | bytes 208904 | tf_op jit(solution)/shard_map/ppermute | solution.py:503
  45.1 4.5 %collective-permute-start.14 = (f32[128,128]{1,0:T(8,128)S(1)}, f32[128,128]{1,0:T(8,128)S(1)}, u32[]{:S(2)}, u32[]{:S(2)}) collective-permute-start(f32[128,128]{1,0:T(8,128)S(1)} %get-tuple-element.79.refs_0_), channel_id=1, source_target_pairs={{0,8},{8,0},{16,24},{24,16},{1,9},{9,1},{17,25},{25,17},{2,10},{10... | collective-permute-start | bytes 196616 | tf_op jit(solution)/shard_map/ppermute | solution.py:503
  47.0 5.5 %collective-permute-start.13 = (f32[272,128]{1,0:T(8,128)S(1)}, f32[272,128]{1,0:T(8,128)S(1)}, u32[]{:S(2)}, u32[]{:S(2)}) collective-permute-start(f32[272,128]{1,0:T(8,128)S(1)} %shard_map.64.own_ref), channel_id=1, source_target_pairs={{0,8},{8,0},{16,24},{24,16},{1,9},{9,1},{17,25},{25,17},{2,10},{10... | collective-permute-start | bytes 417800 | tf_op jit(solution)/shard_map/ppermute | solution.py:503
  52.9 4.4 %collective-permute-start.15 = (f32[136,128]{1,0:T(8,128)S(1)}, f32[136,128]{1,0:T(8,128)S(1)}, u32[]{:S(2)}, u32[]{:S(2)}) collective-permute-start(f32[136,128]{1,0:T(8,128)S(1)} %get-tuple-element.80.own_ref), channel_id=1, source_target_pairs={{0,16},{8,24},{16,0},{24,8},{1,17},{9,25},{17,1},{25,9},{2,18},{10... | collective-permute-start | bytes 208904 | tf_op jit(solution)/shard_map/ppermute | solution.py:503

commit v5 on v4

--- a/solution.py
+++ b/solution.py
@@ -618,18 +618,6 @@
         elif spread and level == 2:
             other_quarter = partner(quarter, level, inner_bits)
             other_key = partner(key, level, inner_bits)
-            scaled, key = lax.optimization_barrier((scaled, key))
-            (weights,) = call(
-                functools.partial(back_kernel, width, blocks),
-                [(padded, leaf_rows)],
-                scaled,
-                lower,
-                cost=1.0,
-            )
-            quarter, weights = lax.optimization_barrier((quarter, weights))
-            (quarter,) = call(add_kernel, [quarter.shape], quarter, other_quarter, cost=0.1)
-            opposite = flip(quarter, 2)
-            far_last, _ = lax.optimization_barrier((far_last, quarter))
             (last_half,) = call(
                 functools.partial(half_update, plan, width, counts[1] - width, levels - 2),
                 [(plan.far3, width)],
@@ -643,7 +631,18 @@
                 scratch=[pltpu.VMEM((plan.last3, width), F32)],
             )
             other_half = partner(last_half, level, inner_bits)
-            other_key, _ = lax.optimization_barrier((other_key, last_half))
+            other_quarter, _ = lax.optimization_barrier((other_quarter, last_half))
+            (quarter,) = call(add_kernel, [quarter.shape], quarter, other_quarter, cost=0.1)
+            opposite = flip(quarter, 2)
+            scaled, _ = lax.optimization_barrier((scaled, quarter))
+            (weights,) = call(
+                functools.partial(back_kernel, width, blocks),
+                [(padded, leaf_rows)],
+                scaled,
+                lower,
+                cost=1.0,
+            )
+            other_key, weights = lax.optimization_barrier((other_key, weights))
             (half,) = call(functools.partial(pivot_kernel, 0, middle), [square], key, other_key)
             half, opposite = lax.optimization_barrier((half, opposite))
             (joined,) = call(join_kernel, [(2 * plan.near3, width)], quarter, opposite, cost=0.1)

time: 61.1 us -> 60.5 us (level)
  transfers between devices with their start and end apart: 16 -> 16, of which waited for: 6 -> 7; matrix products, arithmetic and copies ran while one was open for 0% -> 0% of each run, Pallas kernels for 29% -> 29%
where the time goes in v5:
time: 60.5 us; the launch traced here: 60.3 us
  Pallas kernels  34 us (56%)
  starting transfers between devices  20.2 us (33%)
  waiting for transfers between devices  5.91 us (10%)
    pallas_call x23, Pallas kernels, call(): pl.pallas_call(kernel, out_shape=outs, in_specs=space, out_specs=[pl.Bloc...  34 us
    ppermute x16, starting transfers between devices, flip(): return lax.ppermute(value, axis, pairs)  20.2 us
    ppermute x16, waiting for transfers between devices, flip(): return lax.ppermute(value, axis, pairs)  5.91 us
  transfers between devices with their start and end apart: 16, of which 7 were waited for; matrix products, arithmetic and copies ran while one was open for 0% of the time, Pallas kernels for 29%

profile of v5, /device:TPU:0, one launch (start us, length us, event | category | flops | bytes accessed | tf_op | source)
XLA Modules:
  0.0 60.3 jit_solution(16776853219874601936)
XLA Ops:
  0.0 11.8 %shard_map.46 = (f32[128,128]{1,0:T(8,128)S(1)}, f32[1832,128]{1,0:T(8,128)S(1)}, f32[3,656,128]{2,1,0:T(8,128)S(1)}, f32[3,2,128,128]{3,2,1,0:T(8,128)S(1)}, bf...) custom-call(s32[1]{0:T(128)} %bitcast.place_ref.refs_0_, s32[31]{0:T(128)} %ranks_hbm.1, f32[8,384]{1,0:T(8,128)} %bitcast.3, ...), custom_call_target="tpu_custom_call" | custom-call | flops 1500000000 | bytes 5000000 | tf_op jit(solution)/shard_map/pallas_call | solution.py:490
  11.9 0.5 collective-permute-start
  12.4 0.7 %shard_map.47.refs_0_ = f32[1832,128]{1,0:T(8,128)S(1)} custom-call(f32[1832,128]{1,0:T(8,128)S(1)} %get-tuple-element.42.part_ref, bf16[656,768]{1,0:T(8,128)(2,1)S(1)} %get-tuple-element.43.v6_ref, bf16[640,768]{1,0:T(8,128)(2,1)S(1)} %get-tuple-element.44.s6_ref), custom_call_target="tpu_custom_call" | custom-call | flops 1500000000 | bytes 5000000 | tf_op jit(solution)/shard_map/pallas_call | solution.py:490
  13.1 0.2 collective-permute-done.refs_1_
  13.3 0.4 collective-permute-start.1
  13.6 2.8 %shard_map.48.refs_2_ = f32[128,128]{1,0:T(8,128)S(1)} custom-call(f32[128,128]{1,0:T(8,128)S(1)} %get-tuple-element.45.refs_0_, f32[128,128]{1,0:T(8,128)S(1)} %collective-permute-done.refs_1_), custom_call_target="tpu_custom_call" | custom-call | flops 1500000000 | bytes 5000000 | tf_op jit(solution)/shard_map/pallas_call | solution.py:490
  16.4 0.0 collective-permute-done.1.refs_1_
  16.4 0.5 shard_map.49
  17.0 2.8 %collective-permute-start.2 = (f32[128,128]{1,0:T(8,128)S(1)}, f32[128,128]{1,0:T(8,128)S(1)}, u32[]{:S(2)}, u32[]{:S(2)}) collective-permute-start(f32[128,128]{1,0:T(8,128)S(1)} %get-tuple-element.54.refs_0_), channel_id=1, source_target_pairs={{0,2},{1,3},{2,0},{3,1},{4,6},{5,7},{6,4},{7,5},{8,10},{9,11},{10,... | collective-permute-start | bytes 196616 | tf_op jit(solution)/shard_map/ppermute | solution.py:503
  19.8 0.6 shard_map.50
  20.4 0.1 collective-permute-start.3
  20.4 0.5 shard_map.51
  20.9 2.1 %collective-permute-start.5 = (f32[104,128]{1,0:T(8,128)S(1)}, f32[104,128]{1,0:T(8,128)S(1)}, u32[]{:S(2)}, u32[]{:S(2)}) collective-permute-start(f32[104,128]{1,0:T(8,128)S(1)} %get-tuple-element.58), channel_id=1, source_target_pairs={{0,2},{1,3},{2,0},{3,1},{4,6},{5,7},{6,4},{7,5},{8,10},{9,11},{10,... | collective-permute-start | bytes 159752 | tf_op jit(solution)/shard_map/ppermute | solution.py:503
  23.0 1.4 %shard_map.52.refs_0_ = f32[128,128]{1,0:T(8,128)S(1)} custom-call(f32[128,128]{1,0:T(8,128)S(1)} %get-tuple-element.54.refs_0_, f32[128,128]{1,0:T(8,128)S(1)} %collective-permute-done.2.refs_1_), custom_call_target="tpu_custom_call" | custom-call | flops 1500000000 | bytes 5000000 | tf_op jit(solution)/shard_map/pallas_call | solution.py:490
  24.4 1.7 %collective-permute-start.6 = (f32[136,128]{1,0:T(8,128)S(1)}, f32[136,128]{1,0:T(8,128)S(1)}, u32[]{:S(2)}, u32[]{:S(2)}) collective-permute-start(f32[136,128]{1,0:T(8,128)S(1)} %get-tuple-element.62), channel_id=1, source_target_pairs={{0,2},{1,3},{2,0},{3,1},{4,6},{5,7},{6,4},{7,5},{8,10},{9,11},{10,... | collective-permute-start | bytes 208904 | tf_op jit(solution)/shard_map/ppermute | solution.py:503
  26.2 0.4 collective-permute-done.3.refs_2_
  26.6 1.4 %shard_map.53.refs_6_ = f32[128,128]{1,0:T(8,128)S(1)} custom-call(f32[128,128]{1,0:T(8,128)S(1)} %shard_map.52.refs_0_), custom_call_target="tpu_custom_call" | custom-call | flops 1500000000 | bytes 5000000 | tf_op jit(solution)/shard_map/pallas_call | solution.py:490
  28.0 0.0 collective-permute-done.5.refs_5_
  28.0 0.0 collective-permute-done.4.refs_3_
  28.0 0.9 %shard_map.54 = (f32[520,128]{1,0:T(8,128)S(1)}, f32[392,128]{1,0:T(8,128)S(1)}, f32[104,128]{1,0:T(8,128)S(1)}) custom-call(s32[1]{0:T(128)} %bitcast.place_ref.refs_0_, f32[520,128]{1,0:T(8,128)S(1)} %get-tuple-element.50.refs_1_, f32[264,128]{1,0:T(8,128)S(1)} %collective-permute-done.3.refs_2_, f32[264,128]{1,0:T(8,128)S(1)} %collective-permute-done.4.refs_3_, ...), custom_call_target="tpu_custom_call" | custom-call | flops 1500000000 | bytes 5000000 | tf_op jit(solution)/shard_map/pallas_call | solution.py:490
  28.9 2.7 %collective-permute-start.8 = (f32[104,128]{1,0:T(8,128)S(1)}, f32[104,128]{1,0:T(8,128)S(1)}, u32[]{:S(2)}, u32[]{:S(2)}) collective-permute-start(f32[104,128]{1,0:T(8,128)S(1)} %get-tuple-element.64.own_ref), channel_id=1, source_target_pairs={{0,4},{1,5},{2,6},{3,7},{4,0},{5,1},{6,2},{7,3},{8,12},{9,13},{10,... | collective-permute-start | bytes 159752 | tf_op jit(solution)/shard_map/ppermute | solution.py:503
  31.5 0.2 shard_map.56.refs_0_
  31.8 0.4 collective-permute-start.7
  32.2 0.0 collective-permute-done.6.refs_4_
  32.2 0.3 shard_map.55.own_ref
  32.5 2.7 %collective-permute-start.10 = (f32[136,128]{1,0:T(8,128)S(1)}, f32[136,128]{1,0:T(8,128)S(1)}, u32[]{:S(2)}, u32[]{:S(2)}) collective-permute-start(f32[136,128]{1,0:T(8,128)S(1)} %shard_map.55.own_ref), channel_id=1, source_target_pairs={{0,4},{1,5},{2,6},{3,7},{4,0},{5,1},{6,2},{7,3},{8,12},{9,13},{10,... | collective-permute-start | bytes 208904 | tf_op jit(solution)/shard_map/ppermute | solution.py:503
  35.1 0.1 collective-permute-done.8.other_ref
  35.2 2.6 %collective-permute-start.9 = (f32[104,128]{1,0:T(8,128)S(1)}, f32[104,128]{1,0:T(8,128)S(1)}, u32[]{:S(2)}, u32[]{:S(2)}) collective-permute-start(f32[104,128]{1,0:T(8,128)S(1)} %shard_map.57.first_ref), channel_id=1, source_target_pairs={{0,2},{1,3},{2,0},{3,1},{4,6},{5,7},{6,4},{7,5},{8,10},{9,11},{10,... | collective-permute-start | bytes 159752 | tf_op jit(solution)/shard_map/ppermute | solution.py:503
  37.8 1.0 %shard_map.58.weights_ref = f32[656,384]{1,0:T(8,128)S(1)} custom-call(f32[3,656,128]{2,1,0:T(8,128)S(1)} %get-tuple-element.66.scaled_ref, f32[3,2,128,128]{3,2,1,0:T(8,128)S(1)} %get-tuple-element.67.lower_ref), custom_call_target="tpu_custom_call" | custom-call | flops 1000000000 | bytes 3333333 | tf_op jit(solution)/shard_map/pallas_call | solution.py:490
  38.8 1.6 %collective-permute-done.7.refs_1_ = f32[128,128]{1,0:T(8,128)S(1)} collective-permute-done((f32[128,128]{1,0:T(8,128)S(1)}, f32[128,128]{1,0:T(8,128)S(1)}, u32[]{:S(2)}, u32[]{:S(2)}) %collective-permute-start.7) | collective-permute-done | bytes 65568 | tf_op jit(solution)/shard_map/ppermute | solution.py:503
  40.5 1.4 %shard_map.59.refs_0_ = f32[128,128]{1,0:T(8,128)S(1)} custom-call(f32[128,128]{1,0:T(8,128)S(1)} %shard_map.56.refs_0_, f32[128,128]{1,0:T(8,128)S(1)} %collective-permute-done.7.refs_1_), custom_call_target="tpu_custom_call" | custom-call | flops 1500000000 | bytes 5000000 | tf_op jit(solution)/shard_map/pallas_call | solution.py:490
  41.9 0.0 collective-permute-done.9.second_ref
  41.9 0.1 collective-permute-start.12
  42.0 1.4 %shard_map.60.refs_3_ = f32[128,128]{1,0:T(8,128)S(1)} custom-call(f32[128,128]{1,0:T(8,128)S(1)} %shard_map.59.refs_0_), custom_call_target="tpu_custom_call" | custom-call | flops 1500000000 | bytes 5000000 | tf_op jit(solution)/shard_map/pallas_call | solution.py:490
  43.4 0.0 collective-permute-done.10.other_ref
  43.5 0.6 collective-permute-start.11
  44.0 0.5 shard_map.63
  44.5 1.5 %collective-permute-start.14 = (f32[128,128]{1,0:T(8,128)S(1)}, f32[128,128]{1,0:T(8,128)S(1)}, u32[]{:S(2)}, u32[]{:S(2)}) collective-permute-start(f32[128,128]{1,0:T(8,128)S(1)} %get-tuple-element.75.refs_0_), channel_id=1, source_target_pairs={{0,8},{8,0},{16,24},{24,16},{1,9},{9,1},{17,25},{25,17},{2,10},{10... | collective-permute-start | bytes 196616 | tf_op jit(solution)/shard_map/ppermute | solution.py:503
  46.1 0.3 shard_map.64.own_ref
  46.4 0.6 %collective-permute-start.13 = (f32[272,128]{1,0:T(8,128)S(1)}, f32[272,128]{1,0:T(8,128)S(1)}, u32[]{:S(2)}, u32[]{:S(2)}) collective-permute-start(f32[272,128]{1,0:T(8,128)S(1)} %shard_map.64.own_ref), channel_id=1, source_target_pairs={{0,8},{8,0},{16,24},{24,16},{1,9},{9,1},{17,25},{25,17},{2,10},{10... | collective-permute-start | bytes 417800 | tf_op jit(solution)/shard_map/ppermute | solution.py:503
  47.0 2.0 %collective-permute-done.14.refs_1_ = f32[128,128]{1,0:T(8,128)S(1)} collective-permute-done((f32[128,128]{1,0:T(8,128)S(1)}, f32[128,128]{1,0:T(8,128)S(1)}, u32[]{:S(2)}, u32[]{:S(2)}) %collective-permute-start.14) | collective-permute-done | bytes 65568 | tf_op jit(solution)/shard_map/ppermute | solution.py:503
  49.0 2.8 %shard_map.65.inv_ref = f32[128,128]{1,0:T(8,128)S(1)} custom-call(f32[128,128]{1,0:T(8,128)S(1)} %get-tuple-element.75.refs_0_, f32[128,128]{1,0:T(8,128)S(1)} %collective-permute-done.14.refs_1_), custom_call_target="tpu_custom_call" | custom-call | flops 1500000000 | bytes 5000000 | tf_op jit(solution)/shard_map/pallas_call | solution.py:490
  51.8 0.1 collective-permute-done.13.other_ref
  51.9 0.4 shard_map.66
  52.3 1.6 %collective-permute-start.15 = (f32[136,128]{1,0:T(8,128)S(1)}, f32[136,128]{1,0:T(8,128)S(1)}, u32[]{:S(2)}, u32[]{:S(2)}) collective-permute-start(f32[136,128]{1,0:T(8,128)S(1)} %get-tuple-element.76.own_ref), channel_id=1, source_target_pairs={{0,16},{8,24},{16,0},{24,8},{1,17},{9,25},{17,1},{25,9},{2,18},{10... | collective-permute-start | bytes 208904 | tf_op jit(solution)/shard_map/ppermute | solution.py:503
  53.8 1.3 %shard_map.67.folded_ref = f32[136,384]{1,0:T(8,128)S(1)} custom-call(f32[656,384]{1,0:T(8,128)S(1)} %shard_map.58.weights_ref, f32[520,128]{1,0:T(8,128)S(1)} %get-tuple-element.49.refs_3_.refs_0_, f32[392,128]{1,0:T(8,128)S(1)} %get-tuple-element.61.refs_2_.coef_ref.refs_1_, f32[264,128]{1,0:T(8,128)S(1)} %get-tuple-element.74.refs_4_.refs_2_, ...), custom_call_target="tpu_custom_call" | custom-call | flops 1500000000 | bytes 5000000 | tf_op jit(solution)/shard_map/pallas_call | solution.py:490
  55.2 1.5 %collective-permute-done.15.other_ref = f32[136,128]{1,0:T(8,128)S(1)} collective-permute-done((f32[136,128]{1,0:T(8,128)S(1)}, f32[136,128]{1,0:T(8,128)S(1)}, u32[]{:S(2)}, u32[]{:S(2)}) %collective-permute-start.15) | collective-permute-done | bytes 69664 | tf_op jit(solution)/shard_map/ppermute | solution.py:503
  56.6 3.7 %shard_map.68 = f32[8,384]{1,0:T(8,128)} custom-call(f32[136,128]{1,0:T(8,128)S(1)} %get-tuple-element.76.own_ref, f32[136,128]{1,0:T(8,128)S(1)} %collective-permute-done.15.other_ref, f32[136,384]{1,0:T(8,128)S(1)} %shard_map.67.folded_ref), custom_call_target="tpu_custom_call" | custom-call | flops 1500000000 | bytes 5000000 | tf_op jit(solution)/shard_map/pallas_call | solution.py:490
  (7 shorter events, 0.0 us)
Async XLA Ops:
  11.9 1.4 %collective-permute-start = (f32[128,128]{1,0:T(8,128)S(1)}, f32[128,128]{1,0:T(8,128)S(1)}, u32[]{:S(2)}, u32[]{:S(2)}) collective-permute-start(f32[128,128]{1,0:T(8,128)S(1)} %get-tuple-element.45.refs_0_), channel_id=1, source_target_pairs={{0,1},{1,0},{2,3},{3,2},{4,5},{5,4},{6,7},{7,6},{8,9},{9,8},{10,11... | collective-permute-start | bytes 196616 | tf_op jit(solution)/shard_map/ppermute | solution.py:503
  13.3 3.1 %collective-permute-start.1 = (f32[1832,128]{1,0:T(8,128)S(1)}, f32[1832,128]{1,0:T(8,128)S(1)}, u32[]{:S(2)}, u32[]{:S(2)}) collective-permute-start(f32[1832,128]{1,0:T(8,128)S(1)} %shard_map.47.refs_0_), channel_id=1, source_target_pairs={{0,1},{1,0},{2,3},{3,2},{4,5},{5,4},{6,7},{7,6},{8,9},{9,8},{10,11... | collective-permute-start | bytes 2813960 | tf_op jit(solution)/shard_map/ppermute | solution.py:503
  17.0 6.0 %collective-permute-start.2 = (f32[128,128]{1,0:T(8,128)S(1)}, f32[128,128]{1,0:T(8,128)S(1)}, u32[]{:S(2)}, u32[]{:S(2)}) collective-permute-start(f32[128,128]{1,0:T(8,128)S(1)} %get-tuple-element.54.refs_0_), channel_id=1, source_target_pairs={{0,2},{1,3},{2,0},{3,1},{4,6},{5,7},{6,4},{7,5},{8,10},{9,11},{10,... | collective-permute-start | bytes 196616 | tf_op jit(solution)/shard_map/ppermute | solution.py:503
  20.4 6.2 %collective-permute-start.3 = (f32[264,128]{1,0:T(8,128)S(1)}, f32[264,128]{1,0:T(8,128)S(1)}, u32[]{:S(2)}, u32[]{:S(2)}) collective-permute-start(f32[264,128]{1,0:T(8,128)S(1)} %get-tuple-element.51), channel_id=1, source_target_pairs={{0,2},{1,3},{2,0},{3,1},{4,6},{5,7},{6,4},{7,5},{8,10},{9,11},{10,... | collective-permute-start | bytes 405512 | tf_op jit(solution)/shard_map/ppermute | solution.py:503
  20.9 7.1 %collective-permute-start.5 = (f32[104,128]{1,0:T(8,128)S(1)}, f32[104,128]{1,0:T(8,128)S(1)}, u32[]{:S(2)}, u32[]{:S(2)}) collective-permute-start(f32[104,128]{1,0:T(8,128)S(1)} %get-tuple-element.58), channel_id=1, source_target_pairs={{0,2},{1,3},{2,0},{3,1},{4,6},{5,7},{6,4},{7,5},{8,10},{9,11},{10,... | collective-permute-start | bytes 159752 | tf_op jit(solution)/shard_map/ppermute | solution.py:503
  24.4 7.7 %collective-permute-start.6 = (f32[136,128]{1,0:T(8,128)S(1)}, f32[136,128]{1,0:T(8,128)S(1)}, u32[]{:S(2)}, u32[]{:S(2)}) collective-permute-start(f32[136,128]{1,0:T(8,128)S(1)} %get-tuple-element.62), channel_id=1, source_target_pairs={{0,2},{1,3},{2,0},{3,1},{4,6},{5,7},{6,4},{7,5},{8,10},{9,11},{10,... | collective-permute-start | bytes 208904 | tf_op jit(solution)/shard_map/ppermute | solution.py:503
  26.5 1.4 %collective-permute-start.4 = (f32[264,128]{1,0:T(8,128)S(1)}, f32[264,128]{1,0:T(8,128)S(1)}, u32[]{:S(2)}, u32[]{:S(2)}) collective-permute-start(f32[264,128]{1,0:T(8,128)S(1)} %collective-permute-done.3.refs_2_), channel_id=1, source_target_pairs={{0,1},{1,0},{2,3},{3,2},{4,5},{5,4},{6,7},{7,6},{8,9},{9,8},{10,11... | collective-permute-start | bytes 405512 | tf_op jit(solution)/shard_map/ppermute | solution.py:503
  28.9 6.3 %collective-permute-start.8 = (f32[104,128]{1,0:T(8,128)S(1)}, f32[104,128]{1,0:T(8,128)S(1)}, u32[]{:S(2)}, u32[]{:S(2)}) collective-permute-start(f32[104,128]{1,0:T(8,128)S(1)} %get-tuple-element.64.own_ref), channel_id=1, source_target_pairs={{0,4},{1,5},{2,6},{3,7},{4,0},{5,1},{6,2},{7,3},{8,12},{9,13},{10,... | collective-permute-start | bytes 159752 | tf_op jit(solution)/shard_map/ppermute | solution.py:503
  31.8 8.7 %collective-permute-start.7 = (f32[128,128]{1,0:T(8,128)S(1)}, f32[128,128]{1,0:T(8,128)S(1)}, u32[]{:S(2)}, u32[]{:S(2)}) collective-permute-start(f32[128,128]{1,0:T(8,128)S(1)} %shard_map.56.refs_0_), channel_id=1, source_target_pairs={{0,4},{1,5},{2,6},{3,7},{4,0},{5,1},{6,2},{7,3},{8,12},{9,13},{10,... | collective-permute-start | bytes 196616 | tf_op jit(solution)/shard_map/ppermute | solution.py:503
  32.5 11.0 %collective-permute-start.10 = (f32[136,128]{1,0:T(8,128)S(1)}, f32[136,128]{1,0:T(8,128)S(1)}, u32[]{:S(2)}, u32[]{:S(2)}) collective-permute-start(f32[136,128]{1,0:T(8,128)S(1)} %shard_map.55.own_ref), channel_id=1, source_target_pairs={{0,4},{1,5},{2,6},{3,7},{4,0},{5,1},{6,2},{7,3},{8,12},{9,13},{10,... | collective-permute-start | bytes 208904 | tf_op jit(solution)/shard_map/ppermute | solution.py:503
  35.2 6.7 %collective-permute-start.9 = (f32[104,128]{1,0:T(8,128)S(1)}, f32[104,128]{1,0:T(8,128)S(1)}, u32[]{:S(2)}, u32[]{:S(2)}) collective-permute-start(f32[104,128]{1,0:T(8,128)S(1)} %shard_map.57.first_ref), channel_id=1, source_target_pairs={{0,2},{1,3},{2,0},{3,1},{4,6},{5,7},{6,4},{7,5},{8,10},{9,11},{10,... | collective-permute-start | bytes 159752 | tf_op jit(solution)/shard_map/ppermute | solution.py:503
  41.9 2.1 %collective-permute-start.12 = (f32[208,128]{1,0:T(8,128)S(1)}, f32[208,128]{1,0:T(8,128)S(1)}, u32[]{:S(2)}, u32[]{:S(2)}) collective-permute-start(f32[208,128]{1,0:T(8,128)S(1)} %shard_map.62.refs_1_), channel_id=1, source_target_pairs={{0,1},{1,0},{2,3},{3,2},{4,5},{5,4},{6,7},{7,6},{8,9},{9,8},{10,11... | collective-permute-start | bytes 319496 | tf_op jit(solution)/shard_map/ppermute | solution.py:503
  43.5 2.6 %collective-permute-start.11 = (f32[136,128]{1,0:T(8,128)S(1)}, f32[136,128]{1,0:T(8,128)S(1)}, u32[]{:S(2)}, u32[]{:S(2)}) collective-permute-start(f32[136,128]{1,0:T(8,128)S(1)} %shard_map.61.refs_1_), channel_id=1, source_target_pairs={{0,1},{1,0},{2,3},{3,2},{4,5},{5,4},{6,7},{7,6},{8,9},{9,8},{10,11... | collective-permute-start | bytes 208904 | tf_op jit(solution)/shard_map/ppermute | solution.py:503
  44.5 4.5 %collective-permute-start.14 = (f32[128,128]{1,0:T(8,128)S(1)}, f32[128,128]{1,0:T(8,128)S(1)}, u32[]{:S(2)}, u32[]{:S(2)}) collective-permute-start(f32[128,128]{1,0:T(8,128)S(1)} %get-tuple-element.75.refs_0_), channel_id=1, source_target_pairs={{0,8},{8,0},{16,24},{24,16},{1,9},{9,1},{17,25},{25,17},{2,10},{10... | collective-permute-start | bytes 196616 | tf_op jit(solution)/shard_map/ppermute | solution.py:503
  46.4 5.5 %collective-permute-start.13 = (f32[272,128]{1,0:T(8,128)S(1)}, f32[272,128]{1,0:T(8,128)S(1)}, u32[]{:S(2)}, u32[]{:S(2)}) collective-permute-start(f32[272,128]{1,0:T(8,128)S(1)} %shard_map.64.own_ref), channel_id=1, source_target_pairs={{0,8},{8,0},{16,24},{24,16},{1,9},{9,1},{17,25},{25,17},{2,10},{10... | collective-permute-start | bytes 417800 | tf_op jit(solution)/shard_map/ppermute | solution.py:503
  52.3 4.4 %collective-permute-start.15 = (f32[136,128]{1,0:T(8,128)S(1)}, f32[136,128]{1,0:T(8,128)S(1)}, u32[]{:S(2)}, u32[]{:S(2)}) collective-permute-start(f32[136,128]{1,0:T(8,128)S(1)} %get-tuple-element.76.own_ref), channel_id=1, source_target_pairs={{0,16},{8,24},{16,0},{24,8},{1,17},{9,25},{17,1},{25,9},{2,18},{10... | collective-permute-start | bytes 208904 | tf_op jit(solution)/shard_map/ppermute | solution.py:503

commit v6 on v5

--- a/solution.py
+++ b/solution.py
@@ -424,7 +424,7 @@
     place_ref, half_ref, cross_ref, rest_ref, coef_ref, out_ref, total_ref = refs
     side = place_ref[0] & 1
     for index, source in ((side, half_ref), (side ^ 1, cross_ref)):
-        total_ref[pl.ds(plan.far3_at(index), plan.far3), :] = source[...]
+        total_ref[pl.ds(plan.far3_at(index), plan.far3), :] = source[2 * plan.near3 :, :]
 
     def put(offset, product):
         span = slice(offset, offset + product.shape[0])
@@ -437,10 +437,11 @@
     out_ref[...] = own_ref[...] + other_ref[...]
 
 
-def join_kernel(first_ref, second_ref, out_ref):
+def join_kernel(first_ref, second_ref, own_ref, other_ref, out_ref):
     rows = first_ref.shape[0]
     out_ref[:rows] = first_ref[...]
-    out_ref[rows:] = second_ref[...]
+    out_ref[rows : 2 * rows] = second_ref[...]
+    out_ref[2 * rows :] = own_ref[...] + other_ref[...]
 
 
 def back_kernel(width, blocks, scaled_ref, lower_ref, out_ref):
@@ -644,13 +645,18 @@
             )
             other_key, weights = lax.optimization_barrier((other_key, weights))
             (half,) = call(functools.partial(pivot_kernel, 0, middle), [square], key, other_key)
-            half, opposite = lax.optimization_barrier((half, opposite))
-            (joined,) = call(join_kernel, [(2 * plan.near3, width)], quarter, opposite, cost=0.1)
+            half, opposite, other_half = lax.optimization_barrier((half, opposite, other_half))
+            (joined,) = call(
+                join_kernel,
+                [(2 * plan.near3 + plan.far3, width)],
+                quarter,
+                opposite,
+                last_half,
+                other_half,
+                cost=0.1,
+            )
             joined_cross = flip(joined, 1)
             (inv,) = call(functools.partial(pivot_kernel, middle, width), [square], half)
-            inv, other_half = lax.optimization_barrier((inv, other_half))
-            (last_half,) = call(add_kernel, [last_half.shape], last_half, other_half, cost=0.1)
-            cross = flip(last_half, 1)
             total, coef, key = call(
                 functools.partial(
                     near_update, width, count, functools.partial(take_quarters, plan)
@@ -666,8 +672,8 @@
                 functools.partial(joined_update, plan, width, count, below),
                 [(following, width)],
                 place,
-                last_half,
-                cross,
+                joined,
+                joined_cross,
                 total,
                 coef,
                 smem=1,

time: 60.5 us -> 60.3 us (level)
    ppermute x16 -> x15, starting transfers between devices: 20.2 us -> 19.7 us  [flip(): return lax.ppermute(value, axis, pairs)]
    ppermute x16 -> x15, waiting for transfers between devices: 5.91 us -> 6.28 us  [flip(): return lax.ppermute(value, axis, pairs)]
    pallas_call x23 -> x22, Pallas kernels: 34 us -> 34 us  [call(): pl.pallas_call(kernel, out_shape=outs, in_specs=space, out_specs=[pl.Bloc...]
  transfers between devices with their start and end apart: 16 -> 15, of which waited for: 7 -> 7; matrix products, arithmetic and copies ran while one was open for 0% -> 0% of each run, Pallas kernels for 29% -> 28%
where the time goes in v6:
time: 60.3 us; the launch traced here: 60.1 us
  Pallas kernels  34 us (56%)
  starting transfers between devices  19.7 us (33%)
  waiting for transfers between devices  6.28 us (10%)
    pallas_call x22, Pallas kernels, call(): pl.pallas_call(kernel, out_shape=outs, in_specs=space, out_specs=[pl.Bloc...  34 us
    ppermute x15, starting transfers between devices, flip(): return lax.ppermute(value, axis, pairs)  19.7 us
    ppermute x15, waiting for transfers between devices, flip(): return lax.ppermute(value, axis, pairs)  6.28 us
  transfers between devices with their start and end apart: 15, of which 7 were waited for; matrix products, arithmetic and copies ran while one was open for 0% of the time, Pallas kernels for 28%

profile of v6, /device:TPU:0, one launch (start us, length us, event | category | flops | bytes accessed | tf_op | source)
XLA Modules:
  0.0 60.1 jit_solution(14501624165340692671)
XLA Ops:
  0.0 11.8 %shard_map.46 = (f32[128,128]{1,0:T(8,128)S(1)}, f32[1832,128]{1,0:T(8,128)S(1)}, f32[3,656,128]{2,1,0:T(8,128)S(1)}, f32[3,2,128,128]{3,2,1,0:T(8,128)S(1)}, bf...) custom-call(s32[1]{0:T(128)} %bitcast.place_ref.refs_0_, s32[31]{0:T(128)} %ranks_hbm.1, f32[8,384]{1,0:T(8,128)} %bitcast.3, ...), custom_call_target="tpu_custom_call" | custom-call | flops 1500000000 | bytes 5000000 | tf_op jit(solution)/shard_map/pallas_call | solution.py:491
  11.9 0.5 collective-permute-start
  12.4 0.7 %shard_map.47.refs_0_ = f32[1832,128]{1,0:T(8,128)S(1)} custom-call(f32[1832,128]{1,0:T(8,128)S(1)} %get-tuple-element.41.part_ref, bf16[656,768]{1,0:T(8,128)(2,1)S(1)} %get-tuple-element.42.v6_ref, bf16[640,768]{1,0:T(8,128)(2,1)S(1)} %get-tuple-element.43.s6_ref), custom_call_target="tpu_custom_call" | custom-call | flops 1500000000 | bytes 5000000 | tf_op jit(solution)/shard_map/pallas_call | solution.py:491
  13.1 0.2 collective-permute-done.refs_1_
  13.3 0.4 collective-permute-start.1
  13.6 2.8 %shard_map.48.refs_2_ = f32[128,128]{1,0:T(8,128)S(1)} custom-call(f32[128,128]{1,0:T(8,128)S(1)} %get-tuple-element.44.refs_0_, f32[128,128]{1,0:T(8,128)S(1)} %collective-permute-done.refs_1_), custom_call_target="tpu_custom_call" | custom-call | flops 1500000000 | bytes 5000000 | tf_op jit(solution)/shard_map/pallas_call | solution.py:491
  16.4 0.0 collective-permute-done.1.refs_1_
  16.4 0.5 shard_map.49
  17.0 2.8 %collective-permute-start.2 = (f32[128,128]{1,0:T(8,128)S(1)}, f32[128,128]{1,0:T(8,128)S(1)}, u32[]{:S(2)}, u32[]{:S(2)}) collective-permute-start(f32[128,128]{1,0:T(8,128)S(1)} %get-tuple-element.53.refs_0_), channel_id=1, source_target_pairs={{0,2},{1,3},{2,0},{3,1},{4,6},{5,7},{6,4},{7,5},{8,10},{9,11},{10,... | collective-permute-start | bytes 196616 | tf_op jit(solution)/shard_map/ppermute | solution.py:504
  19.8 0.6 shard_map.50
  20.4 0.1 collective-permute-start.3
  20.4 0.5 shard_map.51
  20.9 2.1 %collective-permute-start.5 = (f32[104,128]{1,0:T(8,128)S(1)}, f32[104,128]{1,0:T(8,128)S(1)}, u32[]{:S(2)}, u32[]{:S(2)}) collective-permute-start(f32[104,128]{1,0:T(8,128)S(1)} %get-tuple-element.57), channel_id=1, source_target_pairs={{0,2},{1,3},{2,0},{3,1},{4,6},{5,7},{6,4},{7,5},{8,10},{9,11},{10,... | collective-permute-start | bytes 159752 | tf_op jit(solution)/shard_map/ppermute | solution.py:504
  23.0 0.0 collective-permute-done.2.refs_1_
  23.0 1.4 %shard_map.52.refs_0_ = f32[128,128]{1,0:T(8,128)S(1)} custom-call(f32[128,128]{1,0:T(8,128)S(1)} %get-tuple-element.53.refs_0_, f32[128,128]{1,0:T(8,128)S(1)} %collective-permute-done.2.refs_1_), custom_call_target="tpu_custom_call" | custom-call | flops 1500000000 | bytes 5000000 | tf_op jit(solution)/shard_map/pallas_call | solution.py:491
  24.4 1.7 %collective-permute-start.7 = (f32[136,128]{1,0:T(8,128)S(1)}, f32[136,128]{1,0:T(8,128)S(1)}, u32[]{:S(2)}, u32[]{:S(2)}) collective-permute-start(f32[136,128]{1,0:T(8,128)S(1)} %get-tuple-element.62), channel_id=1, source_target_pairs={{0,2},{1,3},{2,0},{3,1},{4,6},{5,7},{6,4},{7,5},{8,10},{9,11},{10,... | collective-permute-start | bytes 208904 | tf_op jit(solution)/shard_map/ppermute | solution.py:504
  26.2 0.4 collective-permute-done.3.refs_2_
  26.5 0.0 collective-permute-start.4
  26.6 1.4 %shard_map.53.refs_6_ = f32[128,128]{1,0:T(8,128)S(1)} custom-call(f32[128,128]{1,0:T(8,128)S(1)} %shard_map.52.refs_0_), custom_call_target="tpu_custom_call" | custom-call | flops 1500000000 | bytes 5000000 | tf_op jit(solution)/shard_map/pallas_call | solution.py:491
  28.0 0.0 collective-permute-done.5.refs_5_
  28.0 0.0 collective-permute-done.4.refs_3_
  28.0 0.9 %shard_map.54 = (f32[520,128]{1,0:T(8,128)S(1)}, f32[392,128]{1,0:T(8,128)S(1)}, f32[104,128]{1,0:T(8,128)S(1)}) custom-call(s32[1]{0:T(128)} %bitcast.place_ref.refs_0_, f32[520,128]{1,0:T(8,128)S(1)} %get-tuple-element.49.refs_1_, f32[264,128]{1,0:T(8,128)S(1)} %collective-permute-done.3.refs_2_, f32[264,128]{1,0:T(8,128)S(1)} %collective-permute-done.4.refs_3_, ...), custom_call_target="tpu_custom_call" | custom-call | flops 1500000000 | bytes 5000000 | tf_op jit(solution)/shard_map/pallas_call | solution.py:491
  28.9 2.7 %collective-permute-start.6 = (f32[104,128]{1,0:T(8,128)S(1)}, f32[104,128]{1,0:T(8,128)S(1)}, u32[]{:S(2)}, u32[]{:S(2)}) collective-permute-start(f32[104,128]{1,0:T(8,128)S(1)} %get-tuple-element.59.own_ref), channel_id=1, source_target_pairs={{0,4},{1,5},{2,6},{3,7},{4,0},{5,1},{6,2},{7,3},{8,12},{9,13},{10,... | collective-permute-start | bytes 159752 | tf_op jit(solution)/shard_map/ppermute | solution.py:504
  31.5 0.2 shard_map.57.refs_0_
  31.8 0.4 collective-permute-start.8
  32.2 0.0 collective-permute-done.7.refs_4_
  32.2 0.3 shard_map.55.own_ref
  32.5 2.7 %collective-permute-start.10 = (f32[136,128]{1,0:T(8,128)S(1)}, f32[136,128]{1,0:T(8,128)S(1)}, u32[]{:S(2)}, u32[]{:S(2)}) collective-permute-start(f32[136,128]{1,0:T(8,128)S(1)} %shard_map.55.own_ref), channel_id=1, source_target_pairs={{0,4},{1,5},{2,6},{3,7},{4,0},{5,1},{6,2},{7,3},{8,12},{9,13},{10,... | collective-permute-start | bytes 208904 | tf_op jit(solution)/shard_map/ppermute | solution.py:504
  35.1 0.1 collective-permute-done.6.other_ref
  35.2 2.6 %collective-permute-start.9 = (f32[104,128]{1,0:T(8,128)S(1)}, f32[104,128]{1,0:T(8,128)S(1)}, u32[]{:S(2)}, u32[]{:S(2)}) collective-permute-start(f32[104,128]{1,0:T(8,128)S(1)} %shard_map.56.first_ref), channel_id=1, source_target_pairs={{0,2},{1,3},{2,0},{3,1},{4,6},{5,7},{6,4},{7,5},{8,10},{9,11},{10,... | collective-permute-start | bytes 159752 | tf_op jit(solution)/shard_map/ppermute | solution.py:504
  37.8 1.0 %shard_map.58.weights_ref = f32[656,384]{1,0:T(8,128)S(1)} custom-call(f32[3,656,128]{2,1,0:T(8,128)S(1)} %get-tuple-element.65.scaled_ref, f32[3,2,128,128]{3,2,1,0:T(8,128)S(1)} %get-tuple-element.66.lower_ref), custom_call_target="tpu_custom_call" | custom-call | flops 1000000000 | bytes 3333333 | tf_op jit(solution)/shard_map/pallas_call | solution.py:491
  38.8 1.6 %collective-permute-done.8.refs_1_ = f32[128,128]{1,0:T(8,128)S(1)} collective-permute-done((f32[128,128]{1,0:T(8,128)S(1)}, f32[128,128]{1,0:T(8,128)S(1)}, u32[]{:S(2)}, u32[]{:S(2)}) %collective-permute-start.8) | collective-permute-done | bytes 65568 | tf_op jit(solution)/shard_map/ppermute | solution.py:504
  40.5 1.4 %shard_map.59.refs_0_ = f32[128,128]{1,0:T(8,128)S(1)} custom-call(f32[128,128]{1,0:T(8,128)S(1)} %shard_map.57.refs_0_, f32[128,128]{1,0:T(8,128)S(1)} %collective-permute-done.8.refs_1_), custom_call_target="tpu_custom_call" | custom-call | flops 1500000000 | bytes 5000000 | tf_op jit(solution)/shard_map/pallas_call | solution.py:491
  41.9 0.0 collective-permute-done.9.second_ref
  41.9 0.1 collective-permute-start.11
  42.0 1.4 %shard_map.61.refs_3_ = f32[128,128]{1,0:T(8,128)S(1)} custom-call(f32[128,128]{1,0:T(8,128)S(1)} %shard_map.59.refs_0_), custom_call_target="tpu_custom_call" | custom-call | flops 1500000000 | bytes 5000000 | tf_op jit(solution)/shard_map/pallas_call | solution.py:491
  43.4 0.5 shard_map.62
  44.0 1.5 %collective-permute-start.13 = (f32[128,128]{1,0:T(8,128)S(1)}, f32[128,128]{1,0:T(8,128)S(1)}, u32[]{:S(2)}, u32[]{:S(2)}) collective-permute-start(f32[128,128]{1,0:T(8,128)S(1)} %get-tuple-element.73.refs_0_), channel_id=1, source_target_pairs={{0,8},{8,0},{16,24},{24,16},{1,9},{9,1},{17,25},{25,17},{2,10},{10... | collective-permute-start | bytes 196616 | tf_op jit(solution)/shard_map/ppermute | solution.py:504
  45.5 0.3 shard_map.63.own_ref
  45.8 0.6 %collective-permute-start.12 = (f32[272,128]{1,0:T(8,128)S(1)}, f32[272,128]{1,0:T(8,128)S(1)}, u32[]{:S(2)}, u32[]{:S(2)}) collective-permute-start(f32[272,128]{1,0:T(8,128)S(1)} %shard_map.63.own_ref), channel_id=1, source_target_pairs={{0,8},{8,0},{16,24},{24,16},{1,9},{9,1},{17,25},{25,17},{2,10},{10... | collective-permute-start | bytes 417800 | tf_op jit(solution)/shard_map/ppermute | solution.py:504
  46.4 2.1 %collective-permute-done.13.refs_1_ = f32[128,128]{1,0:T(8,128)S(1)} collective-permute-done((f32[128,128]{1,0:T(8,128)S(1)}, f32[128,128]{1,0:T(8,128)S(1)}, u32[]{:S(2)}, u32[]{:S(2)}) %collective-permute-start.13) | collective-permute-done | bytes 65568 | tf_op jit(solution)/shard_map/ppermute | solution.py:504
  48.5 2.8 %shard_map.64.inv_ref = f32[128,128]{1,0:T(8,128)S(1)} custom-call(f32[128,128]{1,0:T(8,128)S(1)} %get-tuple-element.73.refs_0_, f32[128,128]{1,0:T(8,128)S(1)} %collective-permute-done.13.refs_1_), custom_call_target="tpu_custom_call" | custom-call | flops 1500000000 | bytes 5000000 | tf_op jit(solution)/shard_map/pallas_call | solution.py:491
  51.3 0.4 collective-permute-done.12.other_ref
  51.7 0.4 shard_map.65
  52.1 1.6 %collective-permute-start.14 = (f32[136,128]{1,0:T(8,128)S(1)}, f32[136,128]{1,0:T(8,128)S(1)}, u32[]{:S(2)}, u32[]{:S(2)}) collective-permute-start(f32[136,128]{1,0:T(8,128)S(1)} %get-tuple-element.74.own_ref), channel_id=1, source_target_pairs={{0,16},{8,24},{16,0},{24,8},{1,17},{9,25},{17,1},{25,9},{2,18},{10... | collective-permute-start | bytes 208904 | tf_op jit(solution)/shard_map/ppermute | solution.py:504
  53.7 1.3 %shard_map.66.folded_ref = f32[136,384]{1,0:T(8,128)S(1)} custom-call(f32[656,384]{1,0:T(8,128)S(1)} %shard_map.58.weights_ref, f32[520,128]{1,0:T(8,128)S(1)} %get-tuple-element.48.refs_3_.refs_0_, f32[392,128]{1,0:T(8,128)S(1)} %get-tuple-element.61.refs_2_.coef_ref.refs_1_, f32[264,128]{1,0:T(8,128)S(1)} %get-tuple-element.72.refs_4_.refs_2_, ...), custom_call_target="tpu_custom_call" | custom-call | flops 1500000000 | bytes 5000000 | tf_op jit(solution)/shard_map/pallas_call | solution.py:491
  55.0 1.5 %collective-permute-done.14.other_ref = f32[136,128]{1,0:T(8,128)S(1)} collective-permute-done((f32[136,128]{1,0:T(8,128)S(1)}, f32[136,128]{1,0:T(8,128)S(1)}, u32[]{:S(2)}, u32[]{:S(2)}) %collective-permute-start.14) | collective-permute-done | bytes 69664 | tf_op jit(solution)/shard_map/ppermute | solution.py:504
  56.5 3.7 %shard_map.67 = f32[8,384]{1,0:T(8,128)} custom-call(f32[136,128]{1,0:T(8,128)S(1)} %get-tuple-element.74.own_ref, f32[136,128]{1,0:T(8,128)S(1)} %collective-permute-done.14.other_ref, f32[136,384]{1,0:T(8,128)S(1)} %shard_map.66.folded_ref), custom_call_target="tpu_custom_call" | custom-call | flops 1500000000 | bytes 5000000 | tf_op jit(solution)/shard_map/pallas_call | solution.py:491
  (4 shorter events, 0.0 us)
Async XLA Ops:
  11.9 1.4 %collective-permute-start = (f32[128,128]{1,0:T(8,128)S(1)}, f32[128,128]{1,0:T(8,128)S(1)}, u32[]{:S(2)}, u32[]{:S(2)}) collective-permute-start(f32[128,128]{1,0:T(8,128)S(1)} %get-tuple-element.44.refs_0_), channel_id=1, source_target_pairs={{0,1},{1,0},{2,3},{3,2},{4,5},{5,4},{6,7},{7,6},{8,9},{9,8},{10,11... | collective-permute-start | bytes 196616 | tf_op jit(solution)/shard_map/ppermute | solution.py:504
  13.3 3.1 %collective-permute-start.1 = (f32[1832,128]{1,0:T(8,128)S(1)}, f32[1832,128]{1,0:T(8,128)S(1)}, u32[]{:S(2)}, u32[]{:S(2)}) collective-permute-start(f32[1832,128]{1,0:T(8,128)S(1)} %shard_map.47.refs_0_), channel_id=1, source_target_pairs={{0,1},{1,0},{2,3},{3,2},{4,5},{5,4},{6,7},{7,6},{8,9},{9,8},{10,11... | collective-permute-start | bytes 2813960 | tf_op jit(solution)/shard_map/ppermute | solution.py:504
  17.0 6.0 %collective-permute-start.2 = (f32[128,128]{1,0:T(8,128)S(1)}, f32[128,128]{1,0:T(8,128)S(1)}, u32[]{:S(2)}, u32[]{:S(2)}) collective-permute-start(f32[128,128]{1,0:T(8,128)S(1)} %get-tuple-element.53.refs_0_), channel_id=1, source_target_pairs={{0,2},{1,3},{2,0},{3,1},{4,6},{5,7},{6,4},{7,5},{8,10},{9,11},{10,... | collective-permute-start | bytes 196616 | tf_op jit(solution)/shard_map/ppermute | solution.py:504
  20.4 6.2 %collective-permute-start.3 = (f32[264,128]{1,0:T(8,128)S(1)}, f32[264,128]{1,0:T(8,128)S(1)}, u32[]{:S(2)}, u32[]{:S(2)}) collective-permute-start(f32[264,128]{1,0:T(8,128)S(1)} %get-tuple-element.50), channel_id=1, source_target_pairs={{0,2},{1,3},{2,0},{3,1},{4,6},{5,7},{6,4},{7,5},{8,10},{9,11},{10,... | collective-permute-start | bytes 405512 | tf_op jit(solution)/shard_map/ppermute | solution.py:504
  20.9 7.1 %collective-permute-start.5 = (f32[104,128]{1,0:T(8,128)S(1)}, f32[104,128]{1,0:T(8,128)S(1)}, u32[]{:S(2)}, u32[]{:S(2)}) collective-permute-start(f32[104,128]{1,0:T(8,128)S(1)} %get-tuple-element.57), channel_id=1, source_target_pairs={{0,2},{1,3},{2,0},{3,1},{4,6},{5,7},{6,4},{7,5},{8,10},{9,11},{10,... | collective-permute-start | bytes 159752 | tf_op jit(solution)/shard_map/ppermute | solution.py:504
  24.4 7.7 %collective-permute-start.7 = (f32[136,128]{1,0:T(8,128)S(1)}, f32[136,128]{1,0:T(8,128)S(1)}, u32[]{:S(2)}, u32[]{:S(2)}) collective-permute-start(f32[136,128]{1,0:T(8,128)S(1)} %get-tuple-element.62), channel_id=1, source_target_pairs={{0,2},{1,3},{2,0},{3,1},{4,6},{5,7},{6,4},{7,5},{8,10},{9,11},{10,... | collective-permute-start | bytes 208904 | tf_op jit(solution)/shard_map/ppermute | solution.py:504
  26.5 1.4 %collective-permute-start.4 = (f32[264,128]{1,0:T(8,128)S(1)}, f32[264,128]{1,0:T(8,128)S(1)}, u32[]{:S(2)}, u32[]{:S(2)}) collective-permute-start(f32[264,128]{1,0:T(8,128)S(1)} %collective-permute-done.3.refs_2_), channel_id=1, source_target_pairs={{0,1},{1,0},{2,3},{3,2},{4,5},{5,4},{6,7},{7,6},{8,9},{9,8},{10,11... | collective-permute-start | bytes 405512 | tf_op jit(solution)/shard_map/ppermute | solution.py:504
  28.9 6.3 %collective-permute-start.6 = (f32[104,128]{1,0:T(8,128)S(1)}, f32[104,128]{1,0:T(8,128)S(1)}, u32[]{:S(2)}, u32[]{:S(2)}) collective-permute-start(f32[104,128]{1,0:T(8,128)S(1)} %get-tuple-element.59.own_ref), channel_id=1, source_target_pairs={{0,4},{1,5},{2,6},{3,7},{4,0},{5,1},{6,2},{7,3},{8,12},{9,13},{10,... | collective-permute-start | bytes 159752 | tf_op jit(solution)/shard_map/ppermute | solution.py:504
  31.8 8.7 %collective-permute-start.8 = (f32[128,128]{1,0:T(8,128)S(1)}, f32[128,128]{1,0:T(8,128)S(1)}, u32[]{:S(2)}, u32[]{:S(2)}) collective-permute-start(f32[128,128]{1,0:T(8,128)S(1)} %shard_map.57.refs_0_), channel_id=1, source_target_pairs={{0,4},{1,5},{2,6},{3,7},{4,0},{5,1},{6,2},{7,3},{8,12},{9,13},{10,... | collective-permute-start | bytes 196616 | tf_op jit(solution)/shard_map/ppermute | solution.py:504
  32.5 9.4 %collective-permute-start.10 = (f32[136,128]{1,0:T(8,128)S(1)}, f32[136,128]{1,0:T(8,128)S(1)}, u32[]{:S(2)}, u32[]{:S(2)}) collective-permute-start(f32[136,128]{1,0:T(8,128)S(1)} %shard_map.55.own_ref), channel_id=1, source_target_pairs={{0,4},{1,5},{2,6},{3,7},{4,0},{5,1},{6,2},{7,3},{8,12},{9,13},{10,... | collective-permute-start | bytes 208904 | tf_op jit(solution)/shard_map/ppermute | solution.py:504
  35.2 6.7 %collective-permute-start.9 = (f32[104,128]{1,0:T(8,128)S(1)}, f32[104,128]{1,0:T(8,128)S(1)}, u32[]{:S(2)}, u32[]{:S(2)}) collective-permute-start(f32[104,128]{1,0:T(8,128)S(1)} %shard_map.56.first_ref), channel_id=1, source_target_pairs={{0,2},{1,3},{2,0},{3,1},{4,6},{5,7},{6,4},{7,5},{8,10},{9,11},{10,... | collective-permute-start | bytes 159752 | tf_op jit(solution)/shard_map/ppermute | solution.py:504
  41.9 1.5 %collective-permute-start.11 = (f32[344,128]{1,0:T(8,128)S(1)}, f32[344,128]{1,0:T(8,128)S(1)}, u32[]{:S(2)}, u32[]{:S(2)}) collective-permute-start(f32[344,128]{1,0:T(8,128)S(1)} %shard_map.60.refs_1_), channel_id=1, source_target_pairs={{0,1},{1,0},{2,3},{3,2},{4,5},{5,4},{6,7},{7,6},{8,9},{9,8},{10,11... | collective-permute-start | bytes 528392 | tf_op jit(solution)/shard_map/ppermute | solution.py:504
  44.0 4.6 %collective-permute-start.13 = (f32[128,128]{1,0:T(8,128)S(1)}, f32[128,128]{1,0:T(8,128)S(1)}, u32[]{:S(2)}, u32[]{:S(2)}) collective-permute-start(f32[128,128]{1,0:T(8,128)S(1)} %get-tuple-element.73.refs_0_), channel_id=1, source_target_pairs={{0,8},{8,0},{16,24},{24,16},{1,9},{9,1},{17,25},{25,17},{2,10},{10... | collective-permute-start | bytes 196616 | tf_op jit(solution)/shard_map/ppermute | solution.py:504
  45.8 5.9 %collective-permute-start.12 = (f32[272,128]{1,0:T(8,128)S(1)}, f32[272,128]{1,0:T(8,128)S(1)}, u32[]{:S(2)}, u32[]{:S(2)}) collective-permute-start(f32[272,128]{1,0:T(8,128)S(1)} %shard_map.63.own_ref), channel_id=1, source_target_pairs={{0,8},{8,0},{16,24},{24,16},{1,9},{9,1},{17,25},{25,17},{2,10},{10... | collective-permute-start | bytes 417800 | tf_op jit(solution)/shard_map/ppermute | solution.py:504
  52.1 4.4 %collective-permute-start.14 = (f32[136,128]{1,0:T(8,128)S(1)}, f32[136,128]{1,0:T(8,128)S(1)}, u32[]{:S(2)}, u32[]{:S(2)}) collective-permute-start(f32[136,128]{1,0:T(8,128)S(1)} %get-tuple-element.74.own_ref), channel_id=1, source_target_pairs={{0,16},{8,24},{16,0},{24,8},{1,17},{9,25},{17,1},{25,9},{2,18},{10... | collective-permute-start | bytes 208904 | tf_op jit(solution)/shard_map/ppermute | solution.py:504
